TPU v7x, 256 devices: a whole 4x4x8 slice. The times are simulated.
256 devices in a mesh: vertex: 16 (over z, core), feat: 16 (over x, y).
Axes of the slice: x: 4, y: 4, z: 8, core: 2. Of those that a mesh axis runs over, the one named last changes fastest.
Arguments:
- features: bfloat16 [768, 65536], P('feat', 'vertex'), may hold values from -6 to 6
- neigh_weight: bfloat16 [768, 1024], P('feat'), may hold values from -0.3125 to 0.3125
- self_weight: bfloat16 [768, 1024], P('feat'), may hold values from -0.21875 to 0.21875
- bias: bfloat16 [1024], P('feat'), may hold values from -1 to 1
- neighbors: int32 [25, 32768], P(None, 'vertex'), may hold values from -1 to 8191, as said below
- boundary: int32 [16, 16, 256], P('vertex'), may hold values from 0 to 4095
- counts: int32 [16, 16], P('vertex'), may hold values from 64 to 256, as said below
- cotangent: bfloat16 [1024, 32768], P('feat', 'vertex'), may hold values from -6 to 6
Outputs:
- activation: bfloat16 [1024, 32768], P('feat', 'vertex')
- neigh_grad: float32 [768, 1024], P('feat', 'vertex')
- self_grad: float32 [768, 1024], P('feat', 'vertex')
- bias_grad: float32 [1024], P('feat')
Inputs may be any that keep to these rules, and one draw needn't show every extreme that they name: `counts`: the largest value is reached in every draw. `neighbors`: -1 marks an empty slot; a value v < 4096 is a node of the seed's own partition; v = 4096 + q * 256 + c names slot c of the boundary list from partition q to the seed's partition, with c < counts[q, that partition]. Slot 0 of every seed is not empty.
All inputs are finite; a program needn't handle non-finite values.
Results may differ from a plain program's by a relative error of at most 0.0035.
Values may be sent and summed in bfloat16 or wider, within the bound.
No kernel may reach another device: no remote copies, remote signals or barrier semaphores. Data moves between devices by JAX's collectives and lax.ppermute only.
A program may use at most 64 MiB of HBM per device.

v0:
```python
import math

import jax
import jax.numpy as jnp
from jax import lax
from jax.sharding import PartitionSpec as P


def body(features, neigh_weight, self_weight, bias, neighbors, boundary, counts, cotangent):
    columns, node_count = features.shape
    partitions = lax.axis_size("vertex")
    capacity = boundary.shape[2]
    slot_count, seed_count = neighbors.shape
    node_ids = jnp.arange(node_count, dtype=jnp.int32)[:, None]
    slot_ids = jnp.arange(capacity, dtype=jnp.int32)[None, :]

    def pick_list(listed):
        rows, used = listed
        table = ((node_ids == rows[None, :]) & (slot_ids < used)).astype(jnp.bfloat16)
        return jnp.dot(features, table, preferred_element_type=jnp.float32).astype(jnp.bfloat16)

    picked = lax.map(pick_list, (boundary[0], counts[0]))
    outgoing = jnp.transpose(picked, (1, 0, 2))
    incoming = lax.all_to_all(outgoing, "vertex", split_axis=1, concat_axis=1, tiled=True)
    lookup = jnp.concatenate([features, incoming.reshape(columns, partitions * capacity)], axis=1)
    lookup_width = lookup.shape[1]
    block = math.gcd(256, seed_count)
    block_count = seed_count // block
    lookup_ids = jnp.arange(lookup_width, dtype=jnp.int32)[:, None]

    def block_sums(slots):
        table = jnp.zeros((lookup_width, block), jnp.bfloat16)
        for slot in range(slot_count):
            table = table + (lookup_ids == slots[slot][None, :]).astype(jnp.bfloat16)
        return jnp.dot(lookup, table, preferred_element_type=jnp.float32)

    blocked = jnp.transpose(neighbors.reshape(slot_count, block_count, block), (1, 0, 2))
    summed = jnp.transpose(lax.map(block_sums, blocked), (1, 0, 2)).reshape(columns, seed_count)
    degree = jnp.sum((neighbors >= 0).astype(jnp.float32), axis=0)
    neigh_mean = (summed / degree[None, :]).astype(jnp.bfloat16)
    own_rows = features[:, :seed_count]
    contract_first = (((0,), (0,)), ((), ()))
    partial_sum = lax.dot_general(
        neigh_weight, neigh_mean, contract_first, preferred_element_type=jnp.float32
    ) + lax.dot_general(self_weight, own_rows, contract_first, preferred_element_type=jnp.float32)
    preact = (
        lax.psum_scatter(partial_sum, "feat", scatter_dimension=0, tiled=True)
        + bias.astype(jnp.float32)[:, None]
    )
    activation = jnp.where(preact > 0, preact, jnp.exp(jnp.minimum(preact, 0.0)) - 1.0).astype(
        jnp.bfloat16
    )
    slope = jnp.where(preact > 0, 1.0, jnp.exp(jnp.minimum(preact, 0.0)))
    grad_pre = (cotangent.astype(jnp.float32) * slope).astype(jnp.bfloat16)
    inputs = jnp.concatenate([neigh_mean, own_rows], axis=0)
    grad_terms = lax.dot_general(
        inputs,
        lax.all_gather(grad_pre, "feat", axis=0, tiled=True),
        (((1,), (1,)), ((), ())),
        preferred_element_type=jnp.float32,
    )
    grad_share = lax.psum_scatter(grad_terms, "vertex", scatter_dimension=1, tiled=True)
    bias_sum = lax.psum(jnp.sum(grad_pre.astype(jnp.float32), axis=1), "vertex")
    factor = 1.0 / math.sqrt(seed_count * partitions)
    return (
        activation,
        grad_share[:columns] * factor,
        grad_share[columns:] * factor,
        bias_sum * factor,
    )


def solution(mesh):
    placed = (
        P("feat", "vertex"),
        P("feat", None),
        P("feat", None),
        P("feat"),
        P(None, "vertex"),
        P("vertex", None, None),
        P("vertex", None),
        P("feat", "vertex"),
    )
    return jax.shard_map(
        body,
        mesh=mesh,
        in_specs=placed,
        out_specs=(P("feat", "vertex"), P("feat", "vertex"), P("feat", "vertex"), P("feat")),
        check_vma=False,
    )
```

profile of v0, /device:TPU:36, one launch (start us, length us, event | category | flops | bytes accessed | tf_op | source)
XLA Modules:
  0.0 508.2 jit_solution(889828545391560002)
XLA Ops:
  7.2 82.8 %while.23 = (s32[]{:T(128)}, bf16[16,48,256]{2,1,0:T(8,128)(2,1)}, s32[16,256]{1,0:T(8,128)}, s32[16]{0:T(128)}, bf16[48,4096]{1,0:T(8,128)(2,1)}, /*index=5*/s32[]{:T(128)}) while((s32[]{:T(128)}, bf16[16,48,256]{2,1,0:T(8,128)(2,1)}, s32[16,256]{1,0:T(8,128)}, s32[16]{0:T(128)}, bf16[48,4096]{1,0:T(8,128)(2,1)}, ...), condition=%wide.region_1.2_spmd.clone, body=%wide.region_0.1_spmd.clone.sunk | while | flops 102772992 | bytes 421977 | solution.py:22
  8.0 1.2 dynamic_slice.20
  9.9 2.6 fusion.151
  13.2 1.2 dynamic_slice.20
  15.1 2.6 fusion.151
  18.3 1.2 dynamic_slice.20
  20.2 2.6 fusion.151
  23.5 1.2 dynamic_slice.20
  25.4 2.6 fusion.151
  28.7 1.2 dynamic_slice.20
  30.6 2.6 fusion.151
  33.8 1.2 dynamic_slice.20
  35.7 2.6 fusion.151
  39.0 1.2 dynamic_slice.20
  40.9 2.6 fusion.151
  44.2 1.2 dynamic_slice.20
  46.1 2.6 fusion.151
  49.3 1.2 dynamic_slice.20
  51.2 2.6 fusion.151
  56.4 2.6 fusion.151
  59.7 1.2 dynamic_slice.20
  61.6 2.6 fusion.151
  66.8 2.6 fusion.151
  71.9 2.6 fusion.151
  77.1 2.6 fusion.151
  82.3 2.6 fusion.151
  85.5 1.2 dynamic_slice.20
  87.4 2.6 fusion.151
  90.0 8.7 %all-to-all-start = ((bf16[48,16,256]{2,0,1:T(8,128)(2,1)}), bf16[48,16,256]{2,0,1:T(8,128)(2,1)S(1)}, u32[]{:S(2)}, u32[]{:S(2)}) async-start(bf16[48,16,256]{2,0,1:T(8,128)(2,1)} %bitcast.3), calls=%async_computation | async-start | bytes 786432 | tf_op jit(solution)/shard_map/all_to_all | solution.py:24
  99.0 5.4 %fusion.134 = f32[1024,2048]{0,1:T(8,128)} fusion(bf16[48,1024]{1,0:T(8,128)(2,1)S(1)} %copy-done, bf16[48,4096]{1,0:T(8,128)(2,1)} %get-tuple-element.501), kind=kOutput, calls=%fused_computation.160 | convolution fusion | flops 201326592 | bytes 8683520 | tf_op jit(solution)/shard_map/dot_general | solution.py:45
  104.4 6.2 %all-to-all-done = bf16[48,16,256]{2,0,1:T(8,128)(2,1)S(1)} async-done(((bf16[48,16,256]{2,0,1:T(8,128)(2,1)}), bf16[48,16,256]{2,0,1:T(8,128)(2,1)S(1)}, u32[]{:S(2)}, u32[]{:S(2)}) %all-to-all-start) | async-done | bytes 393248 | tf_op jit(solution)/shard_map/all_to_all | solution.py:24
  110.7 165.8 %while.24 = (s32[]{:T(128)}, f32[8,48,256]{2,1,0:T(8,128)S(1)}, s32[8,25,256]{2,0,1:T(8,128)S(1)}, bf16[48,8192]{1,0:T(8,128)(2,1)S(1)}, s32[]{:T(128)}, /*index...) while((s32[]{:T(128)}, f32[8,48,256]{2,1,0:T(8,128)S(1)}, ...), condition=%wide.region_3.4_spmd.clone.clone, body=%wide.region_2.3_spmd.clone.clone.sunk | while | flops 411041824 | bytes 913041 | solution.py:38
  111.1 20.5 %fusion.154 = f32[8,48,256]{2,1,0:T(8,128)S(1)} fusion(f32[8,48,256]{2,1,0:T(8,128)S(1)} %get-tuple-element.433, s32[]{:T(128)} %get-tuple-element.432, bf16[48,8192]{1,0:T(8,128)(2,1)S(1)} %get-tuple-element.465, s32[256]{0:T(256)S(1)} %bitcast.203, s32[256]{0:T(256)S(1)} %bitcast.180, s32[256]{0:T(256)S(1)} %bitcast.181, s32[256]{0:T(256)S(1)} %bitcast.182, ...), kind=kOutput, calls=%fused_computation.104.clone.1 | convolution fusion | flops 411041792 | bytes 861188 | tf_op jit(solution)/shard_map/while/body/eval_jaxpr/dot_general | solution.py:35
  131.7 20.5 %fusion.154 = f32[8,48,256]{2,1,0:T(8,128)S(1)} fusion(f32[8,48,256]{2,1,0:T(8,128)S(1)} %get-tuple-element.433, s32[]{:T(128)} %get-tuple-element.432, bf16[48,8192]{1,0:T(8,128)(2,1)S(1)} %get-tuple-element.465, s32[256]{0:T(256)S(1)} %bitcast.203, s32[256]{0:T(256)S(1)} %bitcast.180, s32[256]{0:T(256)S(1)} %bitcast.181, s32[256]{0:T(256)S(1)} %bitcast.182, ...), kind=kOutput, calls=%fused_computation.104.clone.1 | convolution fusion | flops 411041792 | bytes 861188 | tf_op jit(solution)/shard_map/while/body/eval_jaxpr/dot_general | solution.py:35
  152.4 20.5 %fusion.154 = f32[8,48,256]{2,1,0:T(8,128)S(1)} fusion(f32[8,48,256]{2,1,0:T(8,128)S(1)} %get-tuple-element.433, s32[]{:T(128)} %get-tuple-element.432, bf16[48,8192]{1,0:T(8,128)(2,1)S(1)} %get-tuple-element.465, s32[256]{0:T(256)S(1)} %bitcast.203, s32[256]{0:T(256)S(1)} %bitcast.180, s32[256]{0:T(256)S(1)} %bitcast.181, s32[256]{0:T(256)S(1)} %bitcast.182, ...), kind=kOutput, calls=%fused_computation.104.clone.1 | convolution fusion | flops 411041792 | bytes 861188 | tf_op jit(solution)/shard_map/while/body/eval_jaxpr/dot_general | solution.py:35
  173.1 20.5 %fusion.154 = f32[8,48,256]{2,1,0:T(8,128)S(1)} fusion(f32[8,48,256]{2,1,0:T(8,128)S(1)} %get-tuple-element.433, s32[]{:T(128)} %get-tuple-element.432, bf16[48,8192]{1,0:T(8,128)(2,1)S(1)} %get-tuple-element.465, s32[256]{0:T(256)S(1)} %bitcast.203, s32[256]{0:T(256)S(1)} %bitcast.180, s32[256]{0:T(256)S(1)} %bitcast.181, s32[256]{0:T(256)S(1)} %bitcast.182, ...), kind=kOutput, calls=%fused_computation.104.clone.1 | convolution fusion | flops 411041792 | bytes 861188 | tf_op jit(solution)/shard_map/while/body/eval_jaxpr/dot_general | solution.py:35
  193.7 20.5 %fusion.154 = f32[8,48,256]{2,1,0:T(8,128)S(1)} fusion(f32[8,48,256]{2,1,0:T(8,128)S(1)} %get-tuple-element.433, s32[]{:T(128)} %get-tuple-element.432, bf16[48,8192]{1,0:T(8,128)(2,1)S(1)} %get-tuple-element.465, s32[256]{0:T(256)S(1)} %bitcast.203, s32[256]{0:T(256)S(1)} %bitcast.180, s32[256]{0:T(256)S(1)} %bitcast.181, s32[256]{0:T(256)S(1)} %bitcast.182, ...), kind=kOutput, calls=%fused_computation.104.clone.1 | convolution fusion | flops 411041792 | bytes 861188 | tf_op jit(solution)/shard_map/while/body/eval_jaxpr/dot_general | solution.py:35
  214.4 20.5 %fusion.154 = f32[8,48,256]{2,1,0:T(8,128)S(1)} fusion(f32[8,48,256]{2,1,0:T(8,128)S(1)} %get-tuple-element.433, s32[]{:T(128)} %get-tuple-element.432, bf16[48,8192]{1,0:T(8,128)(2,1)S(1)} %get-tuple-element.465, s32[256]{0:T(256)S(1)} %bitcast.203, s32[256]{0:T(256)S(1)} %bitcast.180, s32[256]{0:T(256)S(1)} %bitcast.181, s32[256]{0:T(256)S(1)} %bitcast.182, ...), kind=kOutput, calls=%fused_computation.104.clone.1 | convolution fusion | flops 411041792 | bytes 861188 | tf_op jit(solution)/shard_map/while/body/eval_jaxpr/dot_general | solution.py:35
  235.1 20.5 %fusion.154 = f32[8,48,256]{2,1,0:T(8,128)S(1)} fusion(f32[8,48,256]{2,1,0:T(8,128)S(1)} %get-tuple-element.433, s32[]{:T(128)} %get-tuple-element.432, bf16[48,8192]{1,0:T(8,128)(2,1)S(1)} %get-tuple-element.465, s32[256]{0:T(256)S(1)} %bitcast.203, s32[256]{0:T(256)S(1)} %bitcast.180, s32[256]{0:T(256)S(1)} %bitcast.181, s32[256]{0:T(256)S(1)} %bitcast.182, ...), kind=kOutput, calls=%fused_computation.104.clone.1 | convolution fusion | flops 411041792 | bytes 861188 | tf_op jit(solution)/shard_map/while/body/eval_jaxpr/dot_general | solution.py:35
  255.8 20.5 %fusion.154 = f32[8,48,256]{2,1,0:T(8,128)S(1)} fusion(f32[8,48,256]{2,1,0:T(8,128)S(1)} %get-tuple-element.433, s32[]{:T(128)} %get-tuple-element.432, bf16[48,8192]{1,0:T(8,128)(2,1)S(1)} %get-tuple-element.465, s32[256]{0:T(256)S(1)} %bitcast.203, s32[256]{0:T(256)S(1)} %bitcast.180, s32[256]{0:T(256)S(1)} %bitcast.181, s32[256]{0:T(256)S(1)} %bitcast.182, ...), kind=kOutput, calls=%fused_computation.104.clone.1 | convolution fusion | flops 411041792 | bytes 861188 | tf_op jit(solution)/shard_map/while/body/eval_jaxpr/dot_general | solution.py:35
  276.6 7.9 %bitcast_add_fusion = f32[1024,2048]{0,1:T(8,128)} fusion(f32[1024,2048]{0,1:T(8,128)} %fusion.134, bf16[48,2048]{1,0:T(8,128)(2,1)S(1)} %divide_convert_fusion, bf16[48,1024]{1,0:T(8,128)(2,1)S(1)} %copy-done.5), kind=kOutput, calls=%fused_computation.140 | convolution fusion | flops 203423744 | bytes 17072128 | tf_op jit(solution)/shard_map/dot_general | solution.py:43
  284.5 9.3 %copy.43 = f32[1024,2048]{1,0:T(8,128)} copy(f32[1024,2048]{0,1:T(8,128)} %bitcast_add_fusion) | data formatting | bytes 16777216
  294.4 88.7 %reduce-scatter.7.cloned.1.call-done = f32[64,2048]{1,0:T(8,128)} async-done(((f32[1024,2048]{1,0:T(8,128)}), f32[64,2048]{1,0:T(8,128)}) %reduce-scatter.7.cloned.1.call-update) | async-done | bytes 524304 | tf_op jit(solution)/shard_map/reduce_scatter | solution.py:47
  383.1 2.2 convert_reduce_fusion
  385.4 56.5 %all-gather.2.cloned.1.call-done = bf16[1024,2048]{1,0:T(8,128)(2,1)} async-done(((bf16[64,2048]{1,0:T(8,128)(2,1)}), bf16[1024,2048]{1,0:T(8,128)(2,1)}) %all-gather.2.cloned.1.call-update) | async-done | bytes 4194320 | tf_op jit(solution)/shard_map/all_gather | solution.py:58
  441.9 4.2 fusion.129
  446.2 23.3 %psum.7 = f32[64]{0:T(128)S(1)} all-reduce(f32[64]{0:T(128)S(1)} %get-tuple-element.248), channel_id=1, replica_groups=mesh['vertex'=16,'feat'=16] {'vertex'}, use_global_device_ids=true, to_apply=%region_8.9 | all-reduce | flops 64 | bytes 512 | tf_op jit(solution)/shard_map/psum | solution.py:63
  470.0 29.4 %reduce-scatter.5.cloned.1.call-done = f32[96,64]{0,1:T(8,128)} async-done(((f32[96,1024]{0,1:T(8,128)}), f32[96,64]{0,1:T(8,128)}) %reduce-scatter.5.cloned.1.call-update) | async-done | bytes 24592 | tf_op jit(solution)/shard_map/reduce_scatter | solution.py:62
  (88 shorter events, 33.0 us)
Async XLA Ops:
  7.2 91.8 %copy-start = (bf16[48,1024]{1,0:T(8,128)(2,1)S(1)}, bf16[48,1024]{1,0:T(8,128)(2,1)}, u32[]{:S(2)}) copy-start(bf16[48,1024]{1,0:T(8,128)(2,1)} %param.14) | copy-start | bytes 294916
  7.2 91.6 %copy-start.3 = (s32[25,2048]{1,0:T(8,128)S(1)}, s32[25,2048]{1,0:T(8,128)}, u32[]{:S(2)}) copy-start(s32[25,2048]{1,0:T(8,128)} %param.16) | copy-start | bytes 614404
  90.0 20.6 %copy-start.1 = (bf16[48,4096]{1,0:T(8,128)(2,1)S(1)}, bf16[48,4096]{1,0:T(8,128)(2,1)}, u32[]{:S(2)}) copy-start(bf16[48,4096]{1,0:T(8,128)(2,1)} %get-tuple-element.501) | copy-start | bytes 1179652
  90.0 20.6 %all-to-all-start = ((bf16[48,16,256]{2,0,1:T(8,128)(2,1)}), bf16[48,16,256]{2,0,1:T(8,128)(2,1)S(1)}, u32[]{:S(2)}, u32[]{:S(2)}) async-start(bf16[48,16,256]{2,0,1:T(8,128)(2,1)} %bitcast.3), calls=%async_computation | async-start | bytes 786432 | tf_op jit(solution)/shard_map/all_to_all | solution.py:24
  98.7 284.4 %reduce-scatter.7.cloned.1.call-start = ((), (), s32[]{:S(2)}) async-start(), calls=%async_computation.5 | async-start | bytes 8912896 | tf_op jit(solution)/shard_map/reduce_scatter | solution.py:47
  110.7 165.9 %copy-start.5 = (bf16[48,1024]{1,0:T(8,128)(2,1)S(1)}, bf16[48,1024]{1,0:T(8,128)(2,1)}, u32[]{:S(2)}) copy-start(bf16[48,1024]{1,0:T(8,128)(2,1)} %param.13) | copy-start | bytes 294916
  293.8 0.7 copy-start.6
  293.8 89.4 %copy-start.4 = (bf16[64,2048]{1,0:T(8,128)(2,1)S(1)}, bf16[64,2048]{1,0:T(8,128)(2,1)}, u32[]{:S(2)}) copy-start(bf16[64,2048]{1,0:T(8,128)(2,1)} %param.19) | copy-start | bytes 786436
  293.8 91.6 %copy-start.2 = (bf16[48,4096]{1,0:T(8,128)(2,1)S(1)}, bf16[48,4096]{1,0:T(8,128)(2,1)}, u32[]{:S(2)}) copy-start(bf16[48,4096]{1,0:T(8,128)(2,1)} %get-tuple-element.501) | copy-start | bytes 1179652
  293.8 148.1 %all-gather.2.cloned.1.call-start = ((), (), s32[]{:S(2)}) async-start(), calls=%async_computation.3 | async-start | bytes 4456448 | tf_op jit(solution)/shard_map/all_gather | solution.py:58
  385.3 114.1 %reduce-scatter.5.cloned.1.call-start = ((), (), s32[]{:S(2)}) async-start(), calls=%async_computation.4 | async-start | bytes 557056 | tf_op jit(solution)/shard_map/reduce_scatter | solution.py:62
Sparse Core Ops, SparseCore 0:
  293.9 89.1 reduce-scatter.6
  385.5 56.3 all-gather.1
  446.3 53.0 reduce-scatter.4
where the time goes:
time: 514 us; the launch traced here: 508 us
  matrix products  223 us (43%)
  waiting for transfers between devices  181 us (35%)
  local copies, waits for them, and re-layouts  43.5 us (8%)
  blocking collectives  23.3 us (5%)
  other arithmetic  14.4 us (3%)
  between operations  13.9 us (3%)
  starting transfers between devices  8.84 us (2%)
    dot_general x8, matrix products, block_sums(): return jnp.dot(lookup, table, preferred_element_type=jnp.float32)  164 us
    reduce_scatter x1, waiting for transfers between devices, body(): lax.psum_scatter(partial_sum, 'feat', scatter_dimension=0, tiled=True)  88.7 us
    all_gather x1, waiting for transfers between devices, body(): lax.all_gather(grad_pre, 'feat', axis=0, tiled=True)  56.5 us
    dot_general x16, matrix products, pick_list(): jnp.dot(features, table, preferred_element_type=jnp.float32)  41 us
    dynamic_slice x32, local copies, waits for them, and re-layouts, body(): picked = lax.map(pick_list, (boundary[0], counts[0]))  31.1 us
    reduce_scatter x1, waiting for transfers between devices, body(): lax.psum_scatter(grad_terms, 'vertex', scatter_dimension=1, tiled=True)  29.4 us
    psum x1, blocking collectives, body(): bias_sum = lax.psum(jnp.sum(grad_pre.astype(jnp.float32), axis=1), 'vertex')  23.3 us
    unnamed x18, local copies, waits for them, and re-layouts  11.3 us
  transfers between devices with their start and end apart: 4, of which 4 were waited for; matrix products, arithmetic and copies ran while one was open for 1% of the time, Pallas kernels for 0%

commit v1 on v0

v1 whole, which is shorter than its diff:
```python
import functools
import math

import jax
import jax.numpy as jnp
from jax import lax
from jax.experimental import pallas as pl
from jax.experimental.pallas import tpu as pltpu
from jax.sharding import PartitionSpec as P

LOW = 256
UNROLL = 8
FIRST = 3
PAD = 32
GROUP = 8
VMEM = 60 * 1024 * 1024
NT = (((1,), (1,)), ((), ()))
TN = (((0,), (0,)), ((), ()))


def one_hot(keys, rows):
    width = keys.shape[1]
    wide = jnp.broadcast_to(keys, (16, width)).astype(jnp.bfloat16)
    base = lax.broadcasted_iota(jnp.int32, (rows, width), 0).astype(jnp.float32).astype(jnp.bfloat16)
    base = base.reshape(rows // 16, 16, width)
    hit = base == wide[None]
    return jnp.where(hit, jnp.bfloat16(1), jnp.bfloat16(0)).reshape(rows, width)


def pick_kernel(features_ref, boundary_ref, counts_ref, out_ref, rows_ref):
    columns, nodes = features_ref.shape
    groups = nodes // LOW
    lists, capacity = boundary_ref.shape
    for high in range(groups):
        rows_ref[pl.ds(high * columns, columns), :] = features_ref[:, pl.ds(high * LOW, LOW)]
    slot = lax.broadcasted_iota(jnp.int32, (1, capacity), 1)

    def one_list(p):
        listed = boundary_ref[pl.ds(p, 1), :]
        used = slot < counts_ref[0, p]
        high = jnp.where(used, listed // LOW, -1)
        low = (listed % LOW).astype(jnp.float32)
        found = jnp.dot(rows_ref[...], one_hot(low, LOW), preferred_element_type=jnp.float32)
        total = jnp.zeros((columns, capacity), jnp.float32)
        for group in range(groups):
            total = total + jnp.where(high == group, found[group * columns:(group + 1) * columns], 0.0)
        out_ref[p] = total.astype(out_ref.dtype)

    def some_lists(i, carry):
        for k in range(4):
            one_list(4 * i + k)
        return carry

    lax.fori_loop(0, lists // 4, some_lists, 0)


def pick(features, boundary, counts):
    columns, nodes = features.shape
    lists, capacity = boundary.shape
    vm = pl.BlockSpec(memory_space=pltpu.VMEM)
    return pl.pallas_call(
        pick_kernel,
        out_shape=jax.ShapeDtypeStruct((lists, columns, capacity), jnp.bfloat16),
        in_specs=[vm, vm, pl.BlockSpec(memory_space=pltpu.SMEM)],
        out_specs=vm,
        scratch_shapes=[pltpu.VMEM((columns * nodes // LOW, LOW), jnp.bfloat16)],
        compiler_params=pltpu.CompilerParams(vmem_limit_bytes=VMEM),
        name="pick",
    )(features, boundary, counts)


def pack_kernel(parity_ref, features_ref, neigh_weight_ref, self_weight_ref, cotangent_ref, bias_ref,
                inputs_ref, traded_ref):
    shares, _, width = inputs_ref.shape
    half = features_ref.shape[1] // 2
    wide = (width - half) // 2
    for share in range(shares):
        inputs_ref[share, :, pl.ds(0, half)] = features_ref[:, pl.ds((share % 2) * half, half)]
        at = pl.ds((share // 2) * wide, wide)
        inputs_ref[share, :, pl.ds(half, wide)] = neigh_weight_ref[:, at]
        inputs_ref[share, :, pl.ds(half + wide, wide)] = self_weight_ref[:, at]
    traded_ref[:, pl.ds(0, half)] = cotangent_ref[:, pl.ds(pl.multiple_of((1 - parity_ref[0]) * half, half), half)]
    hidden, rest = traded_ref.shape[0], traded_ref.shape[1] - half
    traded_ref[:, pl.ds(half, rest)] = jnp.broadcast_to(bias_ref[...], (hidden, rest))


def pack(parity, features, neigh_weight, self_weight, cotangent, bias, shares):
    columns = features.shape[0]
    hidden, seed_count = cotangent.shape
    half = seed_count // 2
    whole = lambda i: (0, 0)
    return pl.pallas_call(
        pack_kernel,
        grid=(1,),
        out_shape=(jax.ShapeDtypeStruct((shares, columns, half + 4 * hidden), jnp.bfloat16),
                   jax.ShapeDtypeStruct((hidden, half + 128), jnp.bfloat16)),
        in_specs=[pl.BlockSpec(memory_space=pltpu.SMEM),
                  pl.BlockSpec((columns, seed_count), whole),
                  pl.BlockSpec(neigh_weight.shape, whole),
                  pl.BlockSpec(self_weight.shape, whole),
                  pl.BlockSpec(cotangent.shape, whole),
                  pl.BlockSpec(bias.shape, whole)],
        out_specs=(pl.BlockSpec((shares, columns, half + 4 * hidden), lambda i: (0, 0, 0)),
                   pl.BlockSpec((hidden, half + 128), whole)),
        compiler_params=pltpu.CompilerParams(vmem_limit_bytes=VMEM),
        name="pack",
    )(parity, features, neigh_weight, self_weight, cotangent, bias)


def fill_table(first_group, groups, rank_ref, low_ref, store):
    def pairs(i, carry):
        for unrolled in range(UNROLL):
            pair = i * UNROLL + unrolled
            found = []
            for k in range(2):
                group = first_group + 2 * pair + k
                left = one_hot(rank_ref[pl.ds(group, 1), :], rank_ref.shape[1])
                right = one_hot(low_ref[pl.ds(group, 1), :], LOW)
                table = lax.dot_general(left, right, NT, preferred_element_type=jnp.float32)
                found.append(table.reshape(table.shape[0] // GROUP, GROUP, LOW))
            rows = pl.ds(pl.multiple_of(pair * 2 * GROUP, 2 * GROUP), 2 * GROUP)
            store(rows, jnp.concatenate(found, axis=1).astype(jnp.bfloat16))
        return carry

    lax.fori_loop(0, groups // 2 // UNROLL, pairs, 0)


def table_kernel(neighbors_ref, features_ref, remote_ref, local_ref, rank_ref, low_ref, local_table_ref):
    slot_count, seed_count = neighbors_ref.shape
    group_count = seed_count // GROUP
    rows, half = local_table_ref.shape
    highs = half // LOW
    step = pl.program_id(0)

    @pl.when(step == 0)
    def _():
        ranks = []
        lows = []
        for member in range(GROUP):
            value = neighbors_ref[:, pl.ds(member * group_count, group_count)]
            value = jnp.concatenate(
                [value, jnp.full((PAD - slot_count, group_count), -1, jnp.int32)], axis=0)
            rank = jnp.where(value < 0, -1, (value // LOW) * GROUP + member)
            ranks.append(rank.astype(jnp.float32))
            lows.append((value % LOW).astype(jnp.float32))
        rank_ref[...] = jnp.concatenate(ranks, axis=0).T
        low_ref[...] = jnp.concatenate(lows, axis=0).T

    def store(at, table):
        for high in range(highs):
            local_table_ref[at, pl.ds(high * LOW, LOW)] = table[high]
            remote_ref[at, pl.ds(high * LOW, LOW)] = table[highs + high]

    groups = rows // GROUP
    fill_table(step * groups, groups, rank_ref, low_ref, store)
    local_ref[...] = lax.dot_general(
        local_table_ref[...], features_ref[...], NT, preferred_element_type=jnp.float32)


def first_tables(neighbors, features, blocks, rows=256):
    slot_count, seed_count = neighbors.shape
    columns, nodes = features.shape
    group_count = seed_count // GROUP
    keys = jax.ShapeDtypeStruct((group_count, GROUP * PAD), jnp.float32)
    whole = lambda i: (0, 0)
    return pl.pallas_call(
        table_kernel,
        grid=(blocks,),
        out_shape=(jax.ShapeDtypeStruct((blocks * rows, nodes), jnp.bfloat16),
                   jax.ShapeDtypeStruct((blocks * rows, columns), jnp.float32), keys, keys),
        in_specs=[pl.BlockSpec((slot_count, seed_count), whole), pl.BlockSpec((columns, nodes), whole)],
        out_specs=(pl.BlockSpec((rows, nodes), lambda i: (i, 0)),
                   pl.BlockSpec((rows, columns), lambda i: (i, 0)),
                   pl.BlockSpec(keys.shape, whole), pl.BlockSpec(keys.shape, whole)),
        scratch_shapes=[pltpu.VMEM((rows, nodes), jnp.bfloat16)],
        compiler_params=pltpu.CompilerParams(vmem_limit_bytes=VMEM),
        name="first_tables",
    )(neighbors, features)


def mean_kernel(rows, remote_ref, incoming_ref, local_ref, rank_ref, low_ref, neighbors_ref, features_ref,
                out_ref, lookup_ref, sum_ref, table_ref, held_ref, sems):
    sources, columns, capacity = incoming_ref.shape
    nodes = features_ref.shape[1]
    seed_count = sum_ref.shape[0]
    group_count = seed_count // GROUP
    blocks = held_ref.shape[0]
    copies = [
        pltpu.make_async_copy(remote_ref.at[pl.ds(k * rows, rows), :], held_ref.at[k], sems.at[k])
        for k in range(blocks)]
    for copy in copies:
        copy.start()
    lookup_ref[:, pl.ds(0, nodes)] = features_ref[...]
    for source in range(sources):
        lookup_ref[:, pl.ds(nodes + source * capacity, capacity)] = incoming_ref[source]

    def store(at, table):
        for high in range(table.shape[0]):
            table_ref[at, pl.ds(high * LOW, LOW)] = table[high]

    def build(k, carry):
        fill_table(k * (rows // GROUP), rows // GROUP, rank_ref, low_ref, store)
        sum_ref[pl.ds(pl.multiple_of(k * rows, rows), rows), pl.ds(0, columns)] = lax.dot_general(
            table_ref[...], lookup_ref[...], NT, preferred_element_type=jnp.float32)
        return carry

    lax.fori_loop(blocks, seed_count // rows, build, 0)
    for k in range(blocks):
        copies[k].wait()
        at = pl.ds(k * rows, rows)
        sum_ref[at, pl.ds(0, columns)] = local_ref[at, :] + lax.dot_general(
            held_ref[k], lookup_ref[:, nodes:], NT, preferred_element_type=jnp.float32)

    degree = jnp.sum(jnp.where(neighbors_ref[...] >= 0, 1.0, 0.0), axis=0, keepdims=True)
    shares, _, half = out_ref.shape
    for member in range(GROUP):
        mine = sum_ref[pl.ds(member, group_count, stride=GROUP), :].T[:columns]
        start = member * group_count
        mine = mine / degree[:, start:start + group_count]
        mine = mine.astype(jnp.bfloat16)
        for share in range(start // half, shares, 2):
            out_ref[share, :, pl.ds(start % half, group_count)] = mine


def neighbor_mean(remote, incoming, local, rank, low, neighbors, features, shares, rows=256):
    slot_count, seed_count = neighbors.shape
    columns, nodes = features.shape
    sources, _, capacity = incoming.shape
    blocks = remote.shape[0] // rows
    lookup_width = nodes + sources * capacity
    vm = pl.BlockSpec(memory_space=pltpu.VMEM)
    return pl.pallas_call(
        functools.partial(mean_kernel, rows),
        out_shape=jax.ShapeDtypeStruct((shares, columns, seed_count // 2), jnp.bfloat16),
        in_specs=[pl.BlockSpec(memory_space=pl.ANY)] + [vm] * 6,
        out_specs=vm,
        scratch_shapes=[pltpu.VMEM((columns, lookup_width), jnp.bfloat16),
                        pltpu.VMEM((seed_count, 128), jnp.float32),
                        pltpu.VMEM((rows, lookup_width), jnp.bfloat16),
                        pltpu.VMEM((blocks, rows, nodes), jnp.bfloat16),
                        pltpu.SemaphoreType.DMA((blocks,))],
        compiler_params=pltpu.CompilerParams(vmem_limit_bytes=VMEM),
        name="mean",
    )(remote, incoming, local, rank, low, neighbors, features)


def layer_kernel(parity_ref, own_ref, mean_ref, neigh_weight_ref, self_weight_ref, bias_ref, cotangent_ref,
                 traded_ref, traded_bias_ref, kept_ref, sent_ref, grad_ref, total_ref, sums_ref):
    step = pl.program_id(0)
    odd = parity_ref[0] == 1
    hidden = cotangent_ref.shape[0]

    @pl.when(step == 0)
    def _():
        total_ref[...] = jnp.zeros_like(total_ref)
        sums_ref[...] = jnp.zeros_like(sums_ref)

    def ordered(mine, other):
        return jnp.concatenate([jnp.where(odd, other, mine), jnp.where(odd, mine, other)], axis=0)

    bias = ordered(bias_ref[...].astype(jnp.float32), traded_bias_ref[:, :1].astype(jnp.float32))
    cotangent = ordered(cotangent_ref[...].astype(jnp.float32), traded_ref[...].astype(jnp.float32))
    preact = (
        lax.dot_general(neigh_weight_ref[...], mean_ref[...], TN, preferred_element_type=jnp.float32)
        + lax.dot_general(self_weight_ref[...], own_ref[...], TN, preferred_element_type=jnp.float32)
        + bias
    )
    decay = jnp.exp(jnp.minimum(preact, 0.0))
    activation = jnp.where(preact > 0, preact, decay - 1.0)
    kept_ref[...] = jnp.where(odd, activation[hidden:], activation[:hidden]).astype(jnp.bfloat16)
    sent_ref[...] = jnp.where(odd, activation[:hidden], activation[hidden:]).astype(jnp.bfloat16)
    slope = jnp.where(preact > 0, 1.0, decay)
    grad_pre = (cotangent * slope).astype(jnp.bfloat16)
    pair = 2 * hidden
    total_ref[:, pl.ds(0, pair)] += lax.dot_general(
        mean_ref[...], grad_pre, NT, preferred_element_type=jnp.float32)
    total_ref[:, pl.ds(pair, pair)] += lax.dot_general(
        own_ref[...], grad_pre, NT, preferred_element_type=jnp.float32)
    sums_ref[...] += lax.dot_general(
        jnp.ones((sums_ref.shape[0], grad_pre.shape[1]), jnp.bfloat16), grad_pre, NT,
        preferred_element_type=jnp.float32)

    @pl.when(step == pl.num_programs(0) - 1)
    def _():
        shares, rows, _ = grad_ref.shape
        columns = total_ref.shape[0] // shares
        sums = sums_ref[...]
        high = sums.astype(jnp.bfloat16).astype(jnp.float32)
        row = lax.broadcasted_iota(jnp.int32, sums.shape, 0)
        extra = jnp.where(row == 0, high, jnp.where(row == 1, sums - high, 0.0))
        extra = jnp.concatenate([extra, jnp.zeros_like(extra)], axis=1).astype(jnp.bfloat16)
        for share in range(shares):
            grad_ref[share, pl.ds(0, columns), :] = total_ref[
                pl.ds(share * columns, columns), :].astype(jnp.bfloat16)
            grad_ref[share, pl.ds(columns, rows - columns), :] = extra


def layer(parity, inputs, mean, bias, cotangent, traded, shares, block=512):
    features, half = mean.shape
    hidden = cotangent.shape[0]
    pair = 2 * hidden
    extra = 16
    blocks = half // block
    whole = lambda i, parity: (0, 0)
    part = lambda i, parity: (0, i)
    grads = (shares, features // shares + extra, 2 * pair)
    return pl.pallas_call(
        layer_kernel,
        grid_spec=pltpu.PrefetchScalarGridSpec(
            num_scalar_prefetch=1,
            grid=(blocks,),
            in_specs=[pl.BlockSpec((features, block), part),
                      pl.BlockSpec((features, block), part),
                      pl.BlockSpec((features, pair), lambda i, parity: (0, half // pair)),
                      pl.BlockSpec((features, pair), lambda i, parity: (0, half // pair + 1)),
                      pl.BlockSpec((hidden, 1), whole),
                      pl.BlockSpec((hidden, block), lambda i, parity: (0, i + parity[0] * blocks)),
                      pl.BlockSpec((hidden, block), part),
                      pl.BlockSpec((hidden, 128), lambda i, parity: (0, half // 128))],
            out_specs=(pl.BlockSpec((hidden, block), part),
                       pl.BlockSpec((hidden, block), part),
                       pl.BlockSpec(grads, lambda i, parity: (0, 0, 0))),
            scratch_shapes=[pltpu.VMEM((features, 2 * pair), jnp.float32),
                            pltpu.VMEM((extra, pair), jnp.float32)]),
        out_shape=(jax.ShapeDtypeStruct((hidden, half), jnp.bfloat16),
                   jax.ShapeDtypeStruct((hidden, half), jnp.bfloat16),
                   jax.ShapeDtypeStruct(grads, jnp.bfloat16)),
        compiler_params=pltpu.CompilerParams(vmem_limit_bytes=VMEM),
        name="layer",
    )(parity, inputs, mean, inputs, inputs, bias, cotangent, traded, traded)


def body(features, neigh_weight, self_weight, bias, neighbors, boundary, counts, cotangent):
    columns, nodes = features.shape
    partitions = lax.axis_size("vertex")
    shares = lax.axis_size("feat")
    seed_count = neighbors.shape[1]
    hidden = cotangent.shape[0]
    pair = 2 * hidden
    odd = lax.axis_index("feat") % 2
    parity = odd.astype(jnp.int32).reshape(1)
    bias = bias.reshape(hidden, 1)
    trade = [(f, f ^ 1) for f in range(shares)]

    outgoing = pick(features, boundary[0], counts)
    incoming = lax.all_to_all(outgoing, "vertex", split_axis=0, concat_axis=0, tiled=True)
    _, late = lax.optimization_barrier((outgoing, parity))
    inputs, traded = pack(late, features, neigh_weight, self_weight, cotangent, bias, shares)
    remote, local, rank, low = first_tables(neighbors, features, FIRST)
    inputs, _ = lax.optimization_barrier((inputs, local))
    inputs = lax.all_to_all(inputs, "feat", split_axis=0, concat_axis=0, tiled=True)
    inputs = inputs.reshape(shares * columns, inputs.shape[2])
    traded = lax.ppermute(traded, "feat", trade)
    mean = neighbor_mean(remote, incoming, local, rank, low, neighbors, features, shares)
    mean = lax.all_to_all(mean, "feat", split_axis=0, concat_axis=0, tiled=True)
    mean = mean.reshape(shares * columns, mean.shape[2])
    kept, sent, grad = layer(parity, inputs, mean, bias, cotangent, traded, shares)
    grad = lax.all_to_all(grad, "vertex", split_axis=0, concat_axis=0, tiled=True)
    other = lax.ppermute(sent, "feat", trade)
    activation = jnp.concatenate(
        [jnp.where(odd == 1, other, kept), jnp.where(odd == 1, kept, other)], axis=1)

    factor = 1.0 / math.sqrt(seed_count * partitions)
    grad = jnp.sum(grad.astype(jnp.float32), axis=0) * factor
    bias_sum = grad[columns, :pair] + grad[columns + 1, :pair]
    neigh, own = grad[:columns, :pair], grad[:columns, pair:]
    even_part = jnp.concatenate([neigh[:, :hidden], own[:, :hidden]], axis=1)
    odd_part = jnp.concatenate([neigh[:, hidden:], own[:, hidden:]], axis=1)
    pieces = []
    for k in range(2):
        route = [(v * shares + f, (2 * (f // 2) + (f % 2 ^ k)) * shares + v)
                 for v in range(partitions) for f in range(shares)]
        piece = jnp.where((odd ^ k) == 1, odd_part, even_part)
        pieces.append(lax.ppermute(piece, ("vertex", "feat"), route))
    grad = pieces[0] + pieces[1]
    mine = jnp.where(odd == 1, bias_sum[hidden:], bias_sum[:hidden])
    theirs = jnp.where(odd == 1, bias_sum[:hidden], bias_sum[hidden:])
    bias_out = mine + lax.ppermute(theirs, "feat", trade)
    return activation, grad[:, :hidden], grad[:, hidden:], bias_out


def solution(mesh):
    placed = (
        P("feat", "vertex"),
        P("feat", None),
        P("feat", None),
        P("feat"),
        P(None, "vertex"),
        P("vertex", None, None),
        P("vertex", None),
        P("feat", "vertex"),
    )
    return jax.shard_map(
        body,
        mesh=mesh,
        in_specs=placed,
        out_specs=(P("feat", "vertex"), P("feat", "vertex"), P("feat", "vertex"), P("feat")),
        check_vma=False,
    )
```

time: 514 us -> 139 us (0.27)
  matrix products: 223 us -> 0 us
  waiting for transfers between devices: 181 us -> 45.2 us
  local copies, waits for them, and re-layouts: 43.5 us -> 4.05 us
  Pallas kernels: 0 us -> 39 us
  starting transfers between devices: 8.84 us -> 45.6 us
  blocking collectives: 23.3 us -> 0 us
  between operations: 13.9 us -> 0.7 us
  other arithmetic: 14.4 us -> 2.48 us
    dot_general x27 -> x0, matrix products: 223 us -> none  [the longest x8 164 us: block_sums(): return jnp.dot(lookup, table, preferred_element_type=jnp.float32)]
    reduce_scatter x2 -> x0, waiting for transfers between devices: 118 us -> none  [the longest x1 88.7 us: body(): lax.psum_scatter(partial_sum, 'feat', scatter_dimension=0, tiled=True)]
    all_gather x1 -> x0, waiting for transfers between devices: 56.5 us -> none  [body(): lax.all_gather(grad_pre, 'feat', axis=0, tiled=True)]
    pallas_call x0 -> x5, Pallas kernels: none -> 39 us  [the longest x1 18.9 us: neighbor_mean(): pl.pallas_call(functools.partial(mean_kernel, rows), out_shape=jax.ShapeD...]
    dynamic_slice x32 -> x0, local copies, waits for them, and re-layouts: 31.1 us -> none  [body(): picked = lax.map(pick_list, (boundary[0], counts[0]))]
    ppermute x0 -> x5, waiting for transfers between devices: none -> 30.5 us  [the longest x1 19.2 us: body(): traded = lax.ppermute(traded, 'feat', trade)]
    psum x1 -> x0, blocking collectives: 23.3 us -> none  [body(): bias_sum = lax.psum(jnp.sum(grad_pre.astype(jnp.float32), axis=1), 'vertex')]
    all_to_all x1 -> x4, starting transfers between devices: 8.72 us -> 31.7 us  [the longest x1 9.27 us: body(): lax.all_to_all(grad, 'vertex', split_axis=0, concat_axis=0, tiled=True)]
  transfers between devices with their start and end apart: 4 -> 9, of which waited for: 4 -> 5; matrix products, arithmetic and copies ran while one was open for 1% -> 3% of each run, Pallas kernels for 0% -> 22%
where the time goes in v1:
time: 139 us; the launch traced here: 137 us
  starting transfers between devices  45.6 us (33%)
  waiting for transfers between devices  45.2 us (33%)
  Pallas kernels  39 us (28%)
  local copies, waits for them, and re-layouts  4.05 us (3%)
  other arithmetic  2.48 us (2%)
    ppermute x1, waiting for transfers between devices, body(): traded = lax.ppermute(traded, 'feat', trade)  19.2 us
    pallas_call x1, Pallas kernels, neighbor_mean(): pl.pallas_call(functools.partial(mean_kernel, rows), out_shape=jax.ShapeD...  18.9 us
    ppermute x2, starting transfers between devices, body(): pieces.append(lax.ppermute(piece, ('vertex', 'feat'), route))  11.3 us
    all_to_all x1, starting transfers between devices, body(): lax.all_to_all(grad, 'vertex', split_axis=0, concat_axis=0, tiled=True)  9.27 us
    pallas_call x1, Pallas kernels, first_tables(): pl.pallas_call(table_kernel, grid=(blocks,), out_shape=(jax.ShapeDtypeStr...  8.82 us
    all_to_all x1, starting transfers between devices, body(): lax.all_to_all(outgoing, 'vertex', split_axis=0, concat_axis=0, tiled=True)  8.59 us
    all_to_all x1, waiting for transfers between devices, body(): lax.all_to_all(inputs, 'feat', split_axis=0, concat_axis=0, tiled=True)  7.74 us
    all_to_all x1, starting transfers between devices, body(): lax.all_to_all(inputs, 'feat', split_axis=0, concat_axis=0, tiled=True)  7.45 us
  transfers between devices with their start and end apart: 9, of which 5 were waited for; matrix products, arithmetic and copies ran while one was open for 3% of the time, Pallas kernels for 22%

profile of v1, /device:TPU:36, one launch (start us, length us, event | category | flops | bytes accessed | tf_op | source)
XLA Modules:
  0.0 137.1 jit_solution(15437253040056944853)
XLA Ops:
  0.6 4.2 %pick.1 = bf16[16,48,256]{2,1,0:T(8,128)(2,1)} custom-call(bf16[48,4096]{1,0:T(8,128)(2,1)} %features_ref.7, s32[16,256]{1,0:T(8,128)} %bitcast.15, s32[1,16]{1,0:T(1,128)} %counts_ref.1), custom_call_target="tpu_custom_call" | custom-call | tf_op jit(solution)/shard_map/pick/pallas_call | solution.py:61
  4.8 8.6 %all-to-all-start.1 = ((bf16[16,48,256]{2,1,0:T(8,128)(2,1)}), bf16[16,48,256]{2,1,0:T(8,128)(2,1)S(1)}, u32[]{:S(2)}, u32[]{:S(2)}) async-start(bf16[16,48,256]{2,1,0:T(8,128)(2,1)} %pick.1), calls=%async_computation.1 | async-start | bytes 786432 | tf_op jit(solution)/shard_map/all_to_all | solution.py:346
  13.4 1.4 copy.12.bias_ref
  14.7 8.8 %first_tables.1 = (bf16[768,4096]{1,0:T(8,128)(2,1)}, f32[768,48]{1,0:T(8,128)}, f32[256,256]{1,0:T(8,128)}, f32[256,256]{1,0:T(8,128)}) custom-call(s32[25,2048]{1,0:T(8,128)} %neighbors_ref.3, bf16[48,4096]{1,0:T(8,128)(2,1)} %features_ref.7), custom_call_target="tpu_custom_call" | custom-call | tf_op jit(solution)/shard_map/first_tables/pallas_call | solution.py:166
  23.6 2.6 %pack.1 = (bf16[16,48,1280]{2,1,0:T(8,128)(2,1)}, bf16[64,1152]{1,0:T(8,128)(2,1)}) custom-call(s32[1]{0:T(128)} %bitcast.parity_ref, bf16[48,4096]{1,0:T(8,128)(2,1)} %features_ref.7, bf16[48,1024]{1,0:T(8,128)(2,1)} %neigh_weight_ref.1, bf16[48,1024]{1,0:T(8,128)(2,1)} %self_weight_ref.1, bf16[64,2048]{1,0:T(8,128)(2,1)} %cotangent_ref.3, ...), custom_call_target="tpu_custom_call" | custom-call | tf_op jit(solution)/shard_map/pack/pallas_call | solution.py:92
  26.2 0.0 all-to-all-done.1.incoming_ref
  26.2 0.0 copy-start.2
  26.2 0.8 copy-done.2
  26.9 7.4 %all-to-all-start = ((bf16[16,48,1280]{2,1,0:T(8,128)(2,1)}), bf16[16,48,1280]{2,1,0:T(8,128)(2,1)S(1)}, u32[]{:S(2)}, u32[]{:S(2)}) async-start(bf16[16,48,1280]{2,1,0:T(8,128)(2,1)} %get-tuple-element.18), calls=%async_computation | async-start | bytes 3932160 | tf_op jit(solution)/shard_map/all_to_all | solution.py:351
  34.4 18.9 %mean.1 = bf16[16,48,1024]{2,1,0:T(8,128)(2,1)} custom-call(bf16[768,4096]{1,0:T(8,128)(2,1)} %get-tuple-element.19.remote_ref, bf16[16,48,256]{2,1,0:T(8,128)(2,1)} %copy-done.2, f32[768,48]{1,0:T(8,128)} %get-tuple-element.17.local_ref, f32[256,256]{1,0:T(8,128)} %get-tuple-element.20.rank_ref, f32[256,256]{1,0:T(8,128)} %get-tuple-element.21.low_ref, ...), custom_call_target="tpu_custom_call" | custom-call | tf_op jit(solution)/shard_map/mean/pallas_call | solution.py:232
  53.3 7.7 %all-to-all-done = bf16[16,48,1280]{2,1,0:T(8,128)(2,1)S(1)} async-done(((bf16[16,48,1280]{2,1,0:T(8,128)(2,1)}), bf16[16,48,1280]{2,1,0:T(8,128)(2,1)S(1)}, u32[]{:S(2)}, u32[]{:S(2)}) %all-to-all-start) | async-done | bytes 1966112 | tf_op jit(solution)/shard_map/all_to_all | solution.py:351
  61.0 0.0 copy-start
  61.0 6.4 %all-to-all-start.2 = ((bf16[16,48,1024]{2,1,0:T(8,128)(2,1)}), bf16[16,48,1024]{2,1,0:T(8,128)(2,1)S(1)}, u32[]{:S(2)}, u32[]{:S(2)}) async-start(bf16[16,48,1024]{2,1,0:T(8,128)(2,1)} %mean.1), calls=%async_computation.2 | async-start | bytes 3145728 | tf_op jit(solution)/shard_map/all_to_all | solution.py:355
  67.4 1.5 %collective-permute-start = (bf16[64,1152]{1,0:T(8,128)(2,1)}, bf16[64,1152]{1,0:T(8,128)(2,1)}, u32[]{:S(2)}, u32[]{:S(2)}) collective-permute-start(bf16[64,1152]{1,0:T(8,128)(2,1)} %get-tuple-element.22), channel_id=1, source_target_pairs={{0,1},{1,0},{2,3},{3,2},{4,5},{5,4},{6,7},{7,6},{8,9},{9,8},{10,11... | collective-permute-start | bytes 442376 | tf_op jit(solution)/shard_map/ppermute | solution.py:353
  68.9 19.2 %collective-permute-done.traded_ref.traded_bias_ref = bf16[64,1152]{1,0:T(8,128)(2,1)} collective-permute-done((bf16[64,1152]{1,0:T(8,128)(2,1)}, bf16[64,1152]{1,0:T(8,128)(2,1)}, u32[]{:S(2)}, u32[]{:S(2)}) %collective-permute-start) | collective-permute-done | bytes 147488 | tf_op jit(solution)/shard_map/ppermute | solution.py:353
  88.1 0.0 all-to-all-done.2
  88.1 0.0 copy-start.1
  88.1 0.0 copy-done
  88.1 1.2 copy-done.1
  89.2 4.6 %layer.1 = (bf16[64,1024]{1,0:T(8,128)(2,1)}, bf16[64,1024]{1,0:T(8,128)(2,1)}, bf16[16,64,256]{2,1,0:T(8,128)(2,1)}) custom-call(s32[1]{0:T(128)} %bitcast.parity_ref, bf16[768,1280]{1,0:T(8,128)(2,1)} %bitcast.11, bf16[768,1024]{1,0:T(8,128)(2,1)} %bitcast.14, bf16[768,1280]{1,0:T(8,128)(2,1)} %bitcast.12, bf16[768,1280]{1,0:T(8,128)(2,1)} %bitcast.13, ...), custom_call_target="tpu_custom_call" | custom-call | tf_op jit(solution)/shard_map/layer/pallas_call | solution.py:307
  93.8 9.3 %all-to-all-start.3 = ((bf16[16,64,256]{2,1,0:T(8,128)(2,1)}), bf16[16,64,256]{2,1,0:T(8,128)(2,1)S(1)}, u32[]{:S(2)}, u32[]{:S(2)}) async-start(bf16[16,64,256]{2,1,0:T(8,128)(2,1)} %get-tuple-element.25), calls=%async_computation.3 | async-start | bytes 1048576 | tf_op jit(solution)/shard_map/all_to_all | solution.py:358
  103.1 0.6 collective-permute-start.1
  103.7 5.2 %collective-permute-done.1 = bf16[64,1024]{1,0:T(8,128)(2,1)S(1)} collective-permute-done((bf16[64,1024]{1,0:T(8,128)(2,1)}, bf16[64,1024]{1,0:T(8,128)(2,1)S(1)}, u32[]{:S(2)}, u32[]{:S(2)}) %collective-permute-start.1) | collective-permute-done | bytes 131104 | tf_op jit(solution)/shard_map/ppermute | solution.py:359
  108.9 0.9 broadcast_select_fusion.1
  109.8 0.7 pad_maximum_fusion
  110.5 6.9 %all-to-all-done.3 = bf16[16,64,256]{2,1,0:T(8,128)(2,1)S(1)} async-done(((bf16[16,64,256]{2,1,0:T(8,128)(2,1)}), bf16[16,64,256]{2,1,0:T(8,128)(2,1)S(1)}, u32[]{:S(2)}, u32[]{:S(2)}) %all-to-all-start.3) | async-done | bytes 524320 | tf_op jit(solution)/shard_map/all_to_all | solution.py:358
  117.4 0.1 convert_reduce_fusion
  117.5 0.1 fusion.3
  117.6 0.1 fusion.2
  117.7 0.6 collective-permute-start.4
  118.3 0.1 broadcast_select_fusion.2
  118.4 4.5 %collective-permute-start.3 = (f32[48,128]{1,0:T(8,128)S(1)}, f32[48,128]{1,0:T(8,128)S(1)}, u32[]{:S(2)}, u32[]{:S(2)}) collective-permute-start(f32[48,128]{1,0:T(8,128)S(1)} %get-tuple-element.28), channel_id=1, source_target_pairs={{0,16},{1,0},{2,48},{3,32},{4,80},{5,64},{6,112},{7,96},{8,144},{9... | collective-permute-start | bytes 73736 | tf_op jit(solution)/shard_map/ppermute | solution.py:374
  122.9 6.7 %collective-permute-start.2 = (f32[48,128]{1,0:T(8,128)S(1)}, f32[48,128]{1,0:T(8,128)S(1)}, u32[]{:S(2)}, u32[]{:S(2)}) collective-permute-start(f32[48,128]{1,0:T(8,128)S(1)} %get-tuple-element.29), channel_id=1, source_target_pairs={{0,0},{1,16},{2,32},{3,48},{4,64},{5,80},{6,96},{7,112},{8,128},{9... | collective-permute-start | bytes 73736 | tf_op jit(solution)/shard_map/ppermute | solution.py:374
  129.6 0.0 collective-permute-done.4
  129.6 0.6 fusion.1
  130.2 0.0 collective-permute-done.3
  130.2 6.2 %collective-permute-done.2 = f32[48,128]{1,0:T(8,128)S(1)} collective-permute-done((f32[48,128]{1,0:T(8,128)S(1)}, f32[48,128]{1,0:T(8,128)S(1)}, u32[]{:S(2)}, u32[]{:S(2)}) %collective-permute-start.2) | collective-permute-done | bytes 24608 | tf_op jit(solution)/shard_map/ppermute | solution.py:374
  136.4 0.7 fusion.4
  (3 shorter events, 0.0 us)
Async XLA Ops:
  4.8 21.4 %all-to-all-start.1 = ((bf16[16,48,256]{2,1,0:T(8,128)(2,1)}), bf16[16,48,256]{2,1,0:T(8,128)(2,1)S(1)}, u32[]{:S(2)}, u32[]{:S(2)}) async-start(bf16[16,48,256]{2,1,0:T(8,128)(2,1)} %pick.1), calls=%async_computation.1 | async-start | bytes 786432 | tf_op jit(solution)/shard_map/all_to_all | solution.py:346
  26.2 0.8 copy-start.2
  26.9 34.1 %all-to-all-start = ((bf16[16,48,1280]{2,1,0:T(8,128)(2,1)}), bf16[16,48,1280]{2,1,0:T(8,128)(2,1)S(1)}, u32[]{:S(2)}, u32[]{:S(2)}) async-start(bf16[16,48,1280]{2,1,0:T(8,128)(2,1)} %get-tuple-element.18), calls=%async_computation | async-start | bytes 3932160 | tf_op jit(solution)/shard_map/all_to_all | solution.py:351
  61.0 27.1 %copy-start = (bf16[16,48,1280]{2,1,0:T(8,128)(2,1)}, bf16[16,48,1280]{2,1,0:T(8,128)(2,1)S(1)}, u32[]{:S(2)}) copy-start(bf16[16,48,1280]{2,1,0:T(8,128)(2,1)S(1)} %all-to-all-done) | copy-start | bytes 5898244
  61.0 27.1 %all-to-all-start.2 = ((bf16[16,48,1024]{2,1,0:T(8,128)(2,1)}), bf16[16,48,1024]{2,1,0:T(8,128)(2,1)S(1)}, u32[]{:S(2)}, u32[]{:S(2)}) async-start(bf16[16,48,1024]{2,1,0:T(8,128)(2,1)} %mean.1), calls=%async_computation.2 | async-start | bytes 3145728 | tf_op jit(solution)/shard_map/all_to_all | solution.py:355
  67.4 20.6 %collective-permute-start = (bf16[64,1152]{1,0:T(8,128)(2,1)}, bf16[64,1152]{1,0:T(8,128)(2,1)}, u32[]{:S(2)}, u32[]{:S(2)}) collective-permute-start(bf16[64,1152]{1,0:T(8,128)(2,1)} %get-tuple-element.22), channel_id=1, source_target_pairs={{0,1},{1,0},{2,3},{3,2},{4,5},{5,4},{6,7},{7,6},{8,9},{9,8},{10,11... | collective-permute-start | bytes 442376 | tf_op jit(solution)/shard_map/ppermute | solution.py:353
  88.1 1.2 copy-start.1
  93.8 23.6 %all-to-all-start.3 = ((bf16[16,64,256]{2,1,0:T(8,128)(2,1)}), bf16[16,64,256]{2,1,0:T(8,128)(2,1)S(1)}, u32[]{:S(2)}, u32[]{:S(2)}) async-start(bf16[16,64,256]{2,1,0:T(8,128)(2,1)} %get-tuple-element.25), calls=%async_computation.3 | async-start | bytes 1048576 | tf_op jit(solution)/shard_map/all_to_all | solution.py:358
  103.1 5.8 %collective-permute-start.1 = (bf16[64,1024]{1,0:T(8,128)(2,1)}, bf16[64,1024]{1,0:T(8,128)(2,1)S(1)}, u32[]{:S(2)}, u32[]{:S(2)}) collective-permute-start(bf16[64,1024]{1,0:T(8,128)(2,1)} %get-tuple-element.23), channel_id=1, source_target_pairs={{0,1},{1,0},{2,3},{3,2},{4,5},{5,4},{6,7},{7,6},{8,9},{9,8},{10,11... | collective-permute-start | bytes 393224 | tf_op jit(solution)/shard_map/ppermute | solution.py:359
  117.7 11.9 %collective-permute-start.4 = (f32[64]{0:T(128)S(1)}, f32[64]{0:T(128)S(1)}, u32[]{:S(2)}, u32[]{:S(2)}) collective-permute-start(f32[64]{0:T(128)S(1)} %fusion.2), channel_id=1, source_target_pairs={{0,1},{1,0},{2,3},{3,2},{4,5},{5,4},{6,7},{7,6},{8,9},{9,8},{10,11... | collective-permute-start | bytes 776 | tf_op jit(solution)/shard_map/ppermute | solution.py:378
  118.4 11.9 %collective-permute-start.3 = (f32[48,128]{1,0:T(8,128)S(1)}, f32[48,128]{1,0:T(8,128)S(1)}, u32[]{:S(2)}, u32[]{:S(2)}) collective-permute-start(f32[48,128]{1,0:T(8,128)S(1)} %get-tuple-element.28), channel_id=1, source_target_pairs={{0,16},{1,0},{2,48},{3,32},{4,80},{5,64},{6,112},{7,96},{8,144},{9... | collective-permute-start | bytes 73736 | tf_op jit(solution)/shard_map/ppermute | solution.py:374
  122.9 13.5 %collective-permute-start.2 = (f32[48,128]{1,0:T(8,128)S(1)}, f32[48,128]{1,0:T(8,128)S(1)}, u32[]{:S(2)}, u32[]{:S(2)}) collective-permute-start(f32[48,128]{1,0:T(8,128)S(1)} %get-tuple-element.29), channel_id=1, source_target_pairs={{0,0},{1,16},{2,32},{3,48},{4,64},{5,80},{6,96},{7,112},{8,128},{9... | collective-permute-start | bytes 73736 | tf_op jit(solution)/shard_map/ppermute | solution.py:374

commit v2 on v1

v2 whole, which is shorter than its diff:
```python
import functools
import math

import jax
import jax.numpy as jnp
from jax import lax
from jax.experimental import pallas as pl
from jax.experimental.pallas import tpu as pltpu
from jax.sharding import PartitionSpec as P

LOW = 256
ONES = jnp.float8_e4m3fn
UNROLL = 8
FIRST = 4
RADIX = 4
PAD = 32
GROUP = 8
EXTRA = 16
VMEM = 60 * 1024 * 1024
NT = (((1,), (1,)), ((), ()))
TN = (((0,), (0,)), ((), ()))


def one_hot(keys, rows):
    width = keys.shape[1]
    wide = jnp.broadcast_to(keys, (16, width)).astype(jnp.bfloat16)
    base = lax.broadcasted_iota(jnp.int32, (rows, width), 0).astype(jnp.float32).astype(jnp.bfloat16)
    base = base.reshape(rows // 16, 16, width)
    hit = base == wide[None]
    return jnp.where(hit, jnp.bfloat16(1), jnp.bfloat16(0)).reshape(rows, width)


def relative(place, j, k):
    return ((place // RADIX + j) % RADIX) * RADIX + (place % RADIX + k) % RADIX


def pick_kernel(place_ref, features_ref, boundary_ref, counts_ref, *refs):
    out_refs, rows_ref = refs[:RADIX], refs[RADIX]
    columns, nodes = features_ref.shape
    groups = nodes // LOW
    capacity = boundary_ref.shape[1]
    for high in range(groups):
        rows_ref[pl.ds(high * columns, columns), :] = features_ref[:, pl.ds(high * LOW, LOW)]
    slot = lax.broadcasted_iota(jnp.int32, (1, capacity), 1)
    for k in range(RADIX):
        for j in range(RADIX):
            p = relative(place_ref[0], j, k)
            listed = boundary_ref[pl.ds(p, 1), :]
            used = slot < counts_ref[0, p]
            high = jnp.where(used, listed >> 8, -1)
            low = (listed & (LOW - 1)).astype(jnp.float32)
            found = jnp.dot(rows_ref[...], one_hot(low, LOW), preferred_element_type=jnp.float32)
            total = jnp.zeros((columns, capacity), jnp.float32)
            for group in range(groups):
                total = total + jnp.where(high == group, found[group * columns:(group + 1) * columns], 0.0)
            out_refs[k][j] = total.astype(jnp.bfloat16)


def pick(place, features, boundary, counts):
    columns, nodes = features.shape
    capacity = boundary.shape[1]
    vm = pl.BlockSpec(memory_space=pltpu.VMEM)
    sm = pl.BlockSpec(memory_space=pltpu.SMEM)
    return pl.pallas_call(
        pick_kernel,
        out_shape=(jax.ShapeDtypeStruct((RADIX, columns, capacity), jnp.bfloat16),) * RADIX,
        in_specs=[sm, vm, vm, sm],
        out_specs=(vm,) * RADIX,
        scratch_shapes=[pltpu.VMEM((columns * nodes // LOW, LOW), jnp.bfloat16)],
        compiler_params=pltpu.CompilerParams(vmem_limit_bytes=VMEM),
        name="pick",
    )(place, features, boundary, counts)


def regroup_kernel(*refs):
    in_refs, out_refs = refs[:RADIX], refs[RADIX:]
    for j, out_ref in enumerate(out_refs, 1):
        for k, in_ref in enumerate(in_refs):
            out_ref[k] = in_ref[j]


def regroup(pieces):
    vm = pl.BlockSpec(memory_space=pltpu.VMEM)
    return pl.pallas_call(
        regroup_kernel,
        out_shape=(jax.ShapeDtypeStruct(pieces[0].shape, jnp.bfloat16),) * (RADIX - 1),
        in_specs=[vm] * RADIX,
        out_specs=(vm,) * (RADIX - 1),
        name="regroup",
    )(*pieces)


def pack_kernel(parity_ref, features_ref, neigh_weight_ref, self_weight_ref, cotangent_ref, bias_ref,
                inputs_ref, traded_ref):
    shares, _, width = inputs_ref.shape
    half = features_ref.shape[1] // 2
    wide = (width - half) // 2
    for share in range(shares):
        inputs_ref[share, :, pl.ds(0, half)] = features_ref[:, pl.ds((share % 2) * half, half)]
        at = pl.ds((share // 2) * wide, wide)
        inputs_ref[share, :, pl.ds(half, wide)] = neigh_weight_ref[:, at]
        inputs_ref[share, :, pl.ds(half + wide, wide)] = self_weight_ref[:, at]
    hidden = cotangent_ref.shape[0]
    traded_ref[pl.ds(0, hidden), :] = cotangent_ref[
        :, pl.ds(pl.multiple_of((1 - parity_ref[0]) * half, half), half)]
    bias = jnp.concatenate([bias_ref[...], jnp.zeros((1, half - hidden), jnp.bfloat16)], axis=1)
    traded_ref[pl.ds(hidden, EXTRA), :] = jnp.broadcast_to(bias.astype(jnp.float32), (EXTRA, half)).astype(jnp.bfloat16)


def pack(parity, features, neigh_weight, self_weight, cotangent, bias, shares):
    columns = features.shape[0]
    hidden, seed_count = cotangent.shape
    half = seed_count // 2
    whole = lambda i: (0, 0)
    return pl.pallas_call(
        pack_kernel,
        grid=(1,),
        out_shape=(jax.ShapeDtypeStruct((shares, columns, half + 4 * hidden), jnp.bfloat16),
                   jax.ShapeDtypeStruct((hidden + EXTRA, half), jnp.bfloat16)),
        in_specs=[pl.BlockSpec(memory_space=pltpu.SMEM),
                  pl.BlockSpec((columns, seed_count), whole),
                  pl.BlockSpec(neigh_weight.shape, whole),
                  pl.BlockSpec(self_weight.shape, whole),
                  pl.BlockSpec(cotangent.shape, whole),
                  pl.BlockSpec(bias.shape, whole)],
        out_specs=(pl.BlockSpec((shares, columns, half + 4 * hidden), lambda i: (0, 0, 0)),
                   pl.BlockSpec((hidden + EXTRA, half), whole)),
        compiler_params=pltpu.CompilerParams(vmem_limit_bytes=VMEM),
        name="pack",
    )(parity, features, neigh_weight, self_weight, cotangent, bias)


def fill_table(first_group, groups, rank_ref, low_ref, store):
    def pairs(i, carry):
        for unrolled in range(UNROLL):
            pair = i * UNROLL + unrolled
            found = []
            for k in range(2):
                group = first_group + 2 * pair + k
                left = one_hot(rank_ref[pl.ds(group, 1), :], rank_ref.shape[1]).astype(ONES)
                right = one_hot(low_ref[pl.ds(group, 1), :], LOW).astype(ONES)
                table = lax.dot_general(left, right, NT, preferred_element_type=jnp.float32)
                found.append(table.reshape(table.shape[0] // GROUP, GROUP, LOW))
            rows = pl.ds(pl.multiple_of(pair * 2 * GROUP, 2 * GROUP), 2 * GROUP)
            store(rows, jnp.concatenate(found, axis=1).astype(jnp.bfloat16))
        return carry

    lax.fori_loop(0, groups // 2 // UNROLL, pairs, 0)


def table_kernel(neighbors_ref, features_ref, remote_ref, local_ref, rank_ref, low_ref, local_table_ref):
    slot_count, seed_count = neighbors_ref.shape
    group_count = seed_count // GROUP
    rows, half = local_table_ref.shape
    highs = half // LOW
    step = pl.program_id(0)

    @pl.when(step == 0)
    def _():
        ranks = []
        lows = []
        for member in range(GROUP):
            value = neighbors_ref[:, pl.ds(member * group_count, group_count)]
            value = jnp.concatenate(
                [value, jnp.full((PAD - slot_count, group_count), -1, jnp.int32)], axis=0)
            rank = jnp.where(value < 0, -1, (value >> 8) * GROUP + member)
            ranks.append(rank.astype(jnp.float32))
            lows.append((value & (LOW - 1)).astype(jnp.float32))
        rank_ref[...] = jnp.concatenate(ranks, axis=0).T
        low_ref[...] = jnp.concatenate(lows, axis=0).T

    def store(at, table):
        for high in range(highs):
            local_table_ref[at, pl.ds(high * LOW, LOW)] = table[high]
            remote_ref[at, pl.ds(high * LOW, LOW)] = table[highs + high]

    groups = rows // GROUP
    fill_table(step * groups, groups, rank_ref, low_ref, store)
    local_ref[...] = lax.dot_general(
        local_table_ref[...], features_ref[...], NT, preferred_element_type=jnp.float32)


def first_tables(neighbors, features, blocks, rows=256):
    slot_count, seed_count = neighbors.shape
    columns, nodes = features.shape
    group_count = seed_count // GROUP
    keys = jax.ShapeDtypeStruct((group_count, GROUP * PAD), jnp.float32)
    whole = lambda i: (0, 0)
    return pl.pallas_call(
        table_kernel,
        grid=(blocks,),
        out_shape=(jax.ShapeDtypeStruct((blocks * rows, nodes), jnp.bfloat16),
                   jax.ShapeDtypeStruct((blocks * rows, columns), jnp.float32), keys, keys),
        in_specs=[pl.BlockSpec((slot_count, seed_count), whole), pl.BlockSpec((columns, nodes), whole)],
        out_specs=(pl.BlockSpec((rows, nodes), lambda i: (i, 0)),
                   pl.BlockSpec((rows, columns), lambda i: (i, 0)),
                   pl.BlockSpec(keys.shape, whole), pl.BlockSpec(keys.shape, whole)),
        scratch_shapes=[pltpu.VMEM((rows, nodes), jnp.bfloat16)],
        compiler_params=pltpu.CompilerParams(vmem_limit_bytes=VMEM),
        name="first_tables",
    )(neighbors, features)


def mean_kernel(rows, place_ref, remote_ref, near_refs, far_refs, local_ref, rank_ref, low_ref, neighbors_ref,
                features_ref, out_ref, lookup_ref, sum_ref, table_ref, held_ref, sems):
    _, columns, capacity = near_refs[0].shape
    nodes = features_ref.shape[1]
    seed_count = sum_ref.shape[0]
    group_count = seed_count // GROUP
    blocks = held_ref.shape[0]
    copies = [
        pltpu.make_async_copy(remote_ref.at[pl.ds(k * rows, rows), :], held_ref.at[k], sems.at[k])
        for k in range(blocks)]
    for copy in copies:
        copy.start()
    lookup_ref[:, pl.ds(0, nodes)] = features_ref[...]
    for j in range(RADIX):
        for k in range(RADIX):
            source = relative(place_ref[0], RADIX - j, RADIX - k)
            at = pl.ds(pl.multiple_of(nodes + source * capacity, capacity), capacity)
            lookup_ref[:, at] = near_refs[k][0] if j == 0 else far_refs[j - 1][k]

    def store(at, table):
        for high in range(table.shape[0]):
            table_ref[at, pl.ds(high * LOW, LOW)] = table[high]

    def build(k, carry):
        fill_table(k * (rows // GROUP), rows // GROUP, rank_ref, low_ref, store)
        sum_ref[pl.ds(pl.multiple_of(k * rows, rows), rows), pl.ds(0, columns)] = lax.dot_general(
            table_ref[...], lookup_ref[...], NT, preferred_element_type=jnp.float32)
        return carry

    lax.fori_loop(blocks, seed_count // rows, build, 0)
    for k in range(blocks):
        copies[k].wait()
        at = pl.ds(k * rows, rows)
        sum_ref[at, pl.ds(0, columns)] = local_ref[at, :] + lax.dot_general(
            held_ref[k], lookup_ref[:, nodes:], NT, preferred_element_type=jnp.float32)

    degree = jnp.sum(jnp.where(neighbors_ref[...] >= 0, 1.0, 0.0), axis=0, keepdims=True)
    shares, _, half = out_ref.shape
    for member in range(GROUP):
        mine = sum_ref[pl.ds(member, group_count, stride=GROUP), :].T[:columns]
        start = member * group_count
        mine = mine / degree[:, start:start + group_count]
        mine = mine.astype(jnp.bfloat16)
        for share in range(start // half, shares, 2):
            out_ref[share, :, pl.ds(start % half, group_count)] = mine


def neighbor_mean(place, remote, near, far, local, rank, low, neighbors, features, shares, rows=256):
    slot_count, seed_count = neighbors.shape
    columns, nodes = features.shape
    capacity = near[0].shape[2]
    blocks = remote.shape[0] // rows
    lookup_width = nodes + RADIX * RADIX * capacity
    vm = pl.BlockSpec(memory_space=pltpu.VMEM)

    def kernel(place_ref, remote_ref, *refs):
        mean_kernel(rows, place_ref, remote_ref, refs[:RADIX], refs[RADIX:2 * RADIX - 1], *refs[2 * RADIX - 1:])

    return pl.pallas_call(
        kernel,
        out_shape=jax.ShapeDtypeStruct((shares, columns, seed_count // 2), jnp.bfloat16),
        in_specs=[pl.BlockSpec(memory_space=pltpu.SMEM), pl.BlockSpec(memory_space=pl.ANY)]
        + [vm] * (2 * RADIX - 1 + 5),
        out_specs=vm,
        scratch_shapes=[pltpu.VMEM((columns, lookup_width), jnp.bfloat16),
                        pltpu.VMEM((seed_count, 128), jnp.float32),
                        pltpu.VMEM((rows, lookup_width), jnp.bfloat16),
                        pltpu.VMEM((blocks, rows, nodes), jnp.bfloat16),
                        pltpu.SemaphoreType.DMA((blocks,))],
        compiler_params=pltpu.CompilerParams(vmem_limit_bytes=VMEM),
        name="mean",
    )(place, remote, *near, *far, local, rank, low, neighbors, features)


def layer_kernel(parity_ref, own_ref, mean_ref, neigh_weight_ref, self_weight_ref, bias_ref, cotangent_ref,
                 traded_ref, traded_bias_ref, kept_ref, sent_ref, grad_ref, total_ref, sums_ref):
    step = pl.program_id(0)
    odd = parity_ref[0] == 1
    hidden = cotangent_ref.shape[0]

    @pl.when(step == 0)
    def _():
        total_ref[...] = jnp.zeros_like(total_ref)
        sums_ref[...] = jnp.zeros_like(sums_ref)

    def ordered(mine, other):
        return jnp.concatenate([jnp.where(odd, other, mine), jnp.where(odd, mine, other)], axis=0)

    mine = bias_ref[...].astype(jnp.float32)
    theirs = traded_bias_ref[:1, :hidden].astype(jnp.float32)
    bias = jnp.concatenate([jnp.where(odd, theirs, mine), jnp.where(odd, mine, theirs)], axis=1)
    row = lax.broadcasted_iota(jnp.int32, (EXTRA, 2 * hidden), 0)
    bias = jnp.where(row == 0, bias, 0.0).astype(jnp.bfloat16)
    ones = jnp.ones((EXTRA, own_ref.shape[1]), jnp.bfloat16)
    cotangent = ordered(cotangent_ref[...].astype(jnp.float32), traded_ref[...].astype(jnp.float32))
    preact = (
        lax.dot_general(neigh_weight_ref[...], mean_ref[...], TN, preferred_element_type=jnp.float32)
        + lax.dot_general(self_weight_ref[...], own_ref[...], TN, preferred_element_type=jnp.float32)
        + lax.dot_general(bias, ones, TN, preferred_element_type=jnp.float32)
    )
    decay = jnp.exp(jnp.minimum(preact, 0.0))
    activation = jnp.where(preact > 0, preact, decay - 1.0)
    kept_ref[...] = jnp.where(odd, activation[hidden:], activation[:hidden]).astype(jnp.bfloat16)
    sent_ref[...] = jnp.where(odd, activation[:hidden], activation[hidden:]).astype(jnp.bfloat16)
    slope = jnp.where(preact > 0, 1.0, decay)
    grad_pre = (cotangent * slope).astype(jnp.bfloat16)
    first, second = grad_pre[:hidden], grad_pre[hidden:]
    blank = jnp.zeros_like(first)
    for_neigh = jnp.concatenate([first, blank, second, blank], axis=0)
    for_own = jnp.concatenate([blank, first, blank, second], axis=0)
    total_ref[...] += (
        lax.dot_general(mean_ref[...], for_neigh, NT, preferred_element_type=jnp.float32)
        + lax.dot_general(own_ref[...], for_own, NT, preferred_element_type=jnp.float32))
    sums_ref[...] += lax.dot_general(ones, for_neigh, NT, preferred_element_type=jnp.float32)

    @pl.when(step == pl.num_programs(0) - 1)
    def _():
        chunks, rows, width = grad_ref.shape
        columns = rows - EXTRA
        sums = sums_ref[...]
        high = sums.astype(jnp.bfloat16).astype(jnp.float32)
        row = lax.broadcasted_iota(jnp.int32, sums.shape, 0)
        extra = jnp.where(row == 0, high, jnp.where(row == 1, sums - high, 0.0)).astype(jnp.bfloat16)
        for chunk in range(chunks):
            at = pl.ds((chunk % 2) * width, width)
            grad_ref[chunk, pl.ds(0, columns), :] = total_ref[
                pl.ds((chunk // 2) * columns, columns), at].astype(jnp.bfloat16)
            grad_ref[chunk, pl.ds(columns, EXTRA), :] = extra[:, (chunk % 2) * width:(chunk % 2 + 1) * width]


def layer(parity, inputs, mean, bias, cotangent, traded, shares, block=512):
    features, half = mean.shape
    hidden = cotangent.shape[0]
    pair = 2 * hidden
    blocks = half // block
    whole = lambda i, parity: (0, 0)
    part = lambda i, parity: (0, i)
    grads = (2 * shares, features // shares + EXTRA, pair)
    return pl.pallas_call(
        layer_kernel,
        grid_spec=pltpu.PrefetchScalarGridSpec(
            num_scalar_prefetch=1,
            grid=(blocks,),
            in_specs=[pl.BlockSpec((features, block), part),
                      pl.BlockSpec((features, block), part),
                      pl.BlockSpec((features, pair), lambda i, parity: (0, half // pair)),
                      pl.BlockSpec((features, pair), lambda i, parity: (0, half // pair + 1)),
                      pl.BlockSpec((1, hidden), whole),
                      pl.BlockSpec((hidden, block), lambda i, parity: (0, i + parity[0] * blocks)),
                      pl.BlockSpec((hidden, block), part),
                      pl.BlockSpec((EXTRA, 128), lambda i, parity: (hidden // EXTRA, 0))],
            out_specs=(pl.BlockSpec((hidden, block), part),
                       pl.BlockSpec((hidden, block), part),
                       pl.BlockSpec(grads, lambda i, parity: (0, 0, 0))),
            scratch_shapes=[pltpu.VMEM((features, 2 * pair), jnp.float32),
                            pltpu.VMEM((EXTRA, 2 * pair), jnp.float32)]),
        out_shape=(jax.ShapeDtypeStruct((hidden, half), jnp.bfloat16),
                   jax.ShapeDtypeStruct((hidden, half), jnp.bfloat16),
                   jax.ShapeDtypeStruct(grads, jnp.bfloat16)),
        compiler_params=pltpu.CompilerParams(vmem_limit_bytes=VMEM // 2),
        name="layer",
    )(parity, inputs, mean, inputs, inputs, bias, cotangent, traded, traded)


def body(features, neigh_weight, self_weight, bias, neighbors, boundary, counts, cotangent):
    columns, nodes = features.shape
    partitions = lax.axis_size("vertex")
    shares = lax.axis_size("feat")
    seed_count = neighbors.shape[1]
    hidden = cotangent.shape[0]
    pair = 2 * hidden
    odd = lax.axis_index("feat") % 2
    parity = odd.astype(jnp.int32).reshape(1)
    bias = bias.reshape(1, hidden)
    trade = [(f, f ^ 1) for f in range(shares)]

    place = lax.axis_index("vertex").astype(jnp.int32).reshape(1)
    near = list(pick(place, features, boundary[0], counts))
    near[1:], late = lax.optimization_barrier((near[1:], parity))
    for k in range(1, RADIX):
        near[k] = lax.ppermute(
            near[k], "vertex", [(v, v // RADIX * RADIX + (v + k) % RADIX) for v in range(partitions)])
    inputs, traded = pack(late, features, neigh_weight, self_weight, cotangent, bias, shares)
    near[1:], inputs = lax.optimization_barrier((near[1:], inputs))
    inputs = lax.all_to_all(inputs, "feat", split_axis=0, concat_axis=0, tiled=True)
    far = list(regroup(near))
    far, early, traded = lax.optimization_barrier((far, neighbors, traded))
    for j in range(1, RADIX):
        far[j - 1] = lax.ppermute(
            far[j - 1], "vertex", [(v, (v + j * RADIX) % partitions) for v in range(partitions)])
    traded = lax.ppermute(traded, "feat", trade)
    remote, local, rank, low = first_tables(early, features, FIRST)
    mean = neighbor_mean(place, remote, near, far, local, rank, low, neighbors, features, shares)
    mean, inputs, traded, parity = lax.optimization_barrier((mean, inputs, traded, parity))
    inputs = inputs.reshape(shares * columns, inputs.shape[2])
    mean = lax.all_to_all(mean, "feat", split_axis=0, concat_axis=0, tiled=True)
    mean = mean.reshape(shares * columns, mean.shape[2])
    kept, sent, grad = layer(parity, inputs, mean, bias, cotangent, traded, shares)
    members = [[v * shares + 2 * q + k for v in range(partitions) for k in range(2)] for q in range(shares // 2)]
    grad = lax.all_to_all(
        grad, ("vertex", "feat"), split_axis=0, concat_axis=0, tiled=True, axis_index_groups=members)
    other = lax.ppermute(sent, "feat", trade)
    activation = jnp.concatenate(
        [jnp.where(odd == 1, other, kept), jnp.where(odd == 1, kept, other)], axis=1)

    factor = 1.0 / math.sqrt(seed_count * partitions)
    grad = jnp.sum(grad.astype(jnp.float32), axis=0) * factor
    bias_out = grad[columns, :hidden] + grad[columns + 1, :hidden]
    swap = [(v * shares + f, f * shares + v) for v in range(partitions) for f in range(shares)]
    grad = lax.ppermute(grad[:columns], ("vertex", "feat"), swap)
    return activation, grad[:, :hidden], grad[:, hidden:], bias_out


def solution(mesh):
    placed = (
        P("feat", "vertex"),
        P("feat", None),
        P("feat", None),
        P("feat"),
        P(None, "vertex"),
        P("vertex", None, None),
        P("vertex", None),
        P("feat", "vertex"),
    )
    return jax.shard_map(
        body,
        mesh=mesh,
        in_specs=placed,
        out_specs=(P("feat", "vertex"), P("feat", "vertex"), P("feat", "vertex"), P("feat")),
        check_vma=False,
    )
```

time: 139 us -> 125 us (0.90)
  blocking collectives: 0 us -> 27.1 us
  waiting for transfers between devices: 45.2 us -> 23.2 us
  starting transfers between devices: 45.6 us -> 33.7 us
  Pallas kernels: 39 us -> 36.1 us
  local copies, waits for them, and re-layouts: 4.05 us -> 2.04 us
    all_to_all x0 -> x1, blocking collectives: none -> 27.1 us  [body(): mean = lax.all_to_all(mean, 'feat', split_axis=0, concat_axis=0, tiled=True)]
    all_to_all x3 -> x1, starting transfers between devices: 24.3 us -> 4.8 us  [body(): lax.all_to_all(grad, ('vertex', 'feat'), split_axis=0, concat_axis=0, til...]
    ppermute x1, waiting for transfers between devices: 19.2 us -> 0.01 us  [body(): traded = lax.ppermute(traded, 'feat', trade)]
    all_to_all x1, waiting for transfers between devices: 7.74 us -> 0.01 us  [body(): lax.all_to_all(inputs, 'feat', split_axis=0, concat_axis=0, tiled=True)]
    ppermute x3 -> x7, starting transfers between devices: 11.8 us -> 18.4 us  [the longest x3 10.6 us: body(): lax.ppermute(far[j - 1], 'vertex', [(v, (v + j * RADIX) % partitions) for...]
    ppermute x3 -> x7, waiting for transfers between devices: 6.18 us -> 8.68 us  [the longest x1 7.22 us: body(): grad = lax.ppermute(grad[:columns], ('vertex', 'feat'), swap)]
    pallas_call x2 -> x3, Pallas kernels: 23 us -> 20.6 us  [the longest x1 15.4 us: neighbor_mean(): pl.pallas_call(kernel, out_shape=jax.ShapeDtypeStruct((shares, columns, s...]
    all_to_all x3 -> x1, waiting for transfers between devices: 6.93 us -> 8.43 us  [body(): lax.all_to_all(grad, ('vertex', 'feat'), split_axis=0, concat_axis=0, til...]
  transfers between devices with their start and end apart: 9 -> 11, of which waited for: 5 -> 5; matrix products, arithmetic and copies ran while one was open for 3% -> 1% of each run, Pallas kernels for 22% -> 23%
where the time goes in v2:
time: 125 us; the launch traced here: 124 us
  Pallas kernels  36.1 us (29%)
  starting transfers between devices  33.7 us (27%)
  blocking collectives  27.1 us (22%)
  waiting for transfers between devices  23.2 us (19%)
  local copies, waits for them, and re-layouts  2.04 us (2%)
  other arithmetic  1.35 us (1%)
    all_to_all x1, blocking collectives, body(): mean = lax.all_to_all(mean, 'feat', split_axis=0, concat_axis=0, tiled=True)  27.1 us
    pallas_call x1, Pallas kernels, neighbor_mean(): pl.pallas_call(kernel, out_shape=jax.ShapeDtypeStruct((shares, columns, s...  15.4 us
    ppermute x3, starting transfers between devices, body(): lax.ppermute(far[j - 1], 'vertex', [(v, (v + j * RADIX) % partitions) for...  10.6 us
    pallas_call x1, Pallas kernels, first_tables(): pl.pallas_call(table_kernel, grid=(blocks,), out_shape=(jax.ShapeDtypeStr...  9.33 us
    all_to_all x1, waiting for transfers between devices, body(): lax.all_to_all(grad, ('vertex', 'feat'), split_axis=0, concat_axis=0, til...  8.43 us
    all_to_all x1, starting transfers between devices, body(): lax.all_to_all(inputs, 'feat', split_axis=0, concat_axis=0, tiled=True)  7.45 us
    ppermute x1, waiting for transfers between devices, body(): grad = lax.ppermute(grad[:columns], ('vertex', 'feat'), swap)  7.22 us
    ppermute x1, starting transfers between devices, body(): grad = lax.ppermute(grad[:columns], ('vertex', 'feat'), swap)  6.1 us
  transfers between devices with their start and end apart: 11, of which 5 were waited for; matrix products, arithmetic and copies ran while one was open for 1% of the time, Pallas kernels for 23%

profile of v2, /device:TPU:36, one launch (start us, length us, event | category | flops | bytes accessed | tf_op | source)
XLA Modules:
  0.0 124.4 jit_solution(2523419712499350339)
XLA Ops:
  0.6 3.5 %pick.1 = (bf16[4,48,256]{2,1,0:T(8,128)(2,1)}, bf16[4,48,256]{2,1,0:T(8,128)(2,1)}, bf16[4,48,256]{2,1,0:T(8,128)(2,1)}, bf16[4,48,256]{2,1,0:T(8,128)(2,1)}) custom-call(s32[1]{0:T(128)} %bitcast.place_ref, bf16[48,4096]{1,0:T(8,128)(2,1)} %refs_11_.1, s32[16,256]{1,0:T(8,128)} %bitcast.14, s32[1,16]{1,0:T(1,128)} %counts_ref.1), custom_call_target="tpu_custom_call" | custom-call | tf_op jit(solution)/shard_map/pick/pallas_call | solution.py:64
  4.1 0.0 collective-permute-start
  4.1 0.1 collective-permute-start.1
  4.3 1.6 %collective-permute-start.2 = (bf16[4,48,256]{2,1,0:T(8,128)(2,1)}, bf16[4,48,256]{2,1,0:T(8,128)(2,1)S(1)}, u32[]{:S(2)}, u32[]{:S(2)}) collective-permute-start(bf16[4,48,256]{2,1,0:T(8,128)(2,1)} %get-tuple-element.43), channel_id=1, source_target_pairs={{0,48},{16,0},{32,16},{48,32},{64,112},{80,64},{96,80},{112,96},{1... | collective-permute-start | bytes 294920 | tf_op jit(solution)/shard_map/ppermute | solution.py:384
  5.9 2.6 %pack.1 = (bf16[16,48,1280]{2,1,0:T(8,128)(2,1)}, bf16[80,1024]{1,0:T(8,128)(2,1)}) custom-call(s32[1]{0:T(128)} %bitcast.2.parity_ref, bf16[48,4096]{1,0:T(8,128)(2,1)} %refs_11_.1, bf16[48,1024]{1,0:T(8,128)(2,1)} %neigh_weight_ref.1, bf16[48,1024]{1,0:T(8,128)(2,1)} %self_weight_ref.1, bf16[64,2048]{1,0:T(8,128)(2,1)} %cotangent_ref.3, bf16[1,64]{1,0:T(2,128)(2,1)} %bitcast.12), custom_call_target="tpu_custom_call" | custom-call | tf_op jit(solution)/shard_map/pack/pallas_call | solution.py:115
  8.5 0.3 collective-permute-done.refs_1_
  8.9 0.0 copy-start.2
  8.9 1.1 collective-permute-done.1.refs_2_
  10.0 0.0 copy-start.3
  10.0 0.0 collective-permute-done.2.refs_3_
  10.0 0.0 copy-done.2
  10.0 0.6 copy-done.3
  10.6 0.1 copy-done.4
  10.7 7.5 %all-to-all-start = ((bf16[16,48,1280]{2,1,0:T(8,128)(2,1)}), bf16[16,48,1280]{2,1,0:T(8,128)(2,1)S(1)}, u32[]{:S(2)}, u32[]{:S(2)}) async-start(bf16[16,48,1280]{2,1,0:T(8,128)(2,1)} %get-tuple-element.61), calls=%async_computation | async-start | bytes 3932160 | tf_op jit(solution)/shard_map/all_to_all | solution.py:388
  18.1 1.8 %regroup.1 = (bf16[4,48,256]{2,1,0:T(8,128)(2,1)}, bf16[4,48,256]{2,1,0:T(8,128)(2,1)}, bf16[4,48,256]{2,1,0:T(8,128)(2,1)}) custom-call(bf16[4,48,256]{2,1,0:T(8,128)(2,1)} %get-tuple-element.37.refs_0_, bf16[4,48,256]{2,1,0:T(8,128)(2,1)} %copy-done.2, bf16[4,48,256]{2,1,0:T(8,128)(2,1)} %copy-done.3, bf16[4,48,256]{2,1,0:T(8,128)(2,1)} %copy-done.4), custom_call_target="tpu_custom_call" | custom-call | tf_op jit(solution)/shard_map/regroup/pallas_call | solution.py:84
  19.9 0.0 copy-done.8
  19.9 1.5 %collective-permute-start.6 = (bf16[80,1024]{1,0:T(8,128)(2,1)S(1)}, bf16[80,1024]{1,0:T(8,128)(2,1)S(1)}, u32[]{:S(2)}, u32[]{:S(2)}) collective-permute-start(bf16[80,1024]{1,0:T(8,128)(2,1)S(1)} %copy-done.8), channel_id=1, source_target_pairs={{0,1},{1,0},{2,3},{3,2},{4,5},{5,4},{6,7},{7,6},{8,9},{9,8},{10,11... | collective-permute-start | bytes 491528 | tf_op jit(solution)/shard_map/ppermute | solution.py:394
  21.4 3.3 %collective-permute-start.3 = (bf16[4,48,256]{2,1,0:T(8,128)(2,1)}, bf16[4,48,256]{2,1,0:T(8,128)(2,1)S(1)}, u32[]{:S(2)}, u32[]{:S(2)}) collective-permute-start(bf16[4,48,256]{2,1,0:T(8,128)(2,1)} %get-tuple-element.55), channel_id=1, source_target_pairs={{0,64},{16,80},{32,96},{48,112},{64,128},{80,144},{96,160},{112,17... | collective-permute-start | bytes 294920 | tf_op jit(solution)/shard_map/ppermute | solution.py:392
  24.6 4.6 %collective-permute-start.4 = (bf16[4,48,256]{2,1,0:T(8,128)(2,1)}, bf16[4,48,256]{2,1,0:T(8,128)(2,1)S(1)}, u32[]{:S(2)}, u32[]{:S(2)}) collective-permute-start(bf16[4,48,256]{2,1,0:T(8,128)(2,1)} %get-tuple-element.56), channel_id=1, source_target_pairs={{0,128},{16,144},{32,160},{48,176},{64,192},{80,208},{96,224},{112... | collective-permute-start | bytes 294920 | tf_op jit(solution)/shard_map/ppermute | solution.py:392
  29.3 2.7 %collective-permute-start.5 = (bf16[4,48,256]{2,1,0:T(8,128)(2,1)}, bf16[4,48,256]{2,1,0:T(8,128)(2,1)S(1)}, u32[]{:S(2)}, u32[]{:S(2)}) collective-permute-start(bf16[4,48,256]{2,1,0:T(8,128)(2,1)} %get-tuple-element.57), channel_id=1, source_target_pairs={{0,192},{16,208},{32,224},{48,240},{64,0},{80,16},{96,32},{112,48}... | collective-permute-start | bytes 294920 | tf_op jit(solution)/shard_map/ppermute | solution.py:392
  31.9 9.3 %first_tables.1 = (bf16[1024,4096]{1,0:T(8,128)(2,1)}, f32[1024,48]{1,0:T(8,128)}, f32[256,256]{1,0:T(8,128)}, f32[256,256]{1,0:T(8,128)}) custom-call(s32[25,2048]{1,0:T(8,128)} %refs_10_.1, bf16[48,4096]{1,0:T(8,128)(2,1)} %refs_11_.1), custom_call_target="tpu_custom_call" | custom-call | tf_op jit(solution)/shard_map/first_tables/pallas_call | solution.py:189
  41.2 0.0 collective-permute-done.3.refs_4_
  41.3 0.0 collective-permute-done.4.refs_5_
  41.3 0.0 copy-start.6
  41.3 0.0 collective-permute-done.5.refs_6_
  41.3 0.0 copy-start.7
  41.3 0.6 copy-done.5
  41.9 0.0 copy-done.6
  41.9 0.0 copy-done.7
  42.0 15.4 %mean.1 = bf16[16,48,1024]{2,1,0:T(8,128)(2,1)} custom-call(s32[1]{0:T(128)} %bitcast.place_ref, bf16[1024,4096]{1,0:T(8,128)(2,1)} %get-tuple-element.54.remote_ref, bf16[4,48,256]{2,1,0:T(8,128)(2,1)} %get-tuple-element.37.refs_0_, bf16[4,48,256]{2,1,0:T(8,128)(2,1)} %copy-done.2, bf16[4,48,256]{2,1,0:T(8,128)(2,1)} %copy-done.3, ...), custom_call_target="tpu_custom_call" | custom-call | tf_op jit(solution)/shard_map/mean/pallas_call | solution.py:262
  57.3 0.0 copy-start
  57.3 0.0 copy-start.1
  57.4 0.0 collective-permute-done.6.traded_ref.traded_bias_ref
  57.4 0.0 all-to-all-done
  57.4 27.1 %all_to_all.15 = bf16[16,48,1024]{2,1,0:T(8,128)(2,1)S(1)} all-to-all(bf16[16,48,1024]{2,1,0:T(8,128)(2,1)} %mean.1), channel_id=1, replica_groups=mesh['vertex'=16,'feat'=16] {'feat'}, dimensions={0} | all-to-all | bytes 3145728 | tf_op jit(solution)/shard_map/all_to_all | solution.py:399
  84.5 0.0 copy-done
  84.5 0.0 copy-done.1
  84.5 3.6 %layer.1 = (bf16[64,1024]{1,0:T(8,128)(2,1)S(1)}, bf16[64,1024]{1,0:T(8,128)(2,1)S(1)}, bf16[32,64,128]{2,1,0:T(8,128)(2,1)}) custom-call(s32[1]{0:T(128)} %bitcast.2.parity_ref, bf16[768,1280]{1,0:T(8,128)(2,1)S(1)} %bitcast.8, bf16[768,1024]{1,0:T(8,128)(2,1)S(1)} %bitcast.11, bf16[768,1280]{1,0:T(8,128)(2,1)S(1)} %bitcast.9, ...), custom_call_target="tpu_custom_call" | custom-call | tf_op jit(solution)/shard_map/layer/pallas_call | solution.py:342
  88.1 4.8 %all-to-all-start.2 = ((bf16[32,64,128]{2,1,0:T(8,128)(2,1)}), bf16[32,64,128]{2,1,0:T(8,128)(2,1)S(1)}, u32[]{:S(2)}, u32[]{:S(2)}) async-start(bf16[32,64,128]{2,1,0:T(8,128)(2,1)} %get-tuple-element.69), calls=%async_computation.2 | async-start | bytes 1048576 | tf_op jit(solution)/shard_map/all_to_all | solution.py:403
  92.9 1.6 %collective-permute-start.7 = (bf16[64,1024]{1,0:T(8,128)(2,1)S(1)}, bf16[64,1024]{1,0:T(8,128)(2,1)S(1)}, u32[]{:S(2)}, u32[]{:S(2)}) collective-permute-start(bf16[64,1024]{1,0:T(8,128)(2,1)S(1)} %get-tuple-element.67), channel_id=1, source_target_pairs={{0,1},{1,0},{2,3},{3,2},{4,5},{5,4},{6,7},{7,6},{8,9},{9,8},{10,11... | collective-permute-start | bytes 393224 | tf_op jit(solution)/shard_map/ppermute | solution.py:405
  94.5 6.1 %collective-permute-done.7 = bf16[64,1024]{1,0:T(8,128)(2,1)S(1)} collective-permute-done((bf16[64,1024]{1,0:T(8,128)(2,1)S(1)}, bf16[64,1024]{1,0:T(8,128)(2,1)S(1)}, u32[]{:S(2)}, u32[]{:S(2)}) %collective-permute-start.7) | collective-permute-done | bytes 131104 | tf_op jit(solution)/shard_map/ppermute | solution.py:405
  100.6 0.7 pad_maximum_fusion
  101.3 8.4 %all-to-all-done.2 = bf16[32,64,128]{2,1,0:T(8,128)(2,1)S(1)} async-done(((bf16[32,64,128]{2,1,0:T(8,128)(2,1)}), bf16[32,64,128]{2,1,0:T(8,128)(2,1)S(1)}, u32[]{:S(2)}, u32[]{:S(2)}) %all-to-all-start.2) | async-done | bytes 524320 | tf_op jit(solution)/shard_map/all_to_all | solution.py:403
  109.7 0.1 convert_reduce_fusion
  109.8 6.1 %collective-permute-start.8 = (f32[48,128]{1,0:T(8,128)S(1)}, f32[48,128]{1,0:T(8,128)S(1)}, u32[]{:S(2)}, u32[]{:S(2)}) collective-permute-start(f32[48,128]{1,0:T(8,128)S(1)} %slice.20), channel_id=1, source_target_pairs={{0,0},{1,16},{2,32},{3,48},{4,64},{5,80},{6,96},{7,112},{8,128},{9... | collective-permute-start | bytes 73736 | tf_op jit(solution)/shard_map/ppermute | solution.py:413
  115.9 0.5 fusion
  116.5 7.2 %collective-permute-done.8 = f32[48,128]{1,0:T(8,128)S(1)} collective-permute-done((f32[48,128]{1,0:T(8,128)S(1)}, f32[48,128]{1,0:T(8,128)S(1)}, u32[]{:S(2)}, u32[]{:S(2)}) %collective-permute-start.8) | collective-permute-done | bytes 24608 | tf_op jit(solution)/shard_map/ppermute | solution.py:413
  123.7 0.7 fusion.1
  (6 shorter events, 0.0 us)
Async XLA Ops:
  4.1 4.8 %collective-permute-start = (bf16[4,48,256]{2,1,0:T(8,128)(2,1)}, bf16[4,48,256]{2,1,0:T(8,128)(2,1)S(1)}, u32[]{:S(2)}, u32[]{:S(2)}) collective-permute-start(bf16[4,48,256]{2,1,0:T(8,128)(2,1)} %get-tuple-element.41), channel_id=1, source_target_pairs={{0,16},{16,32},{32,48},{48,0},{64,80},{80,96},{96,112},{112,64},{1... | collective-permute-start | bytes 294920 | tf_op jit(solution)/shard_map/ppermute | solution.py:384
  4.1 5.9 %collective-permute-start.1 = (bf16[4,48,256]{2,1,0:T(8,128)(2,1)}, bf16[4,48,256]{2,1,0:T(8,128)(2,1)S(1)}, u32[]{:S(2)}, u32[]{:S(2)}) collective-permute-start(bf16[4,48,256]{2,1,0:T(8,128)(2,1)} %get-tuple-element.42), channel_id=1, source_target_pairs={{0,32},{16,48},{32,0},{48,16},{64,96},{80,112},{96,64},{112,80},{1... | collective-permute-start | bytes 294920 | tf_op jit(solution)/shard_map/ppermute | solution.py:384
  4.3 5.7 %collective-permute-start.2 = (bf16[4,48,256]{2,1,0:T(8,128)(2,1)}, bf16[4,48,256]{2,1,0:T(8,128)(2,1)S(1)}, u32[]{:S(2)}, u32[]{:S(2)}) collective-permute-start(bf16[4,48,256]{2,1,0:T(8,128)(2,1)} %get-tuple-element.43), channel_id=1, source_target_pairs={{0,48},{16,0},{32,16},{48,32},{64,112},{80,64},{96,80},{112,96},{1... | collective-permute-start | bytes 294920 | tf_op jit(solution)/shard_map/ppermute | solution.py:384
  8.9 1.1 copy-start.2
  10.0 0.6 copy-start.3
  10.0 0.7 copy-start.4
  10.0 9.9 %copy-start.8 = (bf16[80,1024]{1,0:T(8,128)(2,1)S(1)}, bf16[80,1024]{1,0:T(8,128)(2,1)}, u32[]{:S(2)}) copy-start(bf16[80,1024]{1,0:T(8,128)(2,1)} %get-tuple-element.62) | copy-start | bytes 491524
  10.7 46.7 %all-to-all-start = ((bf16[16,48,1280]{2,1,0:T(8,128)(2,1)}), bf16[16,48,1280]{2,1,0:T(8,128)(2,1)S(1)}, u32[]{:S(2)}, u32[]{:S(2)}) async-start(bf16[16,48,1280]{2,1,0:T(8,128)(2,1)} %get-tuple-element.61), calls=%async_computation | async-start | bytes 3932160 | tf_op jit(solution)/shard_map/all_to_all | solution.py:388
  19.9 37.5 %collective-permute-start.6 = (bf16[80,1024]{1,0:T(8,128)(2,1)S(1)}, bf16[80,1024]{1,0:T(8,128)(2,1)S(1)}, u32[]{:S(2)}, u32[]{:S(2)}) collective-permute-start(bf16[80,1024]{1,0:T(8,128)(2,1)S(1)} %copy-done.8), channel_id=1, source_target_pairs={{0,1},{1,0},{2,3},{3,2},{4,5},{5,4},{6,7},{7,6},{8,9},{9,8},{10,11... | collective-permute-start | bytes 491528 | tf_op jit(solution)/shard_map/ppermute | solution.py:394
  21.4 19.9 %collective-permute-start.3 = (bf16[4,48,256]{2,1,0:T(8,128)(2,1)}, bf16[4,48,256]{2,1,0:T(8,128)(2,1)S(1)}, u32[]{:S(2)}, u32[]{:S(2)}) collective-permute-start(bf16[4,48,256]{2,1,0:T(8,128)(2,1)} %get-tuple-element.55), channel_id=1, source_target_pairs={{0,64},{16,80},{32,96},{48,112},{64,128},{80,144},{96,160},{112,17... | collective-permute-start | bytes 294920 | tf_op jit(solution)/shard_map/ppermute | solution.py:392
  24.6 16.6 %collective-permute-start.4 = (bf16[4,48,256]{2,1,0:T(8,128)(2,1)}, bf16[4,48,256]{2,1,0:T(8,128)(2,1)S(1)}, u32[]{:S(2)}, u32[]{:S(2)}) collective-permute-start(bf16[4,48,256]{2,1,0:T(8,128)(2,1)} %get-tuple-element.56), channel_id=1, source_target_pairs={{0,128},{16,144},{32,160},{48,176},{64,192},{80,208},{96,224},{112... | collective-permute-start | bytes 294920 | tf_op jit(solution)/shard_map/ppermute | solution.py:392
  29.3 12.0 %collective-permute-start.5 = (bf16[4,48,256]{2,1,0:T(8,128)(2,1)}, bf16[4,48,256]{2,1,0:T(8,128)(2,1)S(1)}, u32[]{:S(2)}, u32[]{:S(2)}) collective-permute-start(bf16[4,48,256]{2,1,0:T(8,128)(2,1)} %get-tuple-element.57), channel_id=1, source_target_pairs={{0,192},{16,208},{32,224},{48,240},{64,0},{80,16},{96,32},{112,48}... | collective-permute-start | bytes 294920 | tf_op jit(solution)/shard_map/ppermute | solution.py:392
  41.3 0.6 copy-start.5
  41.3 0.7 copy-start.6
  41.3 0.7 copy-start.7
  57.3 27.2 %copy-start = (bf16[64,2048]{1,0:T(8,128)(2,1)S(1)}, bf16[64,2048]{1,0:T(8,128)(2,1)}, u32[]{:S(2)}) copy-start(bf16[64,2048]{1,0:T(8,128)(2,1)} %cotangent_ref.3) | copy-start | bytes 786436
  57.3 27.2 %copy-start.1 = (bf16[64]{0:T(256)(128)(2,1)S(1)}, bf16[64]{0:T(256)(128)(2,1)}, u32[]{:S(2)}) copy-start(bf16[64]{0:T(256)(128)(2,1)} %param.11) | copy-start | bytes 388
  88.1 21.6 %all-to-all-start.2 = ((bf16[32,64,128]{2,1,0:T(8,128)(2,1)}), bf16[32,64,128]{2,1,0:T(8,128)(2,1)S(1)}, u32[]{:S(2)}, u32[]{:S(2)}) async-start(bf16[32,64,128]{2,1,0:T(8,128)(2,1)} %get-tuple-element.69), calls=%async_computation.2 | async-start | bytes 1048576 | tf_op jit(solution)/shard_map/all_to_all | solution.py:403
  92.9 7.6 %collective-permute-start.7 = (bf16[64,1024]{1,0:T(8,128)(2,1)S(1)}, bf16[64,1024]{1,0:T(8,128)(2,1)S(1)}, u32[]{:S(2)}, u32[]{:S(2)}) collective-permute-start(bf16[64,1024]{1,0:T(8,128)(2,1)S(1)} %get-tuple-element.67), channel_id=1, source_target_pairs={{0,1},{1,0},{2,3},{3,2},{4,5},{5,4},{6,7},{7,6},{8,9},{9,8},{10,11... | collective-permute-start | bytes 393224 | tf_op jit(solution)/shard_map/ppermute | solution.py:405
  109.8 13.8 %collective-permute-start.8 = (f32[48,128]{1,0:T(8,128)S(1)}, f32[48,128]{1,0:T(8,128)S(1)}, u32[]{:S(2)}, u32[]{:S(2)}) collective-permute-start(f32[48,128]{1,0:T(8,128)S(1)} %slice.20), channel_id=1, source_target_pairs={{0,0},{1,16},{2,32},{3,48},{4,64},{5,80},{6,96},{7,112},{8,128},{9... | collective-permute-start | bytes 73736 | tf_op jit(solution)/shard_map/ppermute | solution.py:413

commit v3 on v2

--- a/solution.py
+++ b/solution.py
@@ -15,6 +15,7 @@
 RADIX = 4
 PAD = 32
 GROUP = 8
+SUMS = 8
 EXTRA = 16
 VMEM = 60 * 1024 * 1024
 NT = (((1,), (1,)), ((), ()))
@@ -157,17 +158,16 @@
 
     @pl.when(step == 0)
     def _():
-        ranks = []
-        lows = []
+        values = []
         for member in range(GROUP):
-            value = neighbors_ref[:, pl.ds(member * group_count, group_count)]
-            value = jnp.concatenate(
-                [value, jnp.full((PAD - slot_count, group_count), -1, jnp.int32)], axis=0)
-            rank = jnp.where(value < 0, -1, (value >> 8) * GROUP + member)
-            ranks.append(rank.astype(jnp.float32))
-            lows.append((value & (LOW - 1)).astype(jnp.float32))
-        rank_ref[...] = jnp.concatenate(ranks, axis=0).T
-        low_ref[...] = jnp.concatenate(lows, axis=0).T
+            value = neighbors_ref[:, pl.ds(member * group_count, group_count)].astype(jnp.float32)
+            values.append(jnp.concatenate(
+                [value, jnp.full((PAD - slot_count, group_count), -1.0, jnp.float32)], axis=0))
+        value = jnp.concatenate(values, axis=0).T
+        member = lax.broadcasted_iota(jnp.int32, value.shape, 1) // PAD
+        high = jnp.floor(value * (1.0 / LOW))
+        rank_ref[...] = jnp.where(value < 0, -1.0, high * GROUP + member.astype(jnp.float32))
+        low_ref[...] = value - high * LOW
 
     def store(at, table):
         for high in range(highs):
@@ -314,21 +314,20 @@
     total_ref[...] += (
         lax.dot_general(mean_ref[...], for_neigh, NT, preferred_element_type=jnp.float32)
         + lax.dot_general(own_ref[...], for_own, NT, preferred_element_type=jnp.float32))
-    sums_ref[...] += lax.dot_general(ones, for_neigh, NT, preferred_element_type=jnp.float32)
+    sums_ref[...] += lax.dot_general(ones[:SUMS], for_neigh, NT, preferred_element_type=jnp.float32)
 
     @pl.when(step == pl.num_programs(0) - 1)
     def _():
         chunks, rows, width = grad_ref.shape
-        columns = rows - EXTRA
+        columns = rows - SUMS
         sums = sums_ref[...]
         high = sums.astype(jnp.bfloat16).astype(jnp.float32)
         row = lax.broadcasted_iota(jnp.int32, sums.shape, 0)
-        extra = jnp.where(row == 0, high, jnp.where(row == 1, sums - high, 0.0)).astype(jnp.bfloat16)
+        extra = jnp.where(row == 0, high, jnp.where(row == 1, sums - high, 0.0))
         for chunk in range(chunks):
-            at = pl.ds((chunk % 2) * width, width)
-            grad_ref[chunk, pl.ds(0, columns), :] = total_ref[
-                pl.ds((chunk // 2) * columns, columns), at].astype(jnp.bfloat16)
-            grad_ref[chunk, pl.ds(columns, EXTRA), :] = extra[:, (chunk % 2) * width:(chunk % 2 + 1) * width]
+            at = slice((chunk % 2) * width, (chunk % 2 + 1) * width)
+            mine = total_ref[pl.ds((chunk // 2) * columns, columns), at]
+            grad_ref[chunk] = jnp.concatenate([mine, extra[:, at]], axis=0).astype(jnp.bfloat16)
 
 
 def layer(parity, inputs, mean, bias, cotangent, traded, shares, block=512):
@@ -338,7 +337,7 @@
     blocks = half // block
     whole = lambda i, parity: (0, 0)
     part = lambda i, parity: (0, i)
-    grads = (2 * shares, features // shares + EXTRA, pair)
+    grads = (2 * shares, features // shares + SUMS, pair)
     return pl.pallas_call(
         layer_kernel,
         grid_spec=pltpu.PrefetchScalarGridSpec(
@@ -356,7 +355,7 @@
                        pl.BlockSpec((hidden, block), part),
                        pl.BlockSpec(grads, lambda i, parity: (0, 0, 0))),
             scratch_shapes=[pltpu.VMEM((features, 2 * pair), jnp.float32),
-                            pltpu.VMEM((EXTRA, 2 * pair), jnp.float32)]),
+                            pltpu.VMEM((SUMS, 2 * pair), jnp.float32)]),
         out_shape=(jax.ShapeDtypeStruct((hidden, half), jnp.bfloat16),
                    jax.ShapeDtypeStruct((hidden, half), jnp.bfloat16),
                    jax.ShapeDtypeStruct(grads, jnp.bfloat16)),
@@ -385,9 +384,9 @@
             near[k], "vertex", [(v, v // RADIX * RADIX + (v + k) % RADIX) for v in range(partitions)])
     inputs, traded = pack(late, features, neigh_weight, self_weight, cotangent, bias, shares)
     near[1:], inputs = lax.optimization_barrier((near[1:], inputs))
+    far = list(regroup(near))
+    far, early, traded, inputs = lax.optimization_barrier((far, neighbors, traded, inputs))
     inputs = lax.all_to_all(inputs, "feat", split_axis=0, concat_axis=0, tiled=True)
-    far = list(regroup(near))
-    far, early, traded = lax.optimization_barrier((far, neighbors, traded))
     for j in range(1, RADIX):
         far[j - 1] = lax.ppermute(
             far[j - 1], "vertex", [(v, (v + j * RADIX) % partitions) for v in range(partitions)])

time: 125 us -> 123 us (0.984)
  waiting for transfers between devices: 23.2 us -> 21.8 us
  transfers between devices with their start and end apart: 11 -> 11, of which waited for: 5 -> 5; matrix products, arithmetic and copies ran while one was open for 1% -> 1% of each run, Pallas kernels for 23% -> 22%
where the time goes in v3:
time: 123 us
  Pallas kernels  36 us (29%)
  starting transfers between devices  33.8 us (27%)
  blocking collectives  27.1 us (22%)
  waiting for transfers between devices  21.8 us (18%)
  local copies, waits for them, and re-layouts  2.05 us (2%)
  other arithmetic  1.34 us (1%)
    all_to_all x1, blocking collectives, body(): mean = lax.all_to_all(mean, 'feat', split_axis=0, concat_axis=0, tiled=True)  27.1 us
    pallas_call x1, Pallas kernels, neighbor_mean(): pl.pallas_call(kernel, out_shape=jax.ShapeDtypeStruct((shares, columns, s...  15.4 us
    ppermute x3, starting transfers between devices, body(): lax.ppermute(far[j - 1], 'vertex', [(v, (v + j * RADIX) % partitions) for...  10.6 us
    pallas_call x1, Pallas kernels, first_tables(): pl.pallas_call(table_kernel, grid=(blocks,), out_shape=(jax.ShapeDtypeStr...  9.25 us
    all_to_all x1, starting transfers between devices, body(): lax.all_to_all(inputs, 'feat', split_axis=0, concat_axis=0, tiled=True)  7.6 us
    all_to_all x1, waiting for transfers between devices, body(): lax.all_to_all(grad, ('vertex', 'feat'), split_axis=0, concat_axis=0, til...  7.36 us
    ppermute x1, waiting for transfers between devices, body(): grad = lax.ppermute(grad[:columns], ('vertex', 'feat'), swap)  7.22 us
    ppermute x1, starting transfers between devices, body(): grad = lax.ppermute(grad[:columns], ('vertex', 'feat'), swap)  6.1 us
  transfers between devices with their start and end apart: 11, of which 5 were waited for; matrix products, arithmetic and copies ran while one was open for 1% of the time, Pallas kernels for 22%

profile of v3, /device:TPU:36, one launch (start us, length us, event | category | flops | bytes accessed | tf_op | source)
XLA Modules:
  0.0 123.0 jit_solution(16516123277951192138)
XLA Ops:
  0.6 3.5 %pick.1 = (bf16[4,48,256]{2,1,0:T(8,128)(2,1)}, bf16[4,48,256]{2,1,0:T(8,128)(2,1)}, bf16[4,48,256]{2,1,0:T(8,128)(2,1)}, bf16[4,48,256]{2,1,0:T(8,128)(2,1)}) custom-call(s32[1]{0:T(128)} %bitcast.place_ref, bf16[48,4096]{1,0:T(8,128)(2,1)} %refs_11_.1, s32[16,256]{1,0:T(8,128)} %bitcast.14, s32[1,16]{1,0:T(1,128)} %counts_ref.1), custom_call_target="tpu_custom_call" | custom-call | tf_op jit(solution)/shard_map/pick/pallas_call | solution.py:65
  4.1 0.0 collective-permute-start
  4.1 0.1 collective-permute-start.1
  4.3 1.6 %collective-permute-start.2 = (bf16[4,48,256]{2,1,0:T(8,128)(2,1)}, bf16[4,48,256]{2,1,0:T(8,128)(2,1)S(1)}, u32[]{:S(2)}, u32[]{:S(2)}) collective-permute-start(bf16[4,48,256]{2,1,0:T(8,128)(2,1)} %get-tuple-element.44), channel_id=1, source_target_pairs={{0,48},{16,0},{32,16},{48,32},{64,112},{80,64},{96,80},{112,96},{1... | collective-permute-start | bytes 294920 | tf_op jit(solution)/shard_map/ppermute | solution.py:383
  5.9 2.6 %pack.1 = (bf16[16,48,1280]{2,1,0:T(8,128)(2,1)}, bf16[80,1024]{1,0:T(8,128)(2,1)}) custom-call(s32[1]{0:T(128)} %bitcast.2.parity_ref, bf16[48,4096]{1,0:T(8,128)(2,1)} %refs_11_.1, bf16[48,1024]{1,0:T(8,128)(2,1)} %neigh_weight_ref.1, bf16[48,1024]{1,0:T(8,128)(2,1)} %self_weight_ref.1, bf16[64,2048]{1,0:T(8,128)(2,1)} %cotangent_ref.3, bf16[1,64]{1,0:T(2,128)(2,1)} %bitcast.12), custom_call_target="tpu_custom_call" | custom-call | tf_op jit(solution)/shard_map/pack/pallas_call | solution.py:116
  8.5 0.4 collective-permute-done.refs_1_
  8.9 1.1 collective-permute-done.1.refs_2_
  10.0 0.0 collective-permute-done.2.refs_3_
  10.0 0.0 copy-done.2
  10.0 0.6 copy-done.3
  10.6 0.0 copy-done.4
  10.7 1.8 %regroup.1 = (bf16[4,48,256]{2,1,0:T(8,128)(2,1)}, bf16[4,48,256]{2,1,0:T(8,128)(2,1)}, bf16[4,48,256]{2,1,0:T(8,128)(2,1)}) custom-call(bf16[4,48,256]{2,1,0:T(8,128)(2,1)} %get-tuple-element.38.refs_0_, bf16[4,48,256]{2,1,0:T(8,128)(2,1)} %copy-done.2, bf16[4,48,256]{2,1,0:T(8,128)(2,1)} %copy-done.3, bf16[4,48,256]{2,1,0:T(8,128)(2,1)} %copy-done.4), custom_call_target="tpu_custom_call" | custom-call | tf_op jit(solution)/shard_map/regroup/pallas_call | solution.py:85
  12.4 0.0 copy-start.9
  12.4 7.6 %all-to-all-start = ((bf16[16,48,1280]{2,1,0:T(8,128)(2,1)}), bf16[16,48,1280]{2,1,0:T(8,128)(2,1)S(1)}, u32[]{:S(2)}, u32[]{:S(2)}) async-start(bf16[16,48,1280]{2,1,0:T(8,128)(2,1)} %get-tuple-element.63), calls=%async_computation | async-start | bytes 3932160 | tf_op jit(solution)/shard_map/all_to_all | solution.py:389
  20.0 0.0 copy-done.8
  20.0 1.6 %collective-permute-start.6 = (bf16[80,1024]{1,0:T(8,128)(2,1)S(1)}, bf16[80,1024]{1,0:T(8,128)(2,1)S(1)}, u32[]{:S(2)}, u32[]{:S(2)}) collective-permute-start(bf16[80,1024]{1,0:T(8,128)(2,1)S(1)} %copy-done.8), channel_id=1, source_target_pairs={{0,1},{1,0},{2,3},{3,2},{4,5},{5,4},{6,7},{7,6},{8,9},{9,8},{10,11... | collective-permute-start | bytes 491528 | tf_op jit(solution)/shard_map/ppermute | solution.py:393
  21.6 0.0 copy-done.11
  21.6 3.3 %collective-permute-start.3 = (bf16[4,48,256]{2,1,0:T(8,128)(2,1)S(1)}, bf16[4,48,256]{2,1,0:T(8,128)(2,1)S(1)}, u32[]{:S(2)}, u32[]{:S(2)}) collective-permute-start(bf16[4,48,256]{2,1,0:T(8,128)(2,1)S(1)} %copy-done.11), channel_id=1, source_target_pairs={{0,64},{16,80},{32,96},{48,112},{64,128},{80,144},{96,160},{112,17... | collective-permute-start | bytes 294920 | tf_op jit(solution)/shard_map/ppermute | solution.py:391
  24.8 0.0 copy-done.10
  24.9 4.6 %collective-permute-start.4 = (bf16[4,48,256]{2,1,0:T(8,128)(2,1)S(1)}, bf16[4,48,256]{2,1,0:T(8,128)(2,1)S(1)}, u32[]{:S(2)}, u32[]{:S(2)}) collective-permute-start(bf16[4,48,256]{2,1,0:T(8,128)(2,1)S(1)} %copy-done.10), channel_id=1, source_target_pairs={{0,128},{16,144},{32,160},{48,176},{64,192},{80,208},{96,224},{112... | collective-permute-start | bytes 294920 | tf_op jit(solution)/shard_map/ppermute | solution.py:391
  29.5 0.0 copy-done.9
  29.5 2.7 %collective-permute-start.5 = (bf16[4,48,256]{2,1,0:T(8,128)(2,1)S(1)}, bf16[4,48,256]{2,1,0:T(8,128)(2,1)S(1)}, u32[]{:S(2)}, u32[]{:S(2)}) collective-permute-start(bf16[4,48,256]{2,1,0:T(8,128)(2,1)S(1)} %copy-done.9), channel_id=1, source_target_pairs={{0,192},{16,208},{32,224},{48,240},{64,0},{80,16},{96,32},{112,48}... | collective-permute-start | bytes 294920 | tf_op jit(solution)/shard_map/ppermute | solution.py:391
  32.2 9.3 %first_tables.1 = (bf16[1024,4096]{1,0:T(8,128)(2,1)}, f32[1024,48]{1,0:T(8,128)}, f32[256,256]{1,0:T(8,128)}, f32[256,256]{1,0:T(8,128)}) custom-call(s32[25,2048]{1,0:T(8,128)} %refs_10_.1, bf16[48,4096]{1,0:T(8,128)(2,1)} %refs_11_.1), custom_call_target="tpu_custom_call" | custom-call | tf_op jit(solution)/shard_map/first_tables/pallas_call | solution.py:189
  41.4 0.0 collective-permute-done.3.refs_4_
  41.4 0.0 collective-permute-done.4.refs_5_
  41.4 0.0 copy-start.6
  41.4 0.0 collective-permute-done.5.refs_6_
  41.5 0.6 copy-done.5
  42.0 0.0 copy-done.6
  42.1 0.0 copy-done.7
  42.1 15.4 %mean.1 = bf16[16,48,1024]{2,1,0:T(8,128)(2,1)} custom-call(s32[1]{0:T(128)} %bitcast.place_ref, bf16[1024,4096]{1,0:T(8,128)(2,1)} %get-tuple-element.56.remote_ref, bf16[4,48,256]{2,1,0:T(8,128)(2,1)} %get-tuple-element.38.refs_0_, bf16[4,48,256]{2,1,0:T(8,128)(2,1)} %copy-done.2, bf16[4,48,256]{2,1,0:T(8,128)(2,1)} %copy-done.3, ...), custom_call_target="tpu_custom_call" | custom-call | tf_op jit(solution)/shard_map/mean/pallas_call | solution.py:262
  57.5 0.0 copy-start
  57.5 0.0 copy-start.1
  57.5 0.0 collective-permute-done.6.traded_ref.traded_bias_ref
  57.6 0.0 all-to-all-done
  57.6 27.1 %all_to_all.15 = bf16[16,48,1024]{2,1,0:T(8,128)(2,1)S(1)} all-to-all(bf16[16,48,1024]{2,1,0:T(8,128)(2,1)} %mean.1), channel_id=1, replica_groups=mesh['vertex'=16,'feat'=16] {'feat'}, dimensions={0} | all-to-all | bytes 3145728 | tf_op jit(solution)/shard_map/all_to_all | solution.py:398
  84.7 0.0 copy-done.1
  84.7 3.5 %layer.1 = (bf16[64,1024]{1,0:T(8,128)(2,1)S(1)}, bf16[64,1024]{1,0:T(8,128)(2,1)S(1)}, bf16[32,56,128]{2,1,0:T(8,128)(2,1)}) custom-call(s32[1]{0:T(128)} %bitcast.2.parity_ref, bf16[768,1280]{1,0:T(8,128)(2,1)S(1)} %bitcast.8, bf16[768,1024]{1,0:T(8,128)(2,1)S(1)} %bitcast.11, bf16[768,1280]{1,0:T(8,128)(2,1)S(1)} %bitcast.9, ...), custom_call_target="tpu_custom_call" | custom-call | tf_op jit(solution)/shard_map/layer/pallas_call | solution.py:341
  88.2 4.7 %all-to-all-start.2 = ((bf16[32,56,128]{2,1,0:T(8,128)(2,1)}), bf16[32,56,128]{2,1,0:T(8,128)(2,1)S(1)}, u32[]{:S(2)}, u32[]{:S(2)}) async-start(bf16[32,56,128]{2,1,0:T(8,128)(2,1)} %get-tuple-element.71), calls=%async_computation.2 | async-start | bytes 917504 | tf_op jit(solution)/shard_map/all_to_all | solution.py:402
  92.9 1.6 %collective-permute-start.7 = (bf16[64,1024]{1,0:T(8,128)(2,1)S(1)}, bf16[64,1024]{1,0:T(8,128)(2,1)S(1)}, u32[]{:S(2)}, u32[]{:S(2)}) collective-permute-start(bf16[64,1024]{1,0:T(8,128)(2,1)S(1)} %get-tuple-element.69), channel_id=1, source_target_pairs={{0,1},{1,0},{2,3},{3,2},{4,5},{5,4},{6,7},{7,6},{8,9},{9,8},{10,11... | collective-permute-start | bytes 393224 | tf_op jit(solution)/shard_map/ppermute | solution.py:404
  94.5 5.8 %collective-permute-done.7 = bf16[64,1024]{1,0:T(8,128)(2,1)S(1)} collective-permute-done((bf16[64,1024]{1,0:T(8,128)(2,1)S(1)}, bf16[64,1024]{1,0:T(8,128)(2,1)S(1)}, u32[]{:S(2)}, u32[]{:S(2)}) %collective-permute-start.7) | collective-permute-done | bytes 131104 | tf_op jit(solution)/shard_map/ppermute | solution.py:404
  100.3 0.7 pad_maximum_fusion
  101.0 7.4 %all-to-all-done.2 = bf16[32,56,128]{2,1,0:T(8,128)(2,1)S(1)} async-done(((bf16[32,56,128]{2,1,0:T(8,128)(2,1)}), bf16[32,56,128]{2,1,0:T(8,128)(2,1)S(1)}, u32[]{:S(2)}, u32[]{:S(2)}) %all-to-all-start.2) | async-done | bytes 458784 | tf_op jit(solution)/shard_map/all_to_all | solution.py:402
  108.3 0.1 convert_reduce_fusion
  108.4 6.1 %collective-permute-start.8 = (f32[48,128]{1,0:T(8,128)S(1)}, f32[48,128]{1,0:T(8,128)S(1)}, u32[]{:S(2)}, u32[]{:S(2)}) collective-permute-start(f32[48,128]{1,0:T(8,128)S(1)} %slice.20), channel_id=1, source_target_pairs={{0,0},{1,16},{2,32},{3,48},{4,64},{5,80},{6,96},{7,112},{8,128},{9... | collective-permute-start | bytes 73736 | tf_op jit(solution)/shard_map/ppermute | solution.py:412
  114.5 0.5 fusion
  115.1 7.2 %collective-permute-done.8 = f32[48,128]{1,0:T(8,128)S(1)} collective-permute-done((f32[48,128]{1,0:T(8,128)S(1)}, f32[48,128]{1,0:T(8,128)S(1)}, u32[]{:S(2)}, u32[]{:S(2)}) %collective-permute-start.8) | collective-permute-done | bytes 24608 | tf_op jit(solution)/shard_map/ppermute | solution.py:412
  122.3 0.7 fusion.1
  (12 shorter events, 0.0 us)
Async XLA Ops:
  4.1 4.8 %collective-permute-start = (bf16[4,48,256]{2,1,0:T(8,128)(2,1)}, bf16[4,48,256]{2,1,0:T(8,128)(2,1)S(1)}, u32[]{:S(2)}, u32[]{:S(2)}) collective-permute-start(bf16[4,48,256]{2,1,0:T(8,128)(2,1)} %get-tuple-element.42), channel_id=1, source_target_pairs={{0,16},{16,32},{32,48},{48,0},{64,80},{80,96},{96,112},{112,64},{1... | collective-permute-start | bytes 294920 | tf_op jit(solution)/shard_map/ppermute | solution.py:383
  4.1 5.9 %collective-permute-start.1 = (bf16[4,48,256]{2,1,0:T(8,128)(2,1)}, bf16[4,48,256]{2,1,0:T(8,128)(2,1)S(1)}, u32[]{:S(2)}, u32[]{:S(2)}) collective-permute-start(bf16[4,48,256]{2,1,0:T(8,128)(2,1)} %get-tuple-element.43), channel_id=1, source_target_pairs={{0,32},{16,48},{32,0},{48,16},{64,96},{80,112},{96,64},{112,80},{1... | collective-permute-start | bytes 294920 | tf_op jit(solution)/shard_map/ppermute | solution.py:383
  4.3 5.7 %collective-permute-start.2 = (bf16[4,48,256]{2,1,0:T(8,128)(2,1)}, bf16[4,48,256]{2,1,0:T(8,128)(2,1)S(1)}, u32[]{:S(2)}, u32[]{:S(2)}) collective-permute-start(bf16[4,48,256]{2,1,0:T(8,128)(2,1)} %get-tuple-element.44), channel_id=1, source_target_pairs={{0,48},{16,0},{32,16},{48,32},{64,112},{80,64},{96,80},{112,96},{1... | collective-permute-start | bytes 294920 | tf_op jit(solution)/shard_map/ppermute | solution.py:383
  8.9 1.1 copy-start.2
  10.0 0.6 copy-start.3
  10.0 0.7 copy-start.4
  12.4 7.6 %copy-start.8 = (bf16[80,1024]{1,0:T(8,128)(2,1)S(1)}, bf16[80,1024]{1,0:T(8,128)(2,1)}, u32[]{:S(2)}) copy-start(bf16[80,1024]{1,0:T(8,128)(2,1)} %get-tuple-element.64) | copy-start | bytes 491524
  12.4 9.2 %copy-start.11 = (bf16[4,48,256]{2,1,0:T(8,128)(2,1)S(1)}, bf16[4,48,256]{2,1,0:T(8,128)(2,1)}, u32[]{:S(2)}) copy-start(bf16[4,48,256]{2,1,0:T(8,128)(2,1)} %get-tuple-element.57) | copy-start | bytes 294916
  12.4 12.4 %copy-start.10 = (bf16[4,48,256]{2,1,0:T(8,128)(2,1)S(1)}, bf16[4,48,256]{2,1,0:T(8,128)(2,1)}, u32[]{:S(2)}) copy-start(bf16[4,48,256]{2,1,0:T(8,128)(2,1)} %get-tuple-element.58) | copy-start | bytes 294916
  12.4 17.1 %copy-start.9 = (bf16[4,48,256]{2,1,0:T(8,128)(2,1)S(1)}, bf16[4,48,256]{2,1,0:T(8,128)(2,1)}, u32[]{:S(2)}) copy-start(bf16[4,48,256]{2,1,0:T(8,128)(2,1)} %get-tuple-element.59) | copy-start | bytes 294916
  12.4 45.1 %all-to-all-start = ((bf16[16,48,1280]{2,1,0:T(8,128)(2,1)}), bf16[16,48,1280]{2,1,0:T(8,128)(2,1)S(1)}, u32[]{:S(2)}, u32[]{:S(2)}) async-start(bf16[16,48,1280]{2,1,0:T(8,128)(2,1)} %get-tuple-element.63), calls=%async_computation | async-start | bytes 3932160 | tf_op jit(solution)/shard_map/all_to_all | solution.py:389
  20.0 37.5 %collective-permute-start.6 = (bf16[80,1024]{1,0:T(8,128)(2,1)S(1)}, bf16[80,1024]{1,0:T(8,128)(2,1)S(1)}, u32[]{:S(2)}, u32[]{:S(2)}) collective-permute-start(bf16[80,1024]{1,0:T(8,128)(2,1)S(1)} %copy-done.8), channel_id=1, source_target_pairs={{0,1},{1,0},{2,3},{3,2},{4,5},{5,4},{6,7},{7,6},{8,9},{9,8},{10,11... | collective-permute-start | bytes 491528 | tf_op jit(solution)/shard_map/ppermute | solution.py:393
  21.6 19.8 %collective-permute-start.3 = (bf16[4,48,256]{2,1,0:T(8,128)(2,1)S(1)}, bf16[4,48,256]{2,1,0:T(8,128)(2,1)S(1)}, u32[]{:S(2)}, u32[]{:S(2)}) collective-permute-start(bf16[4,48,256]{2,1,0:T(8,128)(2,1)S(1)} %copy-done.11), channel_id=1, source_target_pairs={{0,64},{16,80},{32,96},{48,112},{64,128},{80,144},{96,160},{112,17... | collective-permute-start | bytes 294920 | tf_op jit(solution)/shard_map/ppermute | solution.py:391
  24.9 16.6 %collective-permute-start.4 = (bf16[4,48,256]{2,1,0:T(8,128)(2,1)S(1)}, bf16[4,48,256]{2,1,0:T(8,128)(2,1)S(1)}, u32[]{:S(2)}, u32[]{:S(2)}) collective-permute-start(bf16[4,48,256]{2,1,0:T(8,128)(2,1)S(1)} %copy-done.10), channel_id=1, source_target_pairs={{0,128},{16,144},{32,160},{48,176},{64,192},{80,208},{96,224},{112... | collective-permute-start | bytes 294920 | tf_op jit(solution)/shard_map/ppermute | solution.py:391
  29.5 12.0 %collective-permute-start.5 = (bf16[4,48,256]{2,1,0:T(8,128)(2,1)S(1)}, bf16[4,48,256]{2,1,0:T(8,128)(2,1)S(1)}, u32[]{:S(2)}, u32[]{:S(2)}) collective-permute-start(bf16[4,48,256]{2,1,0:T(8,128)(2,1)S(1)} %copy-done.9), channel_id=1, source_target_pairs={{0,192},{16,208},{32,224},{48,240},{64,0},{80,16},{96,32},{112,48}... | collective-permute-start | bytes 294920 | tf_op jit(solution)/shard_map/ppermute | solution.py:391
  41.4 0.6 copy-start.5
  41.4 0.7 copy-start.6
  41.5 0.7 copy-start.7
  57.5 27.2 %copy-start = (bf16[64,2048]{1,0:T(8,128)(2,1)S(1)}, bf16[64,2048]{1,0:T(8,128)(2,1)}, u32[]{:S(2)}) copy-start(bf16[64,2048]{1,0:T(8,128)(2,1)} %cotangent_ref.3) | copy-start | bytes 786436
  57.5 27.2 %copy-start.1 = (bf16[64]{0:T(256)(128)(2,1)S(1)}, bf16[64]{0:T(256)(128)(2,1)}, u32[]{:S(2)}) copy-start(bf16[64]{0:T(256)(128)(2,1)} %param.11) | copy-start | bytes 388
  88.2 20.1 %all-to-all-start.2 = ((bf16[32,56,128]{2,1,0:T(8,128)(2,1)}), bf16[32,56,128]{2,1,0:T(8,128)(2,1)S(1)}, u32[]{:S(2)}, u32[]{:S(2)}) async-start(bf16[32,56,128]{2,1,0:T(8,128)(2,1)} %get-tuple-element.71), calls=%async_computation.2 | async-start | bytes 917504 | tf_op jit(solution)/shard_map/all_to_all | solution.py:402
  92.9 7.3 %collective-permute-start.7 = (bf16[64,1024]{1,0:T(8,128)(2,1)S(1)}, bf16[64,1024]{1,0:T(8,128)(2,1)S(1)}, u32[]{:S(2)}, u32[]{:S(2)}) collective-permute-start(bf16[64,1024]{1,0:T(8,128)(2,1)S(1)} %get-tuple-element.69), channel_id=1, source_target_pairs={{0,1},{1,0},{2,3},{3,2},{4,5},{5,4},{6,7},{7,6},{8,9},{9,8},{10,11... | collective-permute-start | bytes 393224 | tf_op jit(solution)/shard_map/ppermute | solution.py:404
  108.4 13.8 %collective-permute-start.8 = (f32[48,128]{1,0:T(8,128)S(1)}, f32[48,128]{1,0:T(8,128)S(1)}, u32[]{:S(2)}, u32[]{:S(2)}) collective-permute-start(f32[48,128]{1,0:T(8,128)S(1)} %slice.20), channel_id=1, source_target_pairs={{0,0},{1,16},{2,32},{3,48},{4,64},{5,80},{6,96},{7,112},{8,128},{9... | collective-permute-start | bytes 73736 | tf_op jit(solution)/shard_map/ppermute | solution.py:412

commit v4 on v3

--- a/solution.py
+++ b/solution.py
@@ -10,7 +10,7 @@
 
 LOW = 256
 ONES = jnp.float8_e4m3fn
-UNROLL = 8
+UNROLL = 16
 FIRST = 4
 RADIX = 4
 PAD = 32
@@ -33,6 +33,15 @@
 
 def relative(place, j, k):
     return ((place // RADIX + j) % RADIX) * RADIX + (place % RADIX + k) % RADIX
+
+
+def one_hot_small(keys, ones, rows):
+    width = keys.shape[1]
+    wide = jnp.broadcast_to(keys - 128.0, (32, width)).astype(jnp.int32).astype(jnp.int8)
+    ones = jnp.broadcast_to(ones, (32, width)).astype(ONES)
+    base = (lax.broadcasted_iota(jnp.int32, (rows, width), 0) - 128).astype(jnp.int8)
+    hit = base.reshape(rows // 32, 32, width) == wide[None]
+    return jnp.where(hit, ones[None], jnp.zeros((), ONES)).reshape(rows, width)
 
 
 def pick_kernel(place_ref, features_ref, boundary_ref, counts_ref, *refs):
@@ -138,8 +147,10 @@
             found = []
             for k in range(2):
                 group = first_group + 2 * pair + k
-                left = one_hot(rank_ref[pl.ds(group, 1), :], rank_ref.shape[1]).astype(ONES)
-                right = one_hot(low_ref[pl.ds(group, 1), :], LOW).astype(ONES)
+                rank = rank_ref[pl.ds(group, 1), :]
+                named = jnp.where(rank < 0, 0.0, 1.0)
+                left = one_hot_small(jnp.maximum(rank, 0.0), named, rank.shape[1])
+                right = one_hot_small(low_ref[pl.ds(group, 1), :], named, LOW)
                 table = lax.dot_general(left, right, NT, preferred_element_type=jnp.float32)
                 found.append(table.reshape(table.shape[0] // GROUP, GROUP, LOW))
             rows = pl.ds(pl.multiple_of(pair * 2 * GROUP, 2 * GROUP), 2 * GROUP)

time: 123 us -> 122 us (level)
  Pallas kernels: 36 us -> 33.4 us
  starting transfers between devices: 33.8 us -> 35.3 us
    all_to_all x1, starting transfers between devices: 4.65 us -> 6.18 us  [body(): lax.all_to_all(grad, ('vertex', 'feat'), split_axis=0, concat_axis=0, til...]
    pallas_call x1, Pallas kernels: 9.25 us -> 7.75 us  [first_tables(): pl.pallas_call(table_kernel, grid=(blocks,), out_shape=(jax.ShapeDtypeStr...]
  transfers between devices with their start and end apart: 11 -> 11, of which waited for: 5 -> 5; matrix products, arithmetic and copies ran while one was open for 1% -> 1% of each run, Pallas kernels for 22% -> 20%
where the time goes in v4:
time: 122 us
  starting transfers between devices  35.3 us (29%)
  Pallas kernels  33.4 us (27%)
  blocking collectives  27.1 us (22%)
  waiting for transfers between devices  21.8 us (18%)
  local copies, waits for them, and re-layouts  2.05 us (2%)
  other arithmetic  1.34 us (1%)
    all_to_all x1, blocking collectives, body(): mean = lax.all_to_all(mean, 'feat', split_axis=0, concat_axis=0, tiled=True)  27.1 us
    pallas_call x1, Pallas kernels, neighbor_mean(): pl.pallas_call(kernel, out_shape=jax.ShapeDtypeStruct((shares, columns, s...  14.2 us
    ppermute x3, starting transfers between devices, body(): lax.ppermute(far[j - 1], 'vertex', [(v, (v + j * RADIX) % partitions) for...  10.6 us
    pallas_call x1, Pallas kernels, first_tables(): pl.pallas_call(table_kernel, grid=(blocks,), out_shape=(jax.ShapeDtypeStr...  7.75 us
    all_to_all x1, starting transfers between devices, body(): lax.all_to_all(inputs, 'feat', split_axis=0, concat_axis=0, tiled=True)  7.6 us
    all_to_all x1, waiting for transfers between devices, body(): lax.all_to_all(grad, ('vertex', 'feat'), split_axis=0, concat_axis=0, til...  7.36 us
    ppermute x1, waiting for transfers between devices, body(): grad = lax.ppermute(grad[:columns], ('vertex', 'feat'), swap)  7.21 us
    all_to_all x1, starting transfers between devices, body(): lax.all_to_all(grad, ('vertex', 'feat'), split_axis=0, concat_axis=0, til...  6.18 us
  transfers between devices with their start and end apart: 11, of which 5 were waited for; matrix products, arithmetic and copies ran while one was open for 1% of the time, Pallas kernels for 20%

profile of v4, /device:TPU:36, one launch (start us, length us, event | category | flops | bytes accessed | tf_op | source)
XLA Modules:
  0.0 121.8 jit_solution(8509748136427477247)
XLA Ops:
  0.6 3.5 %pick.1 = (bf16[4,48,256]{2,1,0:T(8,128)(2,1)}, bf16[4,48,256]{2,1,0:T(8,128)(2,1)}, bf16[4,48,256]{2,1,0:T(8,128)(2,1)}, bf16[4,48,256]{2,1,0:T(8,128)(2,1)}) custom-call(s32[1]{0:T(128)} %bitcast.place_ref, bf16[48,4096]{1,0:T(8,128)(2,1)} %refs_11_.1, s32[16,256]{1,0:T(8,128)} %bitcast.14, s32[1,16]{1,0:T(1,128)} %counts_ref.1), custom_call_target="tpu_custom_call" | custom-call | tf_op jit(solution)/shard_map/pick/pallas_call | solution.py:74
  4.1 0.0 collective-permute-start
  4.1 0.1 collective-permute-start.1
  4.3 1.6 %collective-permute-start.2 = (bf16[4,48,256]{2,1,0:T(8,128)(2,1)}, bf16[4,48,256]{2,1,0:T(8,128)(2,1)S(1)}, u32[]{:S(2)}, u32[]{:S(2)}) collective-permute-start(bf16[4,48,256]{2,1,0:T(8,128)(2,1)} %get-tuple-element.44), channel_id=1, source_target_pairs={{0,48},{16,0},{32,16},{48,32},{64,112},{80,64},{96,80},{112,96},{1... | collective-permute-start | bytes 294920 | tf_op jit(solution)/shard_map/ppermute | solution.py:394
  5.9 2.6 %pack.1 = (bf16[16,48,1280]{2,1,0:T(8,128)(2,1)}, bf16[80,1024]{1,0:T(8,128)(2,1)}) custom-call(s32[1]{0:T(128)} %bitcast.2.parity_ref, bf16[48,4096]{1,0:T(8,128)(2,1)} %refs_11_.1, bf16[48,1024]{1,0:T(8,128)(2,1)} %neigh_weight_ref.1, bf16[48,1024]{1,0:T(8,128)(2,1)} %self_weight_ref.1, bf16[64,2048]{1,0:T(8,128)(2,1)} %cotangent_ref.3, bf16[1,64]{1,0:T(2,128)(2,1)} %bitcast.12), custom_call_target="tpu_custom_call" | custom-call | tf_op jit(solution)/shard_map/pack/pallas_call | solution.py:125
  8.5 0.4 collective-permute-done.refs_1_
  8.9 1.1 collective-permute-done.1.refs_2_
  10.0 0.0 collective-permute-done.2.refs_3_
  10.0 0.0 copy-done.2
  10.0 0.6 copy-done.3
  10.6 0.0 copy-done.4
  10.7 1.8 %regroup.1 = (bf16[4,48,256]{2,1,0:T(8,128)(2,1)}, bf16[4,48,256]{2,1,0:T(8,128)(2,1)}, bf16[4,48,256]{2,1,0:T(8,128)(2,1)}) custom-call(bf16[4,48,256]{2,1,0:T(8,128)(2,1)} %get-tuple-element.38.refs_0_, bf16[4,48,256]{2,1,0:T(8,128)(2,1)} %copy-done.2, bf16[4,48,256]{2,1,0:T(8,128)(2,1)} %copy-done.3, bf16[4,48,256]{2,1,0:T(8,128)(2,1)} %copy-done.4), custom_call_target="tpu_custom_call" | custom-call | tf_op jit(solution)/shard_map/regroup/pallas_call | solution.py:94
  12.4 0.0 copy-start.9
  12.4 7.6 %all-to-all-start = ((bf16[16,48,1280]{2,1,0:T(8,128)(2,1)}), bf16[16,48,1280]{2,1,0:T(8,128)(2,1)S(1)}, u32[]{:S(2)}, u32[]{:S(2)}) async-start(bf16[16,48,1280]{2,1,0:T(8,128)(2,1)} %get-tuple-element.63), calls=%async_computation | async-start | bytes 3932160 | tf_op jit(solution)/shard_map/all_to_all | solution.py:400
  20.0 0.0 copy-done.8
  20.0 1.6 %collective-permute-start.6 = (bf16[80,1024]{1,0:T(8,128)(2,1)S(1)}, bf16[80,1024]{1,0:T(8,128)(2,1)S(1)}, u32[]{:S(2)}, u32[]{:S(2)}) collective-permute-start(bf16[80,1024]{1,0:T(8,128)(2,1)S(1)} %copy-done.8), channel_id=1, source_target_pairs={{0,1},{1,0},{2,3},{3,2},{4,5},{5,4},{6,7},{7,6},{8,9},{9,8},{10,11... | collective-permute-start | bytes 491528 | tf_op jit(solution)/shard_map/ppermute | solution.py:404
  21.6 0.0 copy-done.11
  21.6 3.3 %collective-permute-start.3 = (bf16[4,48,256]{2,1,0:T(8,128)(2,1)S(1)}, bf16[4,48,256]{2,1,0:T(8,128)(2,1)S(1)}, u32[]{:S(2)}, u32[]{:S(2)}) collective-permute-start(bf16[4,48,256]{2,1,0:T(8,128)(2,1)S(1)} %copy-done.11), channel_id=1, source_target_pairs={{0,64},{16,80},{32,96},{48,112},{64,128},{80,144},{96,160},{112,17... | collective-permute-start | bytes 294920 | tf_op jit(solution)/shard_map/ppermute | solution.py:402
  24.8 0.0 copy-done.10
  24.9 4.6 %collective-permute-start.4 = (bf16[4,48,256]{2,1,0:T(8,128)(2,1)S(1)}, bf16[4,48,256]{2,1,0:T(8,128)(2,1)S(1)}, u32[]{:S(2)}, u32[]{:S(2)}) collective-permute-start(bf16[4,48,256]{2,1,0:T(8,128)(2,1)S(1)} %copy-done.10), channel_id=1, source_target_pairs={{0,128},{16,144},{32,160},{48,176},{64,192},{80,208},{96,224},{112... | collective-permute-start | bytes 294920 | tf_op jit(solution)/shard_map/ppermute | solution.py:402
  29.5 0.0 copy-done.9
  29.5 2.7 %collective-permute-start.5 = (bf16[4,48,256]{2,1,0:T(8,128)(2,1)S(1)}, bf16[4,48,256]{2,1,0:T(8,128)(2,1)S(1)}, u32[]{:S(2)}, u32[]{:S(2)}) collective-permute-start(bf16[4,48,256]{2,1,0:T(8,128)(2,1)S(1)} %copy-done.9), channel_id=1, source_target_pairs={{0,192},{16,208},{32,224},{48,240},{64,0},{80,16},{96,32},{112,48}... | collective-permute-start | bytes 294920 | tf_op jit(solution)/shard_map/ppermute | solution.py:402
  32.2 7.8 %first_tables.1 = (bf16[1024,4096]{1,0:T(8,128)(2,1)}, f32[1024,48]{1,0:T(8,128)}, f32[256,256]{1,0:T(8,128)}, f32[256,256]{1,0:T(8,128)}) custom-call(s32[25,2048]{1,0:T(8,128)} %refs_10_.1, bf16[48,4096]{1,0:T(8,128)(2,1)} %refs_11_.1), custom_call_target="tpu_custom_call" | custom-call | tf_op jit(solution)/shard_map/first_tables/pallas_call | solution.py:200
  39.9 0.0 collective-permute-done.3.refs_4_
  39.9 0.0 collective-permute-done.4.refs_5_
  39.9 0.0 copy-start.6
  39.9 0.0 collective-permute-done.5.refs_6_
  40.0 0.6 copy-done.5
  40.5 0.0 copy-done.6
  40.6 0.0 copy-done.7
  40.6 14.2 %mean.1 = bf16[16,48,1024]{2,1,0:T(8,128)(2,1)} custom-call(s32[1]{0:T(128)} %bitcast.place_ref, bf16[1024,4096]{1,0:T(8,128)(2,1)} %get-tuple-element.56.remote_ref, bf16[4,48,256]{2,1,0:T(8,128)(2,1)} %get-tuple-element.38.refs_0_, bf16[4,48,256]{2,1,0:T(8,128)(2,1)} %copy-done.2, bf16[4,48,256]{2,1,0:T(8,128)(2,1)} %copy-done.3, ...), custom_call_target="tpu_custom_call" | custom-call | tf_op jit(solution)/shard_map/mean/pallas_call | solution.py:273
  54.9 0.0 copy-start
  54.9 0.0 copy-start.1
  54.9 0.0 collective-permute-done.6.traded_ref.traded_bias_ref
  54.9 0.0 all-to-all-done
  54.9 27.1 %all_to_all.15 = bf16[16,48,1024]{2,1,0:T(8,128)(2,1)S(1)} all-to-all(bf16[16,48,1024]{2,1,0:T(8,128)(2,1)} %mean.1), channel_id=1, replica_groups=mesh['vertex'=16,'feat'=16] {'feat'}, dimensions={0} | all-to-all | bytes 3145728 | tf_op jit(solution)/shard_map/all_to_all | solution.py:409
  82.0 0.0 copy-done
  82.0 3.5 %layer.1 = (bf16[64,1024]{1,0:T(8,128)(2,1)S(1)}, bf16[64,1024]{1,0:T(8,128)(2,1)S(1)}, bf16[32,56,128]{2,1,0:T(8,128)(2,1)}) custom-call(s32[1]{0:T(128)} %bitcast.2.parity_ref, bf16[768,1280]{1,0:T(8,128)(2,1)S(1)} %bitcast.8, bf16[768,1024]{1,0:T(8,128)(2,1)S(1)} %bitcast.11, bf16[768,1280]{1,0:T(8,128)(2,1)S(1)} %bitcast.9, ...), custom_call_target="tpu_custom_call" | custom-call | tf_op jit(solution)/shard_map/layer/pallas_call | solution.py:352
  85.6 6.2 %all-to-all-start.2 = ((bf16[32,56,128]{2,1,0:T(8,128)(2,1)}), bf16[32,56,128]{2,1,0:T(8,128)(2,1)S(1)}, u32[]{:S(2)}, u32[]{:S(2)}) async-start(bf16[32,56,128]{2,1,0:T(8,128)(2,1)} %get-tuple-element.71), calls=%async_computation.2 | async-start | bytes 917504 | tf_op jit(solution)/shard_map/all_to_all | solution.py:413
  91.8 1.6 %collective-permute-start.7 = (bf16[64,1024]{1,0:T(8,128)(2,1)S(1)}, bf16[64,1024]{1,0:T(8,128)(2,1)S(1)}, u32[]{:S(2)}, u32[]{:S(2)}) collective-permute-start(bf16[64,1024]{1,0:T(8,128)(2,1)S(1)} %get-tuple-element.69), channel_id=1, source_target_pairs={{0,1},{1,0},{2,3},{3,2},{4,5},{5,4},{6,7},{7,6},{8,9},{9,8},{10,11... | collective-permute-start | bytes 393224 | tf_op jit(solution)/shard_map/ppermute | solution.py:415
  93.3 5.8 %collective-permute-done.7 = bf16[64,1024]{1,0:T(8,128)(2,1)S(1)} collective-permute-done((bf16[64,1024]{1,0:T(8,128)(2,1)S(1)}, bf16[64,1024]{1,0:T(8,128)(2,1)S(1)}, u32[]{:S(2)}, u32[]{:S(2)}) %collective-permute-start.7) | collective-permute-done | bytes 131104 | tf_op jit(solution)/shard_map/ppermute | solution.py:415
  99.1 0.7 pad_maximum_fusion
  99.8 7.4 %all-to-all-done.2 = bf16[32,56,128]{2,1,0:T(8,128)(2,1)S(1)} async-done(((bf16[32,56,128]{2,1,0:T(8,128)(2,1)}), bf16[32,56,128]{2,1,0:T(8,128)(2,1)S(1)}, u32[]{:S(2)}, u32[]{:S(2)}) %all-to-all-start.2) | async-done | bytes 458784 | tf_op jit(solution)/shard_map/all_to_all | solution.py:413
  107.2 0.1 convert_reduce_fusion
  107.3 6.1 %collective-permute-start.8 = (f32[48,128]{1,0:T(8,128)S(1)}, f32[48,128]{1,0:T(8,128)S(1)}, u32[]{:S(2)}, u32[]{:S(2)}) collective-permute-start(f32[48,128]{1,0:T(8,128)S(1)} %slice.20), channel_id=1, source_target_pairs={{0,0},{1,16},{2,32},{3,48},{4,64},{5,80},{6,96},{7,112},{8,128},{9... | collective-permute-start | bytes 73736 | tf_op jit(solution)/shard_map/ppermute | solution.py:423
  113.4 0.5 fusion
  113.9 7.2 %collective-permute-done.8 = f32[48,128]{1,0:T(8,128)S(1)} collective-permute-done((f32[48,128]{1,0:T(8,128)S(1)}, f32[48,128]{1,0:T(8,128)S(1)}, u32[]{:S(2)}, u32[]{:S(2)}) %collective-permute-start.8) | collective-permute-done | bytes 24608 | tf_op jit(solution)/shard_map/ppermute | solution.py:423
  121.1 0.7 fusion.1
  (12 shorter events, 0.0 us)
Async XLA Ops:
  4.1 4.8 %collective-permute-start = (bf16[4,48,256]{2,1,0:T(8,128)(2,1)}, bf16[4,48,256]{2,1,0:T(8,128)(2,1)S(1)}, u32[]{:S(2)}, u32[]{:S(2)}) collective-permute-start(bf16[4,48,256]{2,1,0:T(8,128)(2,1)} %get-tuple-element.42), channel_id=1, source_target_pairs={{0,16},{16,32},{32,48},{48,0},{64,80},{80,96},{96,112},{112,64},{1... | collective-permute-start | bytes 294920 | tf_op jit(solution)/shard_map/ppermute | solution.py:394
  4.1 5.9 %collective-permute-start.1 = (bf16[4,48,256]{2,1,0:T(8,128)(2,1)}, bf16[4,48,256]{2,1,0:T(8,128)(2,1)S(1)}, u32[]{:S(2)}, u32[]{:S(2)}) collective-permute-start(bf16[4,48,256]{2,1,0:T(8,128)(2,1)} %get-tuple-element.43), channel_id=1, source_target_pairs={{0,32},{16,48},{32,0},{48,16},{64,96},{80,112},{96,64},{112,80},{1... | collective-permute-start | bytes 294920 | tf_op jit(solution)/shard_map/ppermute | solution.py:394
  4.3 5.7 %collective-permute-start.2 = (bf16[4,48,256]{2,1,0:T(8,128)(2,1)}, bf16[4,48,256]{2,1,0:T(8,128)(2,1)S(1)}, u32[]{:S(2)}, u32[]{:S(2)}) collective-permute-start(bf16[4,48,256]{2,1,0:T(8,128)(2,1)} %get-tuple-element.44), channel_id=1, source_target_pairs={{0,48},{16,0},{32,16},{48,32},{64,112},{80,64},{96,80},{112,96},{1... | collective-permute-start | bytes 294920 | tf_op jit(solution)/shard_map/ppermute | solution.py:394
  8.9 1.1 copy-start.2
  10.0 0.6 copy-start.3
  10.0 0.7 copy-start.4
  12.4 7.6 %copy-start.8 = (bf16[80,1024]{1,0:T(8,128)(2,1)S(1)}, bf16[80,1024]{1,0:T(8,128)(2,1)}, u32[]{:S(2)}) copy-start(bf16[80,1024]{1,0:T(8,128)(2,1)} %get-tuple-element.64) | copy-start | bytes 491524
  12.4 9.2 %copy-start.11 = (bf16[4,48,256]{2,1,0:T(8,128)(2,1)S(1)}, bf16[4,48,256]{2,1,0:T(8,128)(2,1)}, u32[]{:S(2)}) copy-start(bf16[4,48,256]{2,1,0:T(8,128)(2,1)} %get-tuple-element.57) | copy-start | bytes 294916
  12.4 12.4 %copy-start.10 = (bf16[4,48,256]{2,1,0:T(8,128)(2,1)S(1)}, bf16[4,48,256]{2,1,0:T(8,128)(2,1)}, u32[]{:S(2)}) copy-start(bf16[4,48,256]{2,1,0:T(8,128)(2,1)} %get-tuple-element.58) | copy-start | bytes 294916
  12.4 17.1 %copy-start.9 = (bf16[4,48,256]{2,1,0:T(8,128)(2,1)S(1)}, bf16[4,48,256]{2,1,0:T(8,128)(2,1)}, u32[]{:S(2)}) copy-start(bf16[4,48,256]{2,1,0:T(8,128)(2,1)} %get-tuple-element.59) | copy-start | bytes 294916
  12.4 42.5 %all-to-all-start = ((bf16[16,48,1280]{2,1,0:T(8,128)(2,1)}), bf16[16,48,1280]{2,1,0:T(8,128)(2,1)S(1)}, u32[]{:S(2)}, u32[]{:S(2)}) async-start(bf16[16,48,1280]{2,1,0:T(8,128)(2,1)} %get-tuple-element.63), calls=%async_computation | async-start | bytes 3932160 | tf_op jit(solution)/shard_map/all_to_all | solution.py:400
  20.0 34.9 %collective-permute-start.6 = (bf16[80,1024]{1,0:T(8,128)(2,1)S(1)}, bf16[80,1024]{1,0:T(8,128)(2,1)S(1)}, u32[]{:S(2)}, u32[]{:S(2)}) collective-permute-start(bf16[80,1024]{1,0:T(8,128)(2,1)S(1)} %copy-done.8), channel_id=1, source_target_pairs={{0,1},{1,0},{2,3},{3,2},{4,5},{5,4},{6,7},{7,6},{8,9},{9,8},{10,11... | collective-permute-start | bytes 491528 | tf_op jit(solution)/shard_map/ppermute | solution.py:404
  21.6 18.3 %collective-permute-start.3 = (bf16[4,48,256]{2,1,0:T(8,128)(2,1)S(1)}, bf16[4,48,256]{2,1,0:T(8,128)(2,1)S(1)}, u32[]{:S(2)}, u32[]{:S(2)}) collective-permute-start(bf16[4,48,256]{2,1,0:T(8,128)(2,1)S(1)} %copy-done.11), channel_id=1, source_target_pairs={{0,64},{16,80},{32,96},{48,112},{64,128},{80,144},{96,160},{112,17... | collective-permute-start | bytes 294920 | tf_op jit(solution)/shard_map/ppermute | solution.py:402
  24.9 15.1 %collective-permute-start.4 = (bf16[4,48,256]{2,1,0:T(8,128)(2,1)S(1)}, bf16[4,48,256]{2,1,0:T(8,128)(2,1)S(1)}, u32[]{:S(2)}, u32[]{:S(2)}) collective-permute-start(bf16[4,48,256]{2,1,0:T(8,128)(2,1)S(1)} %copy-done.10), channel_id=1, source_target_pairs={{0,128},{16,144},{32,160},{48,176},{64,192},{80,208},{96,224},{112... | collective-permute-start | bytes 294920 | tf_op jit(solution)/shard_map/ppermute | solution.py:402
  29.5 10.4 %collective-permute-start.5 = (bf16[4,48,256]{2,1,0:T(8,128)(2,1)S(1)}, bf16[4,48,256]{2,1,0:T(8,128)(2,1)S(1)}, u32[]{:S(2)}, u32[]{:S(2)}) collective-permute-start(bf16[4,48,256]{2,1,0:T(8,128)(2,1)S(1)} %copy-done.9), channel_id=1, source_target_pairs={{0,192},{16,208},{32,224},{48,240},{64,0},{80,16},{96,32},{112,48}... | collective-permute-start | bytes 294920 | tf_op jit(solution)/shard_map/ppermute | solution.py:402
  39.9 0.6 copy-start.5
  39.9 0.7 copy-start.6
  39.9 0.7 copy-start.7
  54.9 27.2 %copy-start = (bf16[64,2048]{1,0:T(8,128)(2,1)S(1)}, bf16[64,2048]{1,0:T(8,128)(2,1)}, u32[]{:S(2)}) copy-start(bf16[64,2048]{1,0:T(8,128)(2,1)} %cotangent_ref.3) | copy-start | bytes 786436
  54.9 27.2 %copy-start.1 = (bf16[64]{0:T(256)(128)(2,1)S(1)}, bf16[64]{0:T(256)(128)(2,1)}, u32[]{:S(2)}) copy-start(bf16[64]{0:T(256)(128)(2,1)} %param.11) | copy-start | bytes 388
  85.6 21.6 %all-to-all-start.2 = ((bf16[32,56,128]{2,1,0:T(8,128)(2,1)}), bf16[32,56,128]{2,1,0:T(8,128)(2,1)S(1)}, u32[]{:S(2)}, u32[]{:S(2)}) async-start(bf16[32,56,128]{2,1,0:T(8,128)(2,1)} %get-tuple-element.71), calls=%async_computation.2 | async-start | bytes 917504 | tf_op jit(solution)/shard_map/all_to_all | solution.py:413
  91.8 7.3 %collective-permute-start.7 = (bf16[64,1024]{1,0:T(8,128)(2,1)S(1)}, bf16[64,1024]{1,0:T(8,128)(2,1)S(1)}, u32[]{:S(2)}, u32[]{:S(2)}) collective-permute-start(bf16[64,1024]{1,0:T(8,128)(2,1)S(1)} %get-tuple-element.69), channel_id=1, source_target_pairs={{0,1},{1,0},{2,3},{3,2},{4,5},{5,4},{6,7},{7,6},{8,9},{9,8},{10,11... | collective-permute-start | bytes 393224 | tf_op jit(solution)/shard_map/ppermute | solution.py:415
  107.3 13.8 %collective-permute-start.8 = (f32[48,128]{1,0:T(8,128)S(1)}, f32[48,128]{1,0:T(8,128)S(1)}, u32[]{:S(2)}, u32[]{:S(2)}) collective-permute-start(f32[48,128]{1,0:T(8,128)S(1)} %slice.20), channel_id=1, source_target_pairs={{0,0},{1,16},{2,32},{3,48},{4,64},{5,80},{6,96},{7,112},{8,128},{9... | collective-permute-start | bytes 73736 | tf_op jit(solution)/shard_map/ppermute | solution.py:423

commit v5 on v4

--- a/solution.py
+++ b/solution.py
@@ -11,7 +11,7 @@
 LOW = 256
 ONES = jnp.float8_e4m3fn
 UNROLL = 16
-FIRST = 4
+FIRST = 5
 RADIX = 4
 PAD = 32
 GROUP = 8
@@ -375,6 +375,20 @@
     )(parity, inputs, mean, inputs, inputs, bias, cotangent, traded, traded)
 
 
+def gradient_holders(shares, partitions):
+    side, depth = math.isqrt(shares), partitions // 2
+    ring = lambda a, b, size: min((a - b) % size, (b - a) % size)
+    holders = []
+    for f in range(shares):
+        flat = lambda g: ring(g // side, f // side, side) + ring(g % side, f % side, side)
+        rise = lambda v: 2 * ring(v // 2, f // 2, depth) + (v % 2 != f % 2)
+        row = [0] * shares
+        for v, g in zip(sorted(range(partitions), key=rise), sorted(range(shares), key=flat, reverse=True)):
+            row[g] = v
+        holders.append(row)
+    return holders
+
+
 def body(features, neigh_weight, self_weight, bias, neighbors, boundary, counts, cotangent):
     columns, nodes = features.shape
     partitions = lax.axis_size("vertex")
@@ -409,7 +423,9 @@
     mean = lax.all_to_all(mean, "feat", split_axis=0, concat_axis=0, tiled=True)
     mean = mean.reshape(shares * columns, mean.shape[2])
     kept, sent, grad = layer(parity, inputs, mean, bias, cotangent, traded, shares)
-    members = [[v * shares + 2 * q + k for v in range(partitions) for k in range(2)] for q in range(shares // 2)]
+    holders = gradient_holders(shares, partitions)
+    members = [[holders[2 * q + k][g] * shares + 2 * q + k for g in range(shares) for k in range(2)]
+               for q in range(shares // 2)]
     grad = lax.all_to_all(
         grad, ("vertex", "feat"), split_axis=0, concat_axis=0, tiled=True, axis_index_groups=members)
     other = lax.ppermute(sent, "feat", trade)
@@ -419,7 +435,7 @@
     factor = 1.0 / math.sqrt(seed_count * partitions)
     grad = jnp.sum(grad.astype(jnp.float32), axis=0) * factor
     bias_out = grad[columns, :hidden] + grad[columns + 1, :hidden]
-    swap = [(v * shares + f, f * shares + v) for v in range(partitions) for f in range(shares)]
+    swap = [(holders[f][g] * shares + f, f * shares + g) for f in range(shares) for g in range(shares)]
     grad = lax.ppermute(grad[:columns], ("vertex", "feat"), swap)
     return activation, grad[:, :hidden], grad[:, hidden:], bias_out
 

time: 122 us -> 118 us (0.967)
  the two profiles are of different devices: /device:TPU:36 before, /device:TPU:6 now
where the time goes in v5:
time: 118 us; the launch traced here: 117 us
  starting transfers between devices  34.3 us (29%)
  Pallas kernels  33.6 us (28%)
  blocking collectives  27.4 us (23%)
  waiting for transfers between devices  17.8 us (15%)
  local copies, waits for them, and re-layouts  2.03 us (2%)
  other arithmetic  1.34 us (1%)
    all_to_all x1, blocking collectives, body(): mean = lax.all_to_all(mean, 'feat', split_axis=0, concat_axis=0, tiled=True)  27.4 us
    pallas_call x1, Pallas kernels, neighbor_mean(): pl.pallas_call(kernel, out_shape=jax.ShapeDtypeStruct((shares, columns, s...  13 us
    ppermute x3, starting transfers between devices, body(): lax.ppermute(far[j - 1], 'vertex', [(v, (v + j * RADIX) % partitions) for...  10.4 us
    pallas_call x1, Pallas kernels, first_tables(): pl.pallas_call(table_kernel, grid=(blocks,), out_shape=(jax.ShapeDtypeStr...  9.18 us
    all_to_all x1, starting transfers between devices, body(): lax.all_to_all(inputs, 'feat', split_axis=0, concat_axis=0, tiled=True)  7.57 us
    ppermute x1, waiting for transfers between devices, body(): other = lax.ppermute(sent, 'feat', trade)  6.26 us
    all_to_all x1, starting transfers between devices, body(): lax.all_to_all(grad, ('vertex', 'feat'), split_axis=0, concat_axis=0, til...  6.04 us
    ppermute x1, waiting for transfers between devices, body(): grad = lax.ppermute(grad[:columns], ('vertex', 'feat'), swap)  5.7 us
  transfers between devices with their start and end apart: 11, of which 4 were waited for; matrix products, arithmetic and copies ran while one was open for 1% of the time, Pallas kernels for 21%

profile of v5, /device:TPU:6, one launch (start us, length us, event | category | flops | bytes accessed | tf_op | source)
XLA Modules:
  0.0 117.2 jit_solution(4423913760725791050)
XLA Ops:
  0.6 3.5 %pick.1 = (bf16[4,48,256]{2,1,0:T(8,128)(2,1)}, bf16[4,48,256]{2,1,0:T(8,128)(2,1)}, bf16[4,48,256]{2,1,0:T(8,128)(2,1)}, bf16[4,48,256]{2,1,0:T(8,128)(2,1)}) custom-call(s32[1]{0:T(128)} %bitcast.place_ref, bf16[48,4096]{1,0:T(8,128)(2,1)} %refs_11_.1, s32[16,256]{1,0:T(8,128)} %bitcast.14, s32[1,16]{1,0:T(1,128)} %counts_ref.1), custom_call_target="tpu_custom_call" | custom-call | tf_op jit(solution)/shard_map/pick/pallas_call | solution.py:74
  4.1 0.0 collective-permute-start
  4.1 1.9 %collective-permute-start.1 = (bf16[4,48,256]{2,1,0:T(8,128)(2,1)}, bf16[4,48,256]{2,1,0:T(8,128)(2,1)S(1)}, u32[]{:S(2)}, u32[]{:S(2)}) collective-permute-start(bf16[4,48,256]{2,1,0:T(8,128)(2,1)} %get-tuple-element.43), channel_id=1, source_target_pairs={{0,32},{16,48},{32,0},{48,16},{64,96},{80,112},{96,64},{112,80},{1... | collective-permute-start | bytes 294920 | tf_op jit(solution)/shard_map/ppermute | solution.py:408
  6.1 1.4 %collective-permute-start.2 = (bf16[4,48,256]{2,1,0:T(8,128)(2,1)}, bf16[4,48,256]{2,1,0:T(8,128)(2,1)S(1)}, u32[]{:S(2)}, u32[]{:S(2)}) collective-permute-start(bf16[4,48,256]{2,1,0:T(8,128)(2,1)} %get-tuple-element.44), channel_id=1, source_target_pairs={{0,48},{16,0},{32,16},{48,32},{64,112},{80,64},{96,80},{112,96},{1... | collective-permute-start | bytes 294920 | tf_op jit(solution)/shard_map/ppermute | solution.py:408
  7.5 2.6 %pack.1 = (bf16[16,48,1280]{2,1,0:T(8,128)(2,1)}, bf16[80,1024]{1,0:T(8,128)(2,1)}) custom-call(s32[1]{0:T(128)} %bitcast.2.parity_ref, bf16[48,4096]{1,0:T(8,128)(2,1)} %refs_11_.1, bf16[48,1024]{1,0:T(8,128)(2,1)} %neigh_weight_ref.1, bf16[48,1024]{1,0:T(8,128)(2,1)} %self_weight_ref.1, bf16[64,2048]{1,0:T(8,128)(2,1)} %cotangent_ref.3, bf16[1,64]{1,0:T(2,128)(2,1)} %bitcast.12), custom_call_target="tpu_custom_call" | custom-call | tf_op jit(solution)/shard_map/pack/pallas_call | solution.py:125
  10.1 0.0 collective-permute-done.refs_1_
  10.1 0.0 collective-permute-done.1.refs_2_
  10.1 0.0 copy-start.3
  10.1 1.0 collective-permute-done.2.refs_3_
  11.1 0.0 copy-done.2
  11.1 0.0 copy-done.3
  11.1 0.6 copy-done.4
  11.7 1.8 %regroup.1 = (bf16[4,48,256]{2,1,0:T(8,128)(2,1)}, bf16[4,48,256]{2,1,0:T(8,128)(2,1)}, bf16[4,48,256]{2,1,0:T(8,128)(2,1)}) custom-call(bf16[4,48,256]{2,1,0:T(8,128)(2,1)} %get-tuple-element.38.refs_0_, bf16[4,48,256]{2,1,0:T(8,128)(2,1)} %copy-done.2, bf16[4,48,256]{2,1,0:T(8,128)(2,1)} %copy-done.3, bf16[4,48,256]{2,1,0:T(8,128)(2,1)} %copy-done.4), custom_call_target="tpu_custom_call" | custom-call | tf_op jit(solution)/shard_map/regroup/pallas_call | solution.py:94
  13.5 0.0 copy-start.9
  13.5 7.6 %all-to-all-start = ((bf16[16,48,1280]{2,1,0:T(8,128)(2,1)}), bf16[16,48,1280]{2,1,0:T(8,128)(2,1)S(1)}, u32[]{:S(2)}, u32[]{:S(2)}) async-start(bf16[16,48,1280]{2,1,0:T(8,128)(2,1)} %get-tuple-element.63), calls=%async_computation | async-start | bytes 3932160 | tf_op jit(solution)/shard_map/all_to_all | solution.py:414
  21.1 0.0 copy-done.8
  21.1 1.6 %collective-permute-start.6 = (bf16[80,1024]{1,0:T(8,128)(2,1)S(1)}, bf16[80,1024]{1,0:T(8,128)(2,1)S(1)}, u32[]{:S(2)}, u32[]{:S(2)}) collective-permute-start(bf16[80,1024]{1,0:T(8,128)(2,1)S(1)} %copy-done.8), channel_id=1, source_target_pairs={{0,1},{1,0},{2,3},{3,2},{4,5},{5,4},{6,7},{7,6},{8,9},{9,8},{10,11... | collective-permute-start | bytes 491528 | tf_op jit(solution)/shard_map/ppermute | solution.py:418
  22.6 0.0 copy-done.11
  22.7 3.3 %collective-permute-start.3 = (bf16[4,48,256]{2,1,0:T(8,128)(2,1)S(1)}, bf16[4,48,256]{2,1,0:T(8,128)(2,1)S(1)}, u32[]{:S(2)}, u32[]{:S(2)}) collective-permute-start(bf16[4,48,256]{2,1,0:T(8,128)(2,1)S(1)} %copy-done.11), channel_id=1, source_target_pairs={{0,64},{16,80},{32,96},{48,112},{64,128},{80,144},{96,160},{112,17... | collective-permute-start | bytes 294920 | tf_op jit(solution)/shard_map/ppermute | solution.py:416
  25.9 4.5 %collective-permute-start.4 = (bf16[4,48,256]{2,1,0:T(8,128)(2,1)S(1)}, bf16[4,48,256]{2,1,0:T(8,128)(2,1)S(1)}, u32[]{:S(2)}, u32[]{:S(2)}) collective-permute-start(bf16[4,48,256]{2,1,0:T(8,128)(2,1)S(1)} %copy-done.10), channel_id=1, source_target_pairs={{0,128},{16,144},{32,160},{48,176},{64,192},{80,208},{96,224},{112... | collective-permute-start | bytes 294920 | tf_op jit(solution)/shard_map/ppermute | solution.py:416
  30.4 0.0 copy-done.9
  30.4 2.7 %collective-permute-start.5 = (bf16[4,48,256]{2,1,0:T(8,128)(2,1)S(1)}, bf16[4,48,256]{2,1,0:T(8,128)(2,1)S(1)}, u32[]{:S(2)}, u32[]{:S(2)}) collective-permute-start(bf16[4,48,256]{2,1,0:T(8,128)(2,1)S(1)} %copy-done.9), channel_id=1, source_target_pairs={{0,192},{16,208},{32,224},{48,240},{64,0},{80,16},{96,32},{112,48}... | collective-permute-start | bytes 294920 | tf_op jit(solution)/shard_map/ppermute | solution.py:416
  33.1 9.2 %first_tables.1 = (bf16[1280,4096]{1,0:T(8,128)(2,1)}, f32[1280,48]{1,0:T(8,128)}, f32[256,256]{1,0:T(8,128)}, f32[256,256]{1,0:T(8,128)}) custom-call(s32[25,2048]{1,0:T(8,128)} %refs_10_.1, bf16[48,4096]{1,0:T(8,128)(2,1)} %refs_11_.1), custom_call_target="tpu_custom_call" | custom-call | tf_op jit(solution)/shard_map/first_tables/pallas_call | solution.py:200
  42.3 0.0 collective-permute-done.3.refs_4_
  42.3 0.0 collective-permute-done.4.refs_5_
  42.3 0.0 copy-start.6
  42.3 0.0 collective-permute-done.5.refs_6_
  42.3 0.6 copy-done.5
  42.9 0.0 copy-done.6
  43.0 0.0 copy-done.7
  43.0 13.0 %mean.1 = bf16[16,48,1024]{2,1,0:T(8,128)(2,1)} custom-call(s32[1]{0:T(128)} %bitcast.place_ref, bf16[1280,4096]{1,0:T(8,128)(2,1)} %get-tuple-element.56.remote_ref, bf16[4,48,256]{2,1,0:T(8,128)(2,1)} %get-tuple-element.38.refs_0_, bf16[4,48,256]{2,1,0:T(8,128)(2,1)} %copy-done.2, bf16[4,48,256]{2,1,0:T(8,128)(2,1)} %copy-done.3, ...), custom_call_target="tpu_custom_call" | custom-call | tf_op jit(solution)/shard_map/mean/pallas_call | solution.py:273
  56.0 0.0 copy-start
  56.0 0.0 copy-start.1
  56.0 0.0 collective-permute-done.6.traded_ref.traded_bias_ref
  56.0 0.0 all-to-all-done
  56.0 27.4 %all_to_all.15 = bf16[16,48,1024]{2,1,0:T(8,128)(2,1)S(1)} all-to-all(bf16[16,48,1024]{2,1,0:T(8,128)(2,1)} %mean.1), channel_id=1, replica_groups=mesh['vertex'=16,'feat'=16] {'feat'}, dimensions={0} | all-to-all | bytes 3145728 | tf_op jit(solution)/shard_map/all_to_all | solution.py:423
  83.5 0.0 copy-done.1
  83.5 3.5 %layer.1 = (bf16[64,1024]{1,0:T(8,128)(2,1)S(1)}, bf16[64,1024]{1,0:T(8,128)(2,1)S(1)}, bf16[32,56,128]{2,1,0:T(8,128)(2,1)}) custom-call(s32[1]{0:T(128)} %bitcast.2.parity_ref, bf16[768,1280]{1,0:T(8,128)(2,1)S(1)} %bitcast.8, bf16[768,1024]{1,0:T(8,128)(2,1)S(1)} %bitcast.11, bf16[768,1280]{1,0:T(8,128)(2,1)S(1)} %bitcast.9, ...), custom_call_target="tpu_custom_call" | custom-call | tf_op jit(solution)/shard_map/layer/pallas_call | solution.py:352
  87.0 6.0 %all-to-all-start.2 = ((bf16[32,56,128]{2,1,0:T(8,128)(2,1)}), bf16[32,56,128]{2,1,0:T(8,128)(2,1)S(1)}, u32[]{:S(2)}, u32[]{:S(2)}) async-start(bf16[32,56,128]{2,1,0:T(8,128)(2,1)} %get-tuple-element.71), calls=%async_computation.2 | async-start | bytes 917504 | tf_op jit(solution)/shard_map/all_to_all | solution.py:429
  93.0 1.6 %collective-permute-start.7 = (bf16[64,1024]{1,0:T(8,128)(2,1)S(1)}, bf16[64,1024]{1,0:T(8,128)(2,1)S(1)}, u32[]{:S(2)}, u32[]{:S(2)}) collective-permute-start(bf16[64,1024]{1,0:T(8,128)(2,1)S(1)} %get-tuple-element.69), channel_id=1, source_target_pairs={{0,1},{1,0},{2,3},{3,2},{4,5},{5,4},{6,7},{7,6},{8,9},{9,8},{10,11... | collective-permute-start | bytes 393224 | tf_op jit(solution)/shard_map/ppermute | solution.py:431
  94.6 6.3 %collective-permute-done.7 = bf16[64,1024]{1,0:T(8,128)(2,1)S(1)} collective-permute-done((bf16[64,1024]{1,0:T(8,128)(2,1)S(1)}, bf16[64,1024]{1,0:T(8,128)(2,1)S(1)}, u32[]{:S(2)}, u32[]{:S(2)}) %collective-permute-start.7) | collective-permute-done | bytes 131104 | tf_op jit(solution)/shard_map/ppermute | solution.py:431
  100.9 0.7 pad_maximum_fusion
  101.6 4.9 %all-to-all-done.2 = bf16[32,56,128]{2,1,0:T(8,128)(2,1)S(1)} async-done(((bf16[32,56,128]{2,1,0:T(8,128)(2,1)}), bf16[32,56,128]{2,1,0:T(8,128)(2,1)S(1)}, u32[]{:S(2)}, u32[]{:S(2)}) %all-to-all-start.2) | async-done | bytes 458784 | tf_op jit(solution)/shard_map/all_to_all | solution.py:429
  106.5 0.1 convert_reduce_fusion
  106.6 3.7 %collective-permute-start.8 = (f32[48,128]{1,0:T(8,128)S(1)}, f32[48,128]{1,0:T(8,128)S(1)}, u32[]{:S(2)}, u32[]{:S(2)}) collective-permute-start(f32[48,128]{1,0:T(8,128)S(1)} %slice.20), channel_id=1, source_target_pairs={{144,0},{160,1},{240,2},{112,3},{176,4},{64,5},{16,6},{192,7},{80,... | collective-permute-start | bytes 73736 | tf_op jit(solution)/shard_map/ppermute | solution.py:439
  110.3 0.5 fusion
  110.8 5.7 %collective-permute-done.8 = f32[48,128]{1,0:T(8,128)S(1)} collective-permute-done((f32[48,128]{1,0:T(8,128)S(1)}, f32[48,128]{1,0:T(8,128)S(1)}, u32[]{:S(2)}, u32[]{:S(2)}) %collective-permute-start.8) | collective-permute-done | bytes 24608 | tf_op jit(solution)/shard_map/ppermute | solution.py:439
  116.5 0.7 fusion.1
  (12 shorter events, 0.0 us)
Async XLA Ops:
  4.1 6.0 %collective-permute-start = (bf16[4,48,256]{2,1,0:T(8,128)(2,1)}, bf16[4,48,256]{2,1,0:T(8,128)(2,1)S(1)}, u32[]{:S(2)}, u32[]{:S(2)}) collective-permute-start(bf16[4,48,256]{2,1,0:T(8,128)(2,1)} %get-tuple-element.42), channel_id=1, source_target_pairs={{0,16},{16,32},{32,48},{48,0},{64,80},{80,96},{96,112},{112,64},{1... | collective-permute-start | bytes 294920 | tf_op jit(solution)/shard_map/ppermute | solution.py:408
  4.1 6.0 %collective-permute-start.1 = (bf16[4,48,256]{2,1,0:T(8,128)(2,1)}, bf16[4,48,256]{2,1,0:T(8,128)(2,1)S(1)}, u32[]{:S(2)}, u32[]{:S(2)}) collective-permute-start(bf16[4,48,256]{2,1,0:T(8,128)(2,1)} %get-tuple-element.43), channel_id=1, source_target_pairs={{0,32},{16,48},{32,0},{48,16},{64,96},{80,112},{96,64},{112,80},{1... | collective-permute-start | bytes 294920 | tf_op jit(solution)/shard_map/ppermute | solution.py:408
  6.1 5.0 %collective-permute-start.2 = (bf16[4,48,256]{2,1,0:T(8,128)(2,1)}, bf16[4,48,256]{2,1,0:T(8,128)(2,1)S(1)}, u32[]{:S(2)}, u32[]{:S(2)}) collective-permute-start(bf16[4,48,256]{2,1,0:T(8,128)(2,1)} %get-tuple-element.44), channel_id=1, source_target_pairs={{0,48},{16,0},{32,16},{48,32},{64,112},{80,64},{96,80},{112,96},{1... | collective-permute-start | bytes 294920 | tf_op jit(solution)/shard_map/ppermute | solution.py:408
  10.1 1.0 copy-start.2
  10.1 1.0 copy-start.3
  11.1 0.6 copy-start.4
  13.5 7.6 %copy-start.8 = (bf16[80,1024]{1,0:T(8,128)(2,1)S(1)}, bf16[80,1024]{1,0:T(8,128)(2,1)}, u32[]{:S(2)}) copy-start(bf16[80,1024]{1,0:T(8,128)(2,1)} %get-tuple-element.64) | copy-start | bytes 491524
  13.5 9.1 %copy-start.11 = (bf16[4,48,256]{2,1,0:T(8,128)(2,1)S(1)}, bf16[4,48,256]{2,1,0:T(8,128)(2,1)}, u32[]{:S(2)}) copy-start(bf16[4,48,256]{2,1,0:T(8,128)(2,1)} %get-tuple-element.57) | copy-start | bytes 294916
  13.5 12.4 %copy-start.10 = (bf16[4,48,256]{2,1,0:T(8,128)(2,1)S(1)}, bf16[4,48,256]{2,1,0:T(8,128)(2,1)}, u32[]{:S(2)}) copy-start(bf16[4,48,256]{2,1,0:T(8,128)(2,1)} %get-tuple-element.58) | copy-start | bytes 294916
  13.5 16.9 %copy-start.9 = (bf16[4,48,256]{2,1,0:T(8,128)(2,1)S(1)}, bf16[4,48,256]{2,1,0:T(8,128)(2,1)}, u32[]{:S(2)}) copy-start(bf16[4,48,256]{2,1,0:T(8,128)(2,1)} %get-tuple-element.59) | copy-start | bytes 294916
  13.5 42.5 %all-to-all-start = ((bf16[16,48,1280]{2,1,0:T(8,128)(2,1)}), bf16[16,48,1280]{2,1,0:T(8,128)(2,1)S(1)}, u32[]{:S(2)}, u32[]{:S(2)}) async-start(bf16[16,48,1280]{2,1,0:T(8,128)(2,1)} %get-tuple-element.63), calls=%async_computation | async-start | bytes 3932160 | tf_op jit(solution)/shard_map/all_to_all | solution.py:414
  21.1 34.9 %collective-permute-start.6 = (bf16[80,1024]{1,0:T(8,128)(2,1)S(1)}, bf16[80,1024]{1,0:T(8,128)(2,1)S(1)}, u32[]{:S(2)}, u32[]{:S(2)}) collective-permute-start(bf16[80,1024]{1,0:T(8,128)(2,1)S(1)} %copy-done.8), channel_id=1, source_target_pairs={{0,1},{1,0},{2,3},{3,2},{4,5},{5,4},{6,7},{7,6},{8,9},{9,8},{10,11... | collective-permute-start | bytes 491528 | tf_op jit(solution)/shard_map/ppermute | solution.py:418
  22.7 19.6 %collective-permute-start.3 = (bf16[4,48,256]{2,1,0:T(8,128)(2,1)S(1)}, bf16[4,48,256]{2,1,0:T(8,128)(2,1)S(1)}, u32[]{:S(2)}, u32[]{:S(2)}) collective-permute-start(bf16[4,48,256]{2,1,0:T(8,128)(2,1)S(1)} %copy-done.11), channel_id=1, source_target_pairs={{0,64},{16,80},{32,96},{48,112},{64,128},{80,144},{96,160},{112,17... | collective-permute-start | bytes 294920 | tf_op jit(solution)/shard_map/ppermute | solution.py:416
  25.9 16.4 %collective-permute-start.4 = (bf16[4,48,256]{2,1,0:T(8,128)(2,1)S(1)}, bf16[4,48,256]{2,1,0:T(8,128)(2,1)S(1)}, u32[]{:S(2)}, u32[]{:S(2)}) collective-permute-start(bf16[4,48,256]{2,1,0:T(8,128)(2,1)S(1)} %copy-done.10), channel_id=1, source_target_pairs={{0,128},{16,144},{32,160},{48,176},{64,192},{80,208},{96,224},{112... | collective-permute-start | bytes 294920 | tf_op jit(solution)/shard_map/ppermute | solution.py:416
  30.4 11.9 %collective-permute-start.5 = (bf16[4,48,256]{2,1,0:T(8,128)(2,1)S(1)}, bf16[4,48,256]{2,1,0:T(8,128)(2,1)S(1)}, u32[]{:S(2)}, u32[]{:S(2)}) collective-permute-start(bf16[4,48,256]{2,1,0:T(8,128)(2,1)S(1)} %copy-done.9), channel_id=1, source_target_pairs={{0,192},{16,208},{32,224},{48,240},{64,0},{80,16},{96,32},{112,48}... | collective-permute-start | bytes 294920 | tf_op jit(solution)/shard_map/ppermute | solution.py:416
  42.3 0.6 copy-start.5
  42.3 0.7 copy-start.6
  42.3 0.7 copy-start.7
  56.0 27.5 %copy-start = (bf16[64,2048]{1,0:T(8,128)(2,1)S(1)}, bf16[64,2048]{1,0:T(8,128)(2,1)}, u32[]{:S(2)}) copy-start(bf16[64,2048]{1,0:T(8,128)(2,1)} %cotangent_ref.3) | copy-start | bytes 786436
  56.0 27.5 %copy-start.1 = (bf16[64]{0:T(256)(128)(2,1)S(1)}, bf16[64]{0:T(256)(128)(2,1)}, u32[]{:S(2)}) copy-start(bf16[64]{0:T(256)(128)(2,1)} %param.11) | copy-start | bytes 388
  87.0 19.5 %all-to-all-start.2 = ((bf16[32,56,128]{2,1,0:T(8,128)(2,1)}), bf16[32,56,128]{2,1,0:T(8,128)(2,1)S(1)}, u32[]{:S(2)}, u32[]{:S(2)}) async-start(bf16[32,56,128]{2,1,0:T(8,128)(2,1)} %get-tuple-element.71), calls=%async_computation.2 | async-start | bytes 917504 | tf_op jit(solution)/shard_map/all_to_all | solution.py:429
  93.0 7.8 %collective-permute-start.7 = (bf16[64,1024]{1,0:T(8,128)(2,1)S(1)}, bf16[64,1024]{1,0:T(8,128)(2,1)S(1)}, u32[]{:S(2)}, u32[]{:S(2)}) collective-permute-start(bf16[64,1024]{1,0:T(8,128)(2,1)S(1)} %get-tuple-element.69), channel_id=1, source_target_pairs={{0,1},{1,0},{2,3},{3,2},{4,5},{5,4},{6,7},{7,6},{8,9},{9,8},{10,11... | collective-permute-start | bytes 393224 | tf_op jit(solution)/shard_map/ppermute | solution.py:431
  106.6 9.9 %collective-permute-start.8 = (f32[48,128]{1,0:T(8,128)S(1)}, f32[48,128]{1,0:T(8,128)S(1)}, u32[]{:S(2)}, u32[]{:S(2)}) collective-permute-start(f32[48,128]{1,0:T(8,128)S(1)} %slice.20), channel_id=1, source_target_pairs={{144,0},{160,1},{240,2},{112,3},{176,4},{64,5},{16,6},{192,7},{80,... | collective-permute-start | bytes 73736 | tf_op jit(solution)/shard_map/ppermute | solution.py:439

commit v6 on v5

--- a/solution.py
+++ b/solution.py
@@ -62,7 +62,7 @@
             found = jnp.dot(rows_ref[...], one_hot(low, LOW), preferred_element_type=jnp.float32)
             total = jnp.zeros((columns, capacity), jnp.float32)
             for group in range(groups):
-                total = total + jnp.where(high == group, found[group * columns:(group + 1) * columns], 0.0)
+                total = jnp.where(high == group, found[group * columns:(group + 1) * columns], total)
             out_refs[k][j] = total.astype(jnp.bfloat16)
 
 
@@ -287,15 +287,9 @@
 
 
 def layer_kernel(parity_ref, own_ref, mean_ref, neigh_weight_ref, self_weight_ref, bias_ref, cotangent_ref,
-                 traded_ref, traded_bias_ref, kept_ref, sent_ref, grad_ref, total_ref, sums_ref):
-    step = pl.program_id(0)
+                 traded_ref, traded_bias_ref, kept_ref, sent_ref, grad_ref):
     odd = parity_ref[0] == 1
     hidden = cotangent_ref.shape[0]
-
-    @pl.when(step == 0)
-    def _():
-        total_ref[...] = jnp.zeros_like(total_ref)
-        sums_ref[...] = jnp.zeros_like(sums_ref)
 
     def ordered(mine, other):
         return jnp.concatenate([jnp.where(odd, other, mine), jnp.where(odd, mine, other)], axis=0)
@@ -322,51 +316,43 @@
     blank = jnp.zeros_like(first)
     for_neigh = jnp.concatenate([first, blank, second, blank], axis=0)
     for_own = jnp.concatenate([blank, first, blank, second], axis=0)
-    total_ref[...] += (
+    total = (
         lax.dot_general(mean_ref[...], for_neigh, NT, preferred_element_type=jnp.float32)
         + lax.dot_general(own_ref[...], for_own, NT, preferred_element_type=jnp.float32))
-    sums_ref[...] += lax.dot_general(ones[:SUMS], for_neigh, NT, preferred_element_type=jnp.float32)
-
-    @pl.when(step == pl.num_programs(0) - 1)
-    def _():
-        chunks, rows, width = grad_ref.shape
-        columns = rows - SUMS
-        sums = sums_ref[...]
-        high = sums.astype(jnp.bfloat16).astype(jnp.float32)
-        row = lax.broadcasted_iota(jnp.int32, sums.shape, 0)
-        extra = jnp.where(row == 0, high, jnp.where(row == 1, sums - high, 0.0))
-        for chunk in range(chunks):
-            at = slice((chunk % 2) * width, (chunk % 2 + 1) * width)
-            mine = total_ref[pl.ds((chunk // 2) * columns, columns), at]
-            grad_ref[chunk] = jnp.concatenate([mine, extra[:, at]], axis=0).astype(jnp.bfloat16)
-
-
-def layer(parity, inputs, mean, bias, cotangent, traded, shares, block=512):
+    sums = lax.dot_general(ones[:SUMS], for_neigh, NT, preferred_element_type=jnp.float32)
+    chunks, rows, width = grad_ref.shape
+    columns = rows - SUMS
+    high = sums.astype(jnp.bfloat16).astype(jnp.float32)
+    row = lax.broadcasted_iota(jnp.int32, sums.shape, 0)
+    extra = jnp.where(row == 0, high, jnp.where(row == 1, sums - high, 0.0))
+    for chunk in range(chunks):
+        at = slice((chunk % 2) * width, (chunk % 2 + 1) * width)
+        mine = total[(chunk // 2) * columns:(chunk // 2 + 1) * columns, at]
+        grad_ref[chunk] = jnp.concatenate([mine, extra[:, at]], axis=0).astype(jnp.bfloat16)
+
+
+def layer(parity, inputs, mean, bias, cotangent, traded, shares):
     features, half = mean.shape
     hidden = cotangent.shape[0]
     pair = 2 * hidden
-    blocks = half // block
     whole = lambda i, parity: (0, 0)
-    part = lambda i, parity: (0, i)
     grads = (2 * shares, features // shares + SUMS, pair)
     return pl.pallas_call(
         layer_kernel,
         grid_spec=pltpu.PrefetchScalarGridSpec(
             num_scalar_prefetch=1,
-            grid=(blocks,),
-            in_specs=[pl.BlockSpec((features, block), part),
-                      pl.BlockSpec((features, block), part),
+            grid=(1,),
+            in_specs=[pl.BlockSpec((features, half), whole),
+                      pl.BlockSpec((features, half), whole),
                       pl.BlockSpec((features, pair), lambda i, parity: (0, half // pair)),
                       pl.BlockSpec((features, pair), lambda i, parity: (0, half // pair + 1)),
                       pl.BlockSpec((1, hidden), whole),
-                      pl.BlockSpec((hidden, block), lambda i, parity: (0, i + parity[0] * blocks)),
-                      pl.BlockSpec((hidden, block), part),
+                      pl.BlockSpec((hidden, half), lambda i, parity: (0, parity[0])),
+                      pl.BlockSpec((hidden, half), whole),
                       pl.BlockSpec((EXTRA, 128), lambda i, parity: (hidden // EXTRA, 0))],
-            out_specs=(pl.BlockSpec((hidden, block), part),
-                       pl.BlockSpec((hidden, block), part),
-                       pl.BlockSpec(grads, lambda i, parity: (0, 0, 0))),
-            scratch_shapes=[pltpu.VMEM((features, 2 * pair), jnp.float32),
-                            pltpu.VMEM((SUMS, 2 * pair), jnp.float32)]),
+            out_specs=(pl.BlockSpec((hidden, half), whole),
+                       pl.BlockSpec((hidden, half), whole),
+                       pl.BlockSpec(grads, lambda i, parity: (0, 0, 0)))),
         out_shape=(jax.ShapeDtypeStruct((hidden, half), jnp.bfloat16),
                    jax.ShapeDtypeStruct((hidden, half), jnp.bfloat16),
                    jax.ShapeDtypeStruct(grads, jnp.bfloat16)),

time: 118 us -> 117 us (level)
  no operation moved by 1% of the time
where the time goes in v6:
time: 117 us; the launch traced here: 116 us
  starting transfers between devices  34.3 us (29%)
  Pallas kernels  32.7 us (28%)
  blocking collectives  27.4 us (23%)
  waiting for transfers between devices  17.8 us (15%)
  local copies, waits for them, and re-layouts  2.03 us (2%)
  other arithmetic  1.34 us (1%)
    all_to_all x1, blocking collectives, body(): mean = lax.all_to_all(mean, 'feat', split_axis=0, concat_axis=0, tiled=True)  27.4 us
    pallas_call x1, Pallas kernels, neighbor_mean(): pl.pallas_call(kernel, out_shape=jax.ShapeDtypeStruct((shares, columns, s...  13 us
    ppermute x3, starting transfers between devices, body(): lax.ppermute(far[j - 1], 'vertex', [(v, (v + j * RADIX) % partitions) for...  10.4 us
    pallas_call x1, Pallas kernels, first_tables(): pl.pallas_call(table_kernel, grid=(blocks,), out_shape=(jax.ShapeDtypeStr...  9.18 us
    all_to_all x1, starting transfers between devices, body(): lax.all_to_all(inputs, 'feat', split_axis=0, concat_axis=0, tiled=True)  7.57 us
    ppermute x1, waiting for transfers between devices, body(): other = lax.ppermute(sent, 'feat', trade)  6.26 us
    all_to_all x1, starting transfers between devices, body(): lax.all_to_all(grad, ('vertex', 'feat'), split_axis=0, concat_axis=0, til...  6.06 us
    ppermute x1, waiting for transfers between devices, body(): grad = lax.ppermute(grad[:columns], ('vertex', 'feat'), swap)  5.7 us
  transfers between devices with their start and end apart: 11, of which 4 were waited for; matrix products, arithmetic and copies ran while one was open for 1% of the time, Pallas kernels for 21%

profile of v6, /device:TPU:6, one launch (start us, length us, event | category | flops | bytes accessed | tf_op | source)
XLA Modules:
  0.0 116.4 jit_solution(1272972365528169514)
XLA Ops:
  0.6 3.5 %pick.1 = (bf16[4,48,256]{2,1,0:T(8,128)(2,1)}, bf16[4,48,256]{2,1,0:T(8,128)(2,1)}, bf16[4,48,256]{2,1,0:T(8,128)(2,1)}, bf16[4,48,256]{2,1,0:T(8,128)(2,1)}) custom-call(s32[1]{0:T(128)} %bitcast.place_ref, bf16[48,4096]{1,0:T(8,128)(2,1)} %refs_11_.1, s32[16,256]{1,0:T(8,128)} %bitcast.14, s32[1,16]{1,0:T(1,128)} %counts_ref.1), custom_call_target="tpu_custom_call" | custom-call | tf_op jit(solution)/shard_map/pick/pallas_call | solution.py:74
  4.1 0.0 collective-permute-start
  4.1 1.9 %collective-permute-start.1 = (bf16[4,48,256]{2,1,0:T(8,128)(2,1)}, bf16[4,48,256]{2,1,0:T(8,128)(2,1)S(1)}, u32[]{:S(2)}, u32[]{:S(2)}) collective-permute-start(bf16[4,48,256]{2,1,0:T(8,128)(2,1)} %get-tuple-element.43), channel_id=1, source_target_pairs={{0,32},{16,48},{32,0},{48,16},{64,96},{80,112},{96,64},{112,80},{1... | collective-permute-start | bytes 294920 | tf_op jit(solution)/shard_map/ppermute | solution.py:394
  6.1 1.4 %collective-permute-start.2 = (bf16[4,48,256]{2,1,0:T(8,128)(2,1)}, bf16[4,48,256]{2,1,0:T(8,128)(2,1)S(1)}, u32[]{:S(2)}, u32[]{:S(2)}) collective-permute-start(bf16[4,48,256]{2,1,0:T(8,128)(2,1)} %get-tuple-element.44), channel_id=1, source_target_pairs={{0,48},{16,0},{32,16},{48,32},{64,112},{80,64},{96,80},{112,96},{1... | collective-permute-start | bytes 294920 | tf_op jit(solution)/shard_map/ppermute | solution.py:394
  7.5 2.6 %pack.1 = (bf16[16,48,1280]{2,1,0:T(8,128)(2,1)}, bf16[80,1024]{1,0:T(8,128)(2,1)}) custom-call(s32[1]{0:T(128)} %bitcast.2.parity_ref, bf16[48,4096]{1,0:T(8,128)(2,1)} %refs_11_.1, bf16[48,1024]{1,0:T(8,128)(2,1)} %neigh_weight_ref.1, bf16[48,1024]{1,0:T(8,128)(2,1)} %self_weight_ref.1, bf16[64,2048]{1,0:T(8,128)(2,1)} %cotangent_ref.3, bf16[1,64]{1,0:T(2,128)(2,1)} %bitcast.12), custom_call_target="tpu_custom_call" | custom-call | tf_op jit(solution)/shard_map/pack/pallas_call | solution.py:125
  10.1 0.0 collective-permute-done.refs_1_
  10.1 0.0 collective-permute-done.1.refs_2_
  10.1 0.0 copy-start.3
  10.1 1.0 collective-permute-done.2.refs_3_
  11.1 0.0 copy-done.2
  11.1 0.0 copy-done.3
  11.1 0.6 copy-done.4
  11.7 1.8 %regroup.1 = (bf16[4,48,256]{2,1,0:T(8,128)(2,1)}, bf16[4,48,256]{2,1,0:T(8,128)(2,1)}, bf16[4,48,256]{2,1,0:T(8,128)(2,1)}) custom-call(bf16[4,48,256]{2,1,0:T(8,128)(2,1)} %get-tuple-element.38.refs_0_, bf16[4,48,256]{2,1,0:T(8,128)(2,1)} %copy-done.2, bf16[4,48,256]{2,1,0:T(8,128)(2,1)} %copy-done.3, bf16[4,48,256]{2,1,0:T(8,128)(2,1)} %copy-done.4), custom_call_target="tpu_custom_call" | custom-call | tf_op jit(solution)/shard_map/regroup/pallas_call | solution.py:94
  13.5 0.0 copy-start.9
  13.5 7.6 %all-to-all-start = ((bf16[16,48,1280]{2,1,0:T(8,128)(2,1)}), bf16[16,48,1280]{2,1,0:T(8,128)(2,1)S(1)}, u32[]{:S(2)}, u32[]{:S(2)}) async-start(bf16[16,48,1280]{2,1,0:T(8,128)(2,1)} %get-tuple-element.63), calls=%async_computation | async-start | bytes 3932160 | tf_op jit(solution)/shard_map/all_to_all | solution.py:400
  21.1 0.0 copy-done.8
  21.1 1.6 %collective-permute-start.6 = (bf16[80,1024]{1,0:T(8,128)(2,1)S(1)}, bf16[80,1024]{1,0:T(8,128)(2,1)S(1)}, u32[]{:S(2)}, u32[]{:S(2)}) collective-permute-start(bf16[80,1024]{1,0:T(8,128)(2,1)S(1)} %copy-done.8), channel_id=1, source_target_pairs={{0,1},{1,0},{2,3},{3,2},{4,5},{5,4},{6,7},{7,6},{8,9},{9,8},{10,11... | collective-permute-start | bytes 491528 | tf_op jit(solution)/shard_map/ppermute | solution.py:404
  22.7 0.0 copy-done.11
  22.7 3.3 %collective-permute-start.3 = (bf16[4,48,256]{2,1,0:T(8,128)(2,1)S(1)}, bf16[4,48,256]{2,1,0:T(8,128)(2,1)S(1)}, u32[]{:S(2)}, u32[]{:S(2)}) collective-permute-start(bf16[4,48,256]{2,1,0:T(8,128)(2,1)S(1)} %copy-done.11), channel_id=1, source_target_pairs={{0,64},{16,80},{32,96},{48,112},{64,128},{80,144},{96,160},{112,17... | collective-permute-start | bytes 294920 | tf_op jit(solution)/shard_map/ppermute | solution.py:402
  25.9 0.0 copy-done.10
  25.9 4.5 %collective-permute-start.4 = (bf16[4,48,256]{2,1,0:T(8,128)(2,1)S(1)}, bf16[4,48,256]{2,1,0:T(8,128)(2,1)S(1)}, u32[]{:S(2)}, u32[]{:S(2)}) collective-permute-start(bf16[4,48,256]{2,1,0:T(8,128)(2,1)S(1)} %copy-done.10), channel_id=1, source_target_pairs={{0,128},{16,144},{32,160},{48,176},{64,192},{80,208},{96,224},{112... | collective-permute-start | bytes 294920 | tf_op jit(solution)/shard_map/ppermute | solution.py:402
  30.4 2.7 %collective-permute-start.5 = (bf16[4,48,256]{2,1,0:T(8,128)(2,1)S(1)}, bf16[4,48,256]{2,1,0:T(8,128)(2,1)S(1)}, u32[]{:S(2)}, u32[]{:S(2)}) collective-permute-start(bf16[4,48,256]{2,1,0:T(8,128)(2,1)S(1)} %copy-done.9), channel_id=1, source_target_pairs={{0,192},{16,208},{32,224},{48,240},{64,0},{80,16},{96,32},{112,48}... | collective-permute-start | bytes 294920 | tf_op jit(solution)/shard_map/ppermute | solution.py:402
  33.1 9.2 %first_tables.1 = (bf16[1280,4096]{1,0:T(8,128)(2,1)}, f32[1280,48]{1,0:T(8,128)}, f32[256,256]{1,0:T(8,128)}, f32[256,256]{1,0:T(8,128)}) custom-call(s32[25,2048]{1,0:T(8,128)} %refs_10_.1, bf16[48,4096]{1,0:T(8,128)(2,1)} %refs_11_.1), custom_call_target="tpu_custom_call" | custom-call | tf_op jit(solution)/shard_map/first_tables/pallas_call | solution.py:200
  42.3 0.0 collective-permute-done.3.refs_4_
  42.3 0.0 collective-permute-done.4.refs_5_
  42.3 0.0 copy-start.6
  42.3 0.0 collective-permute-done.5.refs_6_
  42.3 0.6 copy-done.5
  42.9 0.0 copy-done.6
  43.0 0.0 copy-done.7
  43.0 13.0 %mean.1 = bf16[16,48,1024]{2,1,0:T(8,128)(2,1)} custom-call(s32[1]{0:T(128)} %bitcast.place_ref, bf16[1280,4096]{1,0:T(8,128)(2,1)} %get-tuple-element.56.remote_ref, bf16[4,48,256]{2,1,0:T(8,128)(2,1)} %get-tuple-element.38.refs_0_, bf16[4,48,256]{2,1,0:T(8,128)(2,1)} %copy-done.2, bf16[4,48,256]{2,1,0:T(8,128)(2,1)} %copy-done.3, ...), custom_call_target="tpu_custom_call" | custom-call | tf_op jit(solution)/shard_map/mean/pallas_call | solution.py:273
  56.0 0.0 copy-start
  56.0 0.0 copy-start.1
  56.0 0.0 collective-permute-done.6.traded_ref.traded_bias_ref
  56.0 0.0 all-to-all-done
  56.1 27.4 %all_to_all.15 = bf16[16,48,1024]{2,1,0:T(8,128)(2,1)S(1)} all-to-all(bf16[16,48,1024]{2,1,0:T(8,128)(2,1)} %mean.1), channel_id=1, replica_groups=mesh['vertex'=16,'feat'=16] {'feat'}, dimensions={0} | all-to-all | bytes 3145728 | tf_op jit(solution)/shard_map/all_to_all | solution.py:409
  83.5 0.0 copy-done.1
  83.5 2.7 %layer.1 = (bf16[64,1024]{1,0:T(8,128)(2,1)S(1)}, bf16[64,1024]{1,0:T(8,128)(2,1)S(1)}, bf16[32,56,128]{2,1,0:T(8,128)(2,1)}) custom-call(s32[1]{0:T(128)} %bitcast.2.parity_ref, bf16[768,1280]{1,0:T(8,128)(2,1)S(1)} %bitcast.8, bf16[768,1024]{1,0:T(8,128)(2,1)S(1)} %bitcast.11, bf16[768,1280]{1,0:T(8,128)(2,1)S(1)} %bitcast.9, ...), custom_call_target="tpu_custom_call" | custom-call | tf_op jit(solution)/shard_map/layer/pallas_call | solution.py:340
  86.1 6.1 %all-to-all-start.2 = ((bf16[32,56,128]{2,1,0:T(8,128)(2,1)}), bf16[32,56,128]{2,1,0:T(8,128)(2,1)S(1)}, u32[]{:S(2)}, u32[]{:S(2)}) async-start(bf16[32,56,128]{2,1,0:T(8,128)(2,1)} %get-tuple-element.71), calls=%async_computation.2 | async-start | bytes 917504 | tf_op jit(solution)/shard_map/all_to_all | solution.py:415
  92.2 1.6 %collective-permute-start.7 = (bf16[64,1024]{1,0:T(8,128)(2,1)S(1)}, bf16[64,1024]{1,0:T(8,128)(2,1)S(1)}, u32[]{:S(2)}, u32[]{:S(2)}) collective-permute-start(bf16[64,1024]{1,0:T(8,128)(2,1)S(1)} %get-tuple-element.69), channel_id=1, source_target_pairs={{0,1},{1,0},{2,3},{3,2},{4,5},{5,4},{6,7},{7,6},{8,9},{9,8},{10,11... | collective-permute-start | bytes 393224 | tf_op jit(solution)/shard_map/ppermute | solution.py:417
  93.8 6.3 %collective-permute-done.7 = bf16[64,1024]{1,0:T(8,128)(2,1)S(1)} collective-permute-done((bf16[64,1024]{1,0:T(8,128)(2,1)S(1)}, bf16[64,1024]{1,0:T(8,128)(2,1)S(1)}, u32[]{:S(2)}, u32[]{:S(2)}) %collective-permute-start.7) | collective-permute-done | bytes 131104 | tf_op jit(solution)/shard_map/ppermute | solution.py:417
  100.1 0.7 pad_maximum_fusion
  100.8 4.9 %all-to-all-done.2 = bf16[32,56,128]{2,1,0:T(8,128)(2,1)S(1)} async-done(((bf16[32,56,128]{2,1,0:T(8,128)(2,1)}), bf16[32,56,128]{2,1,0:T(8,128)(2,1)S(1)}, u32[]{:S(2)}, u32[]{:S(2)}) %all-to-all-start.2) | async-done | bytes 458784 | tf_op jit(solution)/shard_map/all_to_all | solution.py:415
  105.6 0.1 convert_reduce_fusion
  105.8 3.7 %collective-permute-start.8 = (f32[48,128]{1,0:T(8,128)S(1)}, f32[48,128]{1,0:T(8,128)S(1)}, u32[]{:S(2)}, u32[]{:S(2)}) collective-permute-start(f32[48,128]{1,0:T(8,128)S(1)} %slice.20), channel_id=1, source_target_pairs={{144,0},{160,1},{240,2},{112,3},{176,4},{64,5},{16,6},{192,7},{80,... | collective-permute-start | bytes 73736 | tf_op jit(solution)/shard_map/ppermute | solution.py:425
  109.5 0.5 fusion
  110.0 5.7 %collective-permute-done.8 = f32[48,128]{1,0:T(8,128)S(1)} collective-permute-done((f32[48,128]{1,0:T(8,128)S(1)}, f32[48,128]{1,0:T(8,128)S(1)}, u32[]{:S(2)}, u32[]{:S(2)}) %collective-permute-start.8) | collective-permute-done | bytes 24608 | tf_op jit(solution)/shard_map/ppermute | solution.py:425
  115.7 0.7 fusion.1
  (12 shorter events, 0.0 us)
Async XLA Ops:
  4.1 6.0 %collective-permute-start = (bf16[4,48,256]{2,1,0:T(8,128)(2,1)}, bf16[4,48,256]{2,1,0:T(8,128)(2,1)S(1)}, u32[]{:S(2)}, u32[]{:S(2)}) collective-permute-start(bf16[4,48,256]{2,1,0:T(8,128)(2,1)} %get-tuple-element.42), channel_id=1, source_target_pairs={{0,16},{16,32},{32,48},{48,0},{64,80},{80,96},{96,112},{112,64},{1... | collective-permute-start | bytes 294920 | tf_op jit(solution)/shard_map/ppermute | solution.py:394
  4.1 6.0 %collective-permute-start.1 = (bf16[4,48,256]{2,1,0:T(8,128)(2,1)}, bf16[4,48,256]{2,1,0:T(8,128)(2,1)S(1)}, u32[]{:S(2)}, u32[]{:S(2)}) collective-permute-start(bf16[4,48,256]{2,1,0:T(8,128)(2,1)} %get-tuple-element.43), channel_id=1, source_target_pairs={{0,32},{16,48},{32,0},{48,16},{64,96},{80,112},{96,64},{112,80},{1... | collective-permute-start | bytes 294920 | tf_op jit(solution)/shard_map/ppermute | solution.py:394
  6.1 5.0 %collective-permute-start.2 = (bf16[4,48,256]{2,1,0:T(8,128)(2,1)}, bf16[4,48,256]{2,1,0:T(8,128)(2,1)S(1)}, u32[]{:S(2)}, u32[]{:S(2)}) collective-permute-start(bf16[4,48,256]{2,1,0:T(8,128)(2,1)} %get-tuple-element.44), channel_id=1, source_target_pairs={{0,48},{16,0},{32,16},{48,32},{64,112},{80,64},{96,80},{112,96},{1... | collective-permute-start | bytes 294920 | tf_op jit(solution)/shard_map/ppermute | solution.py:394
  10.1 1.0 copy-start.2
  10.1 1.0 copy-start.3
  11.1 0.6 copy-start.4
  13.5 7.6 %copy-start.8 = (bf16[80,1024]{1,0:T(8,128)(2,1)S(1)}, bf16[80,1024]{1,0:T(8,128)(2,1)}, u32[]{:S(2)}) copy-start(bf16[80,1024]{1,0:T(8,128)(2,1)} %get-tuple-element.64) | copy-start | bytes 491524
  13.5 9.1 %copy-start.11 = (bf16[4,48,256]{2,1,0:T(8,128)(2,1)S(1)}, bf16[4,48,256]{2,1,0:T(8,128)(2,1)}, u32[]{:S(2)}) copy-start(bf16[4,48,256]{2,1,0:T(8,128)(2,1)} %get-tuple-element.57) | copy-start | bytes 294916
  13.5 12.4 %copy-start.10 = (bf16[4,48,256]{2,1,0:T(8,128)(2,1)S(1)}, bf16[4,48,256]{2,1,0:T(8,128)(2,1)}, u32[]{:S(2)}) copy-start(bf16[4,48,256]{2,1,0:T(8,128)(2,1)} %get-tuple-element.58) | copy-start | bytes 294916
  13.5 16.9 %copy-start.9 = (bf16[4,48,256]{2,1,0:T(8,128)(2,1)S(1)}, bf16[4,48,256]{2,1,0:T(8,128)(2,1)}, u32[]{:S(2)}) copy-start(bf16[4,48,256]{2,1,0:T(8,128)(2,1)} %get-tuple-element.59) | copy-start | bytes 294916
  13.5 42.5 %all-to-all-start = ((bf16[16,48,1280]{2,1,0:T(8,128)(2,1)}), bf16[16,48,1280]{2,1,0:T(8,128)(2,1)S(1)}, u32[]{:S(2)}, u32[]{:S(2)}) async-start(bf16[16,48,1280]{2,1,0:T(8,128)(2,1)} %get-tuple-element.63), calls=%async_computation | async-start | bytes 3932160 | tf_op jit(solution)/shard_map/all_to_all | solution.py:400
  21.1 34.9 %collective-permute-start.6 = (bf16[80,1024]{1,0:T(8,128)(2,1)S(1)}, bf16[80,1024]{1,0:T(8,128)(2,1)S(1)}, u32[]{:S(2)}, u32[]{:S(2)}) collective-permute-start(bf16[80,1024]{1,0:T(8,128)(2,1)S(1)} %copy-done.8), channel_id=1, source_target_pairs={{0,1},{1,0},{2,3},{3,2},{4,5},{5,4},{6,7},{7,6},{8,9},{9,8},{10,11... | collective-permute-start | bytes 491528 | tf_op jit(solution)/shard_map/ppermute | solution.py:404
  22.7 19.6 %collective-permute-start.3 = (bf16[4,48,256]{2,1,0:T(8,128)(2,1)S(1)}, bf16[4,48,256]{2,1,0:T(8,128)(2,1)S(1)}, u32[]{:S(2)}, u32[]{:S(2)}) collective-permute-start(bf16[4,48,256]{2,1,0:T(8,128)(2,1)S(1)} %copy-done.11), channel_id=1, source_target_pairs={{0,64},{16,80},{32,96},{48,112},{64,128},{80,144},{96,160},{112,17... | collective-permute-start | bytes 294920 | tf_op jit(solution)/shard_map/ppermute | solution.py:402
  25.9 16.4 %collective-permute-start.4 = (bf16[4,48,256]{2,1,0:T(8,128)(2,1)S(1)}, bf16[4,48,256]{2,1,0:T(8,128)(2,1)S(1)}, u32[]{:S(2)}, u32[]{:S(2)}) collective-permute-start(bf16[4,48,256]{2,1,0:T(8,128)(2,1)S(1)} %copy-done.10), channel_id=1, source_target_pairs={{0,128},{16,144},{32,160},{48,176},{64,192},{80,208},{96,224},{112... | collective-permute-start | bytes 294920 | tf_op jit(solution)/shard_map/ppermute | solution.py:402
  30.4 11.9 %collective-permute-start.5 = (bf16[4,48,256]{2,1,0:T(8,128)(2,1)S(1)}, bf16[4,48,256]{2,1,0:T(8,128)(2,1)S(1)}, u32[]{:S(2)}, u32[]{:S(2)}) collective-permute-start(bf16[4,48,256]{2,1,0:T(8,128)(2,1)S(1)} %copy-done.9), channel_id=1, source_target_pairs={{0,192},{16,208},{32,224},{48,240},{64,0},{80,16},{96,32},{112,48}... | collective-permute-start | bytes 294920 | tf_op jit(solution)/shard_map/ppermute | solution.py:402
  42.3 0.6 copy-start.5
  42.3 0.7 copy-start.6
  42.3 0.7 copy-start.7
  56.0 27.5 %copy-start = (bf16[64,2048]{1,0:T(8,128)(2,1)S(1)}, bf16[64,2048]{1,0:T(8,128)(2,1)}, u32[]{:S(2)}) copy-start(bf16[64,2048]{1,0:T(8,128)(2,1)} %cotangent_ref.3) | copy-start | bytes 786436
  56.0 27.4 %copy-start.1 = (bf16[64]{0:T(256)(128)(2,1)S(1)}, bf16[64]{0:T(256)(128)(2,1)}, u32[]{:S(2)}) copy-start(bf16[64]{0:T(256)(128)(2,1)} %param.11) | copy-start | bytes 388
  86.1 19.5 %all-to-all-start.2 = ((bf16[32,56,128]{2,1,0:T(8,128)(2,1)}), bf16[32,56,128]{2,1,0:T(8,128)(2,1)S(1)}, u32[]{:S(2)}, u32[]{:S(2)}) async-start(bf16[32,56,128]{2,1,0:T(8,128)(2,1)} %get-tuple-element.71), calls=%async_computation.2 | async-start | bytes 917504 | tf_op jit(solution)/shard_map/all_to_all | solution.py:415
  92.2 7.8 %collective-permute-start.7 = (bf16[64,1024]{1,0:T(8,128)(2,1)S(1)}, bf16[64,1024]{1,0:T(8,128)(2,1)S(1)}, u32[]{:S(2)}, u32[]{:S(2)}) collective-permute-start(bf16[64,1024]{1,0:T(8,128)(2,1)S(1)} %get-tuple-element.69), channel_id=1, source_target_pairs={{0,1},{1,0},{2,3},{3,2},{4,5},{5,4},{6,7},{7,6},{8,9},{9,8},{10,11... | collective-permute-start | bytes 393224 | tf_op jit(solution)/shard_map/ppermute | solution.py:417
  105.8 9.9 %collective-permute-start.8 = (f32[48,128]{1,0:T(8,128)S(1)}, f32[48,128]{1,0:T(8,128)S(1)}, u32[]{:S(2)}, u32[]{:S(2)}) collective-permute-start(f32[48,128]{1,0:T(8,128)S(1)} %slice.20), channel_id=1, source_target_pairs={{144,0},{160,1},{240,2},{112,3},{176,4},{64,5},{16,6},{192,7},{80,... | collective-permute-start | bytes 73736 | tf_op jit(solution)/shard_map/ppermute | solution.py:425

commit v7 on v6

--- a/solution.py
+++ b/solution.py
@@ -11,7 +11,7 @@
 LOW = 256
 ONES = jnp.float8_e4m3fn
 UNROLL = 16
-FIRST = 5
+FIRST = 6
 RADIX = 4
 PAD = 32
 GROUP = 8
@@ -398,7 +398,7 @@
     far = list(regroup(near))
     far, early, traded, inputs = lax.optimization_barrier((far, neighbors, traded, inputs))
     inputs = lax.all_to_all(inputs, "feat", split_axis=0, concat_axis=0, tiled=True)
-    for j in range(1, RADIX):
+    for j in (2, 1, 3):
         far[j - 1] = lax.ppermute(
             far[j - 1], "vertex", [(v, (v + j * RADIX) % partitions) for v in range(partitions)])
     traded = lax.ppermute(traded, "feat", trade)

time: 117 us -> 116 us (level)
  the two profiles are of different devices: /device:TPU:6 before, /device:TPU:36 now
where the time goes in v7:
time: 116 us; the launch traced here: 114 us
  starting transfers between devices  33.5 us (29%)
  Pallas kernels  32.7 us (28%)
  blocking collectives  27.1 us (23%)
  waiting for transfers between devices  16.6 us (14%)
  local copies, waits for them, and re-layouts  2.08 us (2%)
  other arithmetic  1.34 us (1%)
    all_to_all x1, blocking collectives, body(): mean = lax.all_to_all(mean, 'feat', split_axis=0, concat_axis=0, tiled=True)  27.1 us
    pallas_call x1, Pallas kernels, neighbor_mean(): pl.pallas_call(kernel, out_shape=jax.ShapeDtypeStruct((shares, columns, s...  11.7 us
    pallas_call x1, Pallas kernels, first_tables(): pl.pallas_call(table_kernel, grid=(blocks,), out_shape=(jax.ShapeDtypeStr...  10.6 us
    ppermute x3, starting transfers between devices, body(): lax.ppermute(far[j - 1], 'vertex', [(v, (v + j * RADIX) % partitions) for...  10.6 us
    all_to_all x1, starting transfers between devices, body(): lax.all_to_all(inputs, 'feat', split_axis=0, concat_axis=0, tiled=True)  7.6 us
    all_to_all x1, starting transfers between devices, body(): lax.all_to_all(grad, ('vertex', 'feat'), split_axis=0, concat_axis=0, til...  7.17 us
    ppermute x1, waiting for transfers between devices, body(): other = lax.ppermute(sent, 'feat', trade)  6.93 us
    ppermute x1, waiting for transfers between devices, body(): grad = lax.ppermute(grad[:columns], ('vertex', 'feat'), swap)  5.12 us
  transfers between devices with their start and end apart: 11, of which 5 were waited for; matrix products, arithmetic and copies ran while one was open for 1% of the time, Pallas kernels for 22%

profile of v7, /device:TPU:36, one launch (start us, length us, event | category | flops | bytes accessed | tf_op | source)
XLA Modules:
  0.0 114.2 jit_solution(12491017929624799572)
XLA Ops:
  0.6 3.5 %pick.1 = (bf16[4,48,256]{2,1,0:T(8,128)(2,1)}, bf16[4,48,256]{2,1,0:T(8,128)(2,1)}, bf16[4,48,256]{2,1,0:T(8,128)(2,1)}, bf16[4,48,256]{2,1,0:T(8,128)(2,1)}) custom-call(s32[1]{0:T(128)} %bitcast.place_ref, bf16[48,4096]{1,0:T(8,128)(2,1)} %refs_11_.1, s32[16,256]{1,0:T(8,128)} %bitcast.14, s32[1,16]{1,0:T(1,128)} %counts_ref.1), custom_call_target="tpu_custom_call" | custom-call | tf_op jit(solution)/shard_map/pick/pallas_call | solution.py:74
  4.1 0.0 collective-permute-start
  4.1 0.1 collective-permute-start.1
  4.3 1.6 %collective-permute-start.2 = (bf16[4,48,256]{2,1,0:T(8,128)(2,1)}, bf16[4,48,256]{2,1,0:T(8,128)(2,1)S(1)}, u32[]{:S(2)}, u32[]{:S(2)}) collective-permute-start(bf16[4,48,256]{2,1,0:T(8,128)(2,1)} %get-tuple-element.44), channel_id=1, source_target_pairs={{0,48},{16,0},{32,16},{48,32},{64,112},{80,64},{96,80},{112,96},{1... | collective-permute-start | bytes 294920 | tf_op jit(solution)/shard_map/ppermute | solution.py:394
  5.9 2.6 %pack.1 = (bf16[16,48,1280]{2,1,0:T(8,128)(2,1)}, bf16[80,1024]{1,0:T(8,128)(2,1)}) custom-call(s32[1]{0:T(128)} %bitcast.2.parity_ref, bf16[48,4096]{1,0:T(8,128)(2,1)} %refs_11_.1, bf16[48,1024]{1,0:T(8,128)(2,1)} %neigh_weight_ref.1, bf16[48,1024]{1,0:T(8,128)(2,1)} %self_weight_ref.1, bf16[64,2048]{1,0:T(8,128)(2,1)} %cotangent_ref.3, bf16[1,64]{1,0:T(2,128)(2,1)} %bitcast.12), custom_call_target="tpu_custom_call" | custom-call | tf_op jit(solution)/shard_map/pack/pallas_call | solution.py:125
  8.5 0.4 collective-permute-done.refs_1_
  8.9 1.1 collective-permute-done.1.refs_2_
  10.0 0.0 collective-permute-done.2.refs_3_
  10.0 0.0 copy-done.2
  10.0 0.6 copy-done.3
  10.6 0.1 copy-done.4
  10.7 1.8 %regroup.1 = (bf16[4,48,256]{2,1,0:T(8,128)(2,1)}, bf16[4,48,256]{2,1,0:T(8,128)(2,1)}, bf16[4,48,256]{2,1,0:T(8,128)(2,1)}) custom-call(bf16[4,48,256]{2,1,0:T(8,128)(2,1)} %get-tuple-element.38.refs_0_, bf16[4,48,256]{2,1,0:T(8,128)(2,1)} %copy-done.2, bf16[4,48,256]{2,1,0:T(8,128)(2,1)} %copy-done.3, bf16[4,48,256]{2,1,0:T(8,128)(2,1)} %copy-done.4), custom_call_target="tpu_custom_call" | custom-call | tf_op jit(solution)/shard_map/regroup/pallas_call | solution.py:94
  12.4 0.0 copy-start.9
  12.4 7.6 %all-to-all-start = ((bf16[16,48,1280]{2,1,0:T(8,128)(2,1)}), bf16[16,48,1280]{2,1,0:T(8,128)(2,1)S(1)}, u32[]{:S(2)}, u32[]{:S(2)}) async-start(bf16[16,48,1280]{2,1,0:T(8,128)(2,1)} %get-tuple-element.63), calls=%async_computation | async-start | bytes 3932160 | tf_op jit(solution)/shard_map/all_to_all | solution.py:400
  20.0 0.0 copy-done.8
  20.0 1.6 %collective-permute-start.6 = (bf16[80,1024]{1,0:T(8,128)(2,1)S(1)}, bf16[80,1024]{1,0:T(8,128)(2,1)S(1)}, u32[]{:S(2)}, u32[]{:S(2)}) collective-permute-start(bf16[80,1024]{1,0:T(8,128)(2,1)S(1)} %copy-done.8), channel_id=1, source_target_pairs={{0,1},{1,0},{2,3},{3,2},{4,5},{5,4},{6,7},{7,6},{8,9},{9,8},{10,11... | collective-permute-start | bytes 491528 | tf_op jit(solution)/shard_map/ppermute | solution.py:404
  21.6 0.0 copy-done.11
  21.6 3.3 %collective-permute-start.3 = (bf16[4,48,256]{2,1,0:T(8,128)(2,1)S(1)}, bf16[4,48,256]{2,1,0:T(8,128)(2,1)S(1)}, u32[]{:S(2)}, u32[]{:S(2)}) collective-permute-start(bf16[4,48,256]{2,1,0:T(8,128)(2,1)S(1)} %copy-done.11), channel_id=1, source_target_pairs={{0,64},{16,80},{32,96},{48,112},{64,128},{80,144},{96,160},{112,17... | collective-permute-start | bytes 294920 | tf_op jit(solution)/shard_map/ppermute | solution.py:402
  24.9 0.0 copy-done.10
  24.9 4.6 %collective-permute-start.4 = (bf16[4,48,256]{2,1,0:T(8,128)(2,1)S(1)}, bf16[4,48,256]{2,1,0:T(8,128)(2,1)S(1)}, u32[]{:S(2)}, u32[]{:S(2)}) collective-permute-start(bf16[4,48,256]{2,1,0:T(8,128)(2,1)S(1)} %copy-done.10), channel_id=1, source_target_pairs={{0,128},{16,144},{32,160},{48,176},{64,192},{80,208},{96,224},{112... | collective-permute-start | bytes 294920 | tf_op jit(solution)/shard_map/ppermute | solution.py:402
  29.5 0.0 copy-done.9
  29.5 2.7 %collective-permute-start.5 = (bf16[4,48,256]{2,1,0:T(8,128)(2,1)S(1)}, bf16[4,48,256]{2,1,0:T(8,128)(2,1)S(1)}, u32[]{:S(2)}, u32[]{:S(2)}) collective-permute-start(bf16[4,48,256]{2,1,0:T(8,128)(2,1)S(1)} %copy-done.9), channel_id=1, source_target_pairs={{0,192},{16,208},{32,224},{48,240},{64,0},{80,16},{96,32},{112,48}... | collective-permute-start | bytes 294920 | tf_op jit(solution)/shard_map/ppermute | solution.py:402
  32.2 10.6 %first_tables.1 = (bf16[1536,4096]{1,0:T(8,128)(2,1)}, f32[1536,48]{1,0:T(8,128)}, f32[256,256]{1,0:T(8,128)}, f32[256,256]{1,0:T(8,128)}) custom-call(s32[25,2048]{1,0:T(8,128)} %refs_10_.1, bf16[48,4096]{1,0:T(8,128)(2,1)} %refs_11_.1), custom_call_target="tpu_custom_call" | custom-call | tf_op jit(solution)/shard_map/first_tables/pallas_call | solution.py:200
  42.8 0.0 collective-permute-done.3.refs_4_
  42.8 0.0 collective-permute-done.4.refs_5_
  42.8 0.0 copy-start.6
  42.8 0.0 collective-permute-done.5.refs_6_
  42.8 0.6 copy-done.5
  43.4 0.1 copy-done.6
  43.5 0.1 copy-done.7
  43.5 11.7 %mean.1 = bf16[16,48,1024]{2,1,0:T(8,128)(2,1)} custom-call(s32[1]{0:T(128)} %bitcast.place_ref, bf16[1536,4096]{1,0:T(8,128)(2,1)} %get-tuple-element.56.remote_ref, bf16[4,48,256]{2,1,0:T(8,128)(2,1)} %get-tuple-element.38.refs_0_, bf16[4,48,256]{2,1,0:T(8,128)(2,1)} %copy-done.2, bf16[4,48,256]{2,1,0:T(8,128)(2,1)} %copy-done.3, ...), custom_call_target="tpu_custom_call" | custom-call | tf_op jit(solution)/shard_map/mean/pallas_call | solution.py:273
  55.2 0.0 copy-start
  55.2 0.0 copy-start.1
  55.2 0.0 collective-permute-done.6.traded_ref.traded_bias_ref
  55.2 0.0 all-to-all-done
  55.2 27.1 %all_to_all.15 = bf16[16,48,1024]{2,1,0:T(8,128)(2,1)S(1)} all-to-all(bf16[16,48,1024]{2,1,0:T(8,128)(2,1)} %mean.1), channel_id=1, replica_groups=mesh['vertex'=16,'feat'=16] {'feat'}, dimensions={0} | all-to-all | bytes 3145728 | tf_op jit(solution)/shard_map/all_to_all | solution.py:409
  82.4 0.0 copy-done.1
  82.4 2.7 %layer.1 = (bf16[64,1024]{1,0:T(8,128)(2,1)S(1)}, bf16[64,1024]{1,0:T(8,128)(2,1)S(1)}, bf16[32,56,128]{2,1,0:T(8,128)(2,1)}) custom-call(s32[1]{0:T(128)} %bitcast.2.parity_ref, bf16[768,1280]{1,0:T(8,128)(2,1)S(1)} %bitcast.8, bf16[768,1024]{1,0:T(8,128)(2,1)S(1)} %bitcast.11, bf16[768,1280]{1,0:T(8,128)(2,1)S(1)} %bitcast.9, ...), custom_call_target="tpu_custom_call" | custom-call | tf_op jit(solution)/shard_map/layer/pallas_call | solution.py:340
  85.0 7.2 %all-to-all-start.2 = ((bf16[32,56,128]{2,1,0:T(8,128)(2,1)}), bf16[32,56,128]{2,1,0:T(8,128)(2,1)S(1)}, u32[]{:S(2)}, u32[]{:S(2)}) async-start(bf16[32,56,128]{2,1,0:T(8,128)(2,1)} %get-tuple-element.71), calls=%async_computation.2 | async-start | bytes 917504 | tf_op jit(solution)/shard_map/all_to_all | solution.py:415
  92.2 1.5 %collective-permute-start.7 = (bf16[64,1024]{1,0:T(8,128)(2,1)S(1)}, bf16[64,1024]{1,0:T(8,128)(2,1)S(1)}, u32[]{:S(2)}, u32[]{:S(2)}) collective-permute-start(bf16[64,1024]{1,0:T(8,128)(2,1)S(1)} %get-tuple-element.69), channel_id=1, source_target_pairs={{0,1},{1,0},{2,3},{3,2},{4,5},{5,4},{6,7},{7,6},{8,9},{9,8},{10,11... | collective-permute-start | bytes 393224 | tf_op jit(solution)/shard_map/ppermute | solution.py:417
  93.7 6.9 %collective-permute-done.7 = bf16[64,1024]{1,0:T(8,128)(2,1)S(1)} collective-permute-done((bf16[64,1024]{1,0:T(8,128)(2,1)S(1)}, bf16[64,1024]{1,0:T(8,128)(2,1)S(1)}, u32[]{:S(2)}, u32[]{:S(2)}) %collective-permute-start.7) | collective-permute-done | bytes 131104 | tf_op jit(solution)/shard_map/ppermute | solution.py:417
  100.6 0.7 pad_maximum_fusion
  101.4 3.1 %all-to-all-done.2 = bf16[32,56,128]{2,1,0:T(8,128)(2,1)S(1)} async-done(((bf16[32,56,128]{2,1,0:T(8,128)(2,1)}), bf16[32,56,128]{2,1,0:T(8,128)(2,1)S(1)}, u32[]{:S(2)}, u32[]{:S(2)}) %all-to-all-start.2) | async-done | bytes 458784 | tf_op jit(solution)/shard_map/all_to_all | solution.py:415
  104.4 0.1 convert_reduce_fusion
  104.5 3.4 %collective-permute-start.8 = (f32[48,128]{1,0:T(8,128)S(1)}, f32[48,128]{1,0:T(8,128)S(1)}, u32[]{:S(2)}, u32[]{:S(2)}) collective-permute-start(f32[48,128]{1,0:T(8,128)S(1)} %slice.20), channel_id=1, source_target_pairs={{144,0},{160,1},{240,2},{112,3},{176,4},{64,5},{16,6},{192,7},{80,... | collective-permute-start | bytes 73736 | tf_op jit(solution)/shard_map/ppermute | solution.py:425
  107.9 0.5 fusion
  108.4 5.1 %collective-permute-done.8 = f32[48,128]{1,0:T(8,128)S(1)} collective-permute-done((f32[48,128]{1,0:T(8,128)S(1)}, f32[48,128]{1,0:T(8,128)S(1)}, u32[]{:S(2)}, u32[]{:S(2)}) %collective-permute-start.8) | collective-permute-done | bytes 24608 | tf_op jit(solution)/shard_map/ppermute | solution.py:425
  113.5 0.7 fusion.1
  (12 shorter events, 0.0 us)
Async XLA Ops:
  4.1 4.8 %collective-permute-start = (bf16[4,48,256]{2,1,0:T(8,128)(2,1)}, bf16[4,48,256]{2,1,0:T(8,128)(2,1)S(1)}, u32[]{:S(2)}, u32[]{:S(2)}) collective-permute-start(bf16[4,48,256]{2,1,0:T(8,128)(2,1)} %get-tuple-element.42), channel_id=1, source_target_pairs={{0,16},{16,32},{32,48},{48,0},{64,80},{80,96},{96,112},{112,64},{1... | collective-permute-start | bytes 294920 | tf_op jit(solution)/shard_map/ppermute | solution.py:394
  4.1 5.9 %collective-permute-start.1 = (bf16[4,48,256]{2,1,0:T(8,128)(2,1)}, bf16[4,48,256]{2,1,0:T(8,128)(2,1)S(1)}, u32[]{:S(2)}, u32[]{:S(2)}) collective-permute-start(bf16[4,48,256]{2,1,0:T(8,128)(2,1)} %get-tuple-element.43), channel_id=1, source_target_pairs={{0,32},{16,48},{32,0},{48,16},{64,96},{80,112},{96,64},{112,80},{1... | collective-permute-start | bytes 294920 | tf_op jit(solution)/shard_map/ppermute | solution.py:394
  4.3 5.7 %collective-permute-start.2 = (bf16[4,48,256]{2,1,0:T(8,128)(2,1)}, bf16[4,48,256]{2,1,0:T(8,128)(2,1)S(1)}, u32[]{:S(2)}, u32[]{:S(2)}) collective-permute-start(bf16[4,48,256]{2,1,0:T(8,128)(2,1)} %get-tuple-element.44), channel_id=1, source_target_pairs={{0,48},{16,0},{32,16},{48,32},{64,112},{80,64},{96,80},{112,96},{1... | collective-permute-start | bytes 294920 | tf_op jit(solution)/shard_map/ppermute | solution.py:394
  8.9 1.1 copy-start.2
  10.0 0.6 copy-start.3
  10.0 0.7 copy-start.4
  12.4 7.6 %copy-start.8 = (bf16[80,1024]{1,0:T(8,128)(2,1)S(1)}, bf16[80,1024]{1,0:T(8,128)(2,1)}, u32[]{:S(2)}) copy-start(bf16[80,1024]{1,0:T(8,128)(2,1)} %get-tuple-element.64) | copy-start | bytes 491524
  12.4 9.2 %copy-start.11 = (bf16[4,48,256]{2,1,0:T(8,128)(2,1)S(1)}, bf16[4,48,256]{2,1,0:T(8,128)(2,1)}, u32[]{:S(2)}) copy-start(bf16[4,48,256]{2,1,0:T(8,128)(2,1)} %get-tuple-element.57) | copy-start | bytes 294916
  12.4 12.4 %copy-start.10 = (bf16[4,48,256]{2,1,0:T(8,128)(2,1)S(1)}, bf16[4,48,256]{2,1,0:T(8,128)(2,1)}, u32[]{:S(2)}) copy-start(bf16[4,48,256]{2,1,0:T(8,128)(2,1)} %get-tuple-element.58) | copy-start | bytes 294916
  12.4 17.1 %copy-start.9 = (bf16[4,48,256]{2,1,0:T(8,128)(2,1)S(1)}, bf16[4,48,256]{2,1,0:T(8,128)(2,1)}, u32[]{:S(2)}) copy-start(bf16[4,48,256]{2,1,0:T(8,128)(2,1)} %get-tuple-element.59) | copy-start | bytes 294916
  12.4 42.8 %all-to-all-start = ((bf16[16,48,1280]{2,1,0:T(8,128)(2,1)}), bf16[16,48,1280]{2,1,0:T(8,128)(2,1)S(1)}, u32[]{:S(2)}, u32[]{:S(2)}) async-start(bf16[16,48,1280]{2,1,0:T(8,128)(2,1)} %get-tuple-element.63), calls=%async_computation | async-start | bytes 3932160 | tf_op jit(solution)/shard_map/all_to_all | solution.py:400
  20.0 35.1 %collective-permute-start.6 = (bf16[80,1024]{1,0:T(8,128)(2,1)S(1)}, bf16[80,1024]{1,0:T(8,128)(2,1)S(1)}, u32[]{:S(2)}, u32[]{:S(2)}) collective-permute-start(bf16[80,1024]{1,0:T(8,128)(2,1)S(1)} %copy-done.8), channel_id=1, source_target_pairs={{0,1},{1,0},{2,3},{3,2},{4,5},{5,4},{6,7},{7,6},{8,9},{9,8},{10,11... | collective-permute-start | bytes 491528 | tf_op jit(solution)/shard_map/ppermute | solution.py:404
  21.6 21.2 %collective-permute-start.3 = (bf16[4,48,256]{2,1,0:T(8,128)(2,1)S(1)}, bf16[4,48,256]{2,1,0:T(8,128)(2,1)S(1)}, u32[]{:S(2)}, u32[]{:S(2)}) collective-permute-start(bf16[4,48,256]{2,1,0:T(8,128)(2,1)S(1)} %copy-done.11), channel_id=1, source_target_pairs={{0,64},{16,80},{32,96},{48,112},{64,128},{80,144},{96,160},{112,17... | collective-permute-start | bytes 294920 | tf_op jit(solution)/shard_map/ppermute | solution.py:402
  24.9 17.9 %collective-permute-start.4 = (bf16[4,48,256]{2,1,0:T(8,128)(2,1)S(1)}, bf16[4,48,256]{2,1,0:T(8,128)(2,1)S(1)}, u32[]{:S(2)}, u32[]{:S(2)}) collective-permute-start(bf16[4,48,256]{2,1,0:T(8,128)(2,1)S(1)} %copy-done.10), channel_id=1, source_target_pairs={{0,128},{16,144},{32,160},{48,176},{64,192},{80,208},{96,224},{112... | collective-permute-start | bytes 294920 | tf_op jit(solution)/shard_map/ppermute | solution.py:402
  29.5 13.3 %collective-permute-start.5 = (bf16[4,48,256]{2,1,0:T(8,128)(2,1)S(1)}, bf16[4,48,256]{2,1,0:T(8,128)(2,1)S(1)}, u32[]{:S(2)}, u32[]{:S(2)}) collective-permute-start(bf16[4,48,256]{2,1,0:T(8,128)(2,1)S(1)} %copy-done.9), channel_id=1, source_target_pairs={{0,192},{16,208},{32,224},{48,240},{64,0},{80,16},{96,32},{112,48}... | collective-permute-start | bytes 294920 | tf_op jit(solution)/shard_map/ppermute | solution.py:402
  42.8 0.6 copy-start.5
  42.8 0.7 copy-start.6
  42.8 0.7 copy-start.7
  55.2 27.2 %copy-start = (bf16[64,2048]{1,0:T(8,128)(2,1)S(1)}, bf16[64,2048]{1,0:T(8,128)(2,1)}, u32[]{:S(2)}) copy-start(bf16[64,2048]{1,0:T(8,128)(2,1)} %cotangent_ref.3) | copy-start | bytes 786436
  55.2 27.2 %copy-start.1 = (bf16[64]{0:T(256)(128)(2,1)S(1)}, bf16[64]{0:T(256)(128)(2,1)}, u32[]{:S(2)}) copy-start(bf16[64]{0:T(256)(128)(2,1)} %param.11) | copy-start | bytes 388
  85.0 19.4 %all-to-all-start.2 = ((bf16[32,56,128]{2,1,0:T(8,128)(2,1)}), bf16[32,56,128]{2,1,0:T(8,128)(2,1)S(1)}, u32[]{:S(2)}, u32[]{:S(2)}) async-start(bf16[32,56,128]{2,1,0:T(8,128)(2,1)} %get-tuple-element.71), calls=%async_computation.2 | async-start | bytes 917504 | tf_op jit(solution)/shard_map/all_to_all | solution.py:415
  92.2 8.4 %collective-permute-start.7 = (bf16[64,1024]{1,0:T(8,128)(2,1)S(1)}, bf16[64,1024]{1,0:T(8,128)(2,1)S(1)}, u32[]{:S(2)}, u32[]{:S(2)}) collective-permute-start(bf16[64,1024]{1,0:T(8,128)(2,1)S(1)} %get-tuple-element.69), channel_id=1, source_target_pairs={{0,1},{1,0},{2,3},{3,2},{4,5},{5,4},{6,7},{7,6},{8,9},{9,8},{10,11... | collective-permute-start | bytes 393224 | tf_op jit(solution)/shard_map/ppermute | solution.py:417
  104.5 9.0 %collective-permute-start.8 = (f32[48,128]{1,0:T(8,128)S(1)}, f32[48,128]{1,0:T(8,128)S(1)}, u32[]{:S(2)}, u32[]{:S(2)}) collective-permute-start(f32[48,128]{1,0:T(8,128)S(1)} %slice.20), channel_id=1, source_target_pairs={{144,0},{160,1},{240,2},{112,3},{176,4},{64,5},{16,6},{192,7},{80,... | collective-permute-start | bytes 73736 | tf_op jit(solution)/shard_map/ppermute | solution.py:425
